TPU v7x, 32 devices: a whole 2x2x4 slice. The times are simulated.
32 devices in a mesh: rep: 8 (over z, core), shard: 4 (over y, x).
Axes of the slice: x: 2, y: 2, z: 4, core: 2. Of those that a mesh axis runs over, the one named last changes fastest.
Arguments:
- tokens: bfloat16 [8192, 2048], P(('rep', 'shard')), may hold values from -6 to 6
- segments: int32 [8192], P(('rep', 'shard')), may hold values from 0 to 3, as said below
- query_w: bfloat16 [2048, 2048], P('shard'), may hold values from -0.125 to 0.125
- key_w: bfloat16 [2048, 512], P('shard'), may hold values from -0.125 to 0.125
- value_w: bfloat16 [2048, 512], P('shard'), may hold values from -0.125 to 0.125
- proj_w: bfloat16 [2048, 2048], P('shard'), may hold values from -1.5 to 1.5
- attn_gain: float32 [2048], replicated, may hold values from 0.1 to 1.9
- gate_w: bfloat16 [2048, 8192], P('shard'), may hold values from -0.125 to 0.125
- up_w: bfloat16 [2048, 8192], P('shard'), may hold values from -0.125 to 0.125
- down_w: bfloat16 [8192, 2048], P('shard'), may hold values from -0.0625 to 0.0625
- mlp_gain: float32 [2048], replicated, may hold values from 0.1 to 1.9
- cotangent: bfloat16 [8192, 2048], P(('rep', 'shard')), may hold values from -6 to 6
Outputs:
- result: float32 [8192, 2048], P(('rep', 'shard'))
- grad_tokens: float32 [8192, 2048], P(('rep', 'shard'))
- grad_query: float32 [2048, 2048], P('shard')
- grad_key: float32 [2048, 512], P('shard')
- grad_value: float32 [2048, 512], P('shard')
- grad_proj: float32 [2048, 2048], P('shard')
- grad_attn_gain: float32 [2048], P('shard')
- grad_gate: float32 [2048, 8192], P('shard')
- grad_up: float32 [2048, 8192], P('shard')
- grad_down: float32 [8192, 2048], P('shard')
- grad_mlp_gain: float32 [2048], P('shard')
Inputs may be any that keep to these rules, and one draw needn't show every extreme that they name: `segments`: each sequence of 1024 tokens (the rows of one index of rep) has segment numbers that start at 0 and never fall, and holds four documents; its second document begins within the sequence's first 256 tokens and ends within its last 256.
All inputs are finite; a program needn't handle non-finite values.
Results may differ from a plain program's by a relative error of at most 0.02.
Values may be sent and summed in bfloat16 or wider, within the bound.
A program may use at most 576 MiB of HBM per device.

v0:
```python
import math

import jax
import jax.numpy as jnp
from jax import lax
from jax.sharding import PartitionSpec as P

HEADS = 32
KV_HEADS = 8
HEAD = 64


epsilon = 1e-05
rope_base = 500000.0


def plain_dot(left, right):
    return jnp.dot(left, right, preferred_element_type=jnp.float32)


def dot_back(left, right):
    return lax.dot_general(
        left, right, (((1,), (1,)), ((), ())), preferred_element_type=jnp.float32
    )


def dot_left(left, right):
    return lax.dot_general(
        left, right, (((0,), (0,)), ((), ())), preferred_element_type=jnp.float32
    )


def normalize(values, gain_vec):
    inv_rms = lax.rsqrt(jnp.mean(values * values, axis=-1, keepdims=True) + epsilon)
    return (values * inv_rms * gain_vec, inv_rms)


def norm_back(values, inv_rms, gain_vec, grad_in):
    weighted = grad_in * gain_vec
    inner = jnp.mean(weighted * values, axis=-1, keepdims=True)
    grad_values = inv_rms * weighted - values * (inv_rms * inv_rms * inv_rms) * inner
    return (grad_values, jnp.sum(grad_in * values * inv_rms, axis=0))


def doc_positions(seg_ids):
    index = jnp.arange(seg_ids.shape[0], dtype=jnp.int32)
    fresh = (index == 0) | (seg_ids != jnp.roll(seg_ids, 1))
    begins = lax.cummax(jnp.where(fresh, index, jnp.zeros_like(index)), axis=0)
    return index - begins


def rope_tables(positions):
    freqs = rope_base ** (-(jnp.arange(HEAD // 2, dtype=jnp.float32) * (2.0 / HEAD)))
    angles = positions.astype(jnp.float32)[:, None] * freqs[None, :]
    return (jnp.cos(angles)[:, None, :], jnp.sin(angles)[:, None, :])


def rotate(values, cos_table, sin_table):
    row_count = values.shape[0]
    shaped = values.reshape(row_count, -1, HEAD)
    first_half = shaped[..., : HEAD // 2]
    second_half = shaped[..., HEAD // 2 :]
    turned = jnp.concatenate(
        [
            first_half * cos_table - second_half * sin_table,
            second_half * cos_table + first_half * sin_table,
        ],
        axis=-1,
    )
    return turned.reshape(row_count, -1)


def attend(query_heads, key_heads, value_heads, allowed):
    scale_factor = 1.0 / math.sqrt(HEAD)

    def head_block(operands):
        query_h, key_h, value_h = operands
        scores = (
            jnp.einsum("gqd,kd->gqk", query_h, key_h, preferred_element_type=jnp.float32)
            * scale_factor
        )
        scores = jnp.where(allowed[None], scores, -1e30)
        top = jnp.max(scores, axis=-1, keepdims=True)
        expo = jnp.exp(scores - top)
        total = jnp.sum(expo, axis=-1, keepdims=True)
        probs_b = (expo / total).astype(jnp.bfloat16)
        mixed = jnp.einsum("gqk,kd->gqd", probs_b, value_h, preferred_element_type=jnp.float32)
        return (mixed, top + jnp.log(total))

    return lax.map(head_block, (query_heads, key_heads, value_heads))


def attend_back(query_heads, key_heads, value_heads, grad_heads, lse_heads, allowed):
    scale_factor = 1.0 / math.sqrt(HEAD)

    def head_block(operands):
        query_h, key_h, value_h, grad_h, lse_h = operands
        scores = (
            jnp.einsum("gqd,kd->gqk", query_h, key_h, preferred_element_type=jnp.float32)
            * scale_factor
        )
        scores = jnp.where(allowed[None], scores, -1e30)
        probs = jnp.exp(scores - lse_h)
        grad_probs = jnp.einsum("gqd,kd->gqk", grad_h, value_h, preferred_element_type=jnp.float32)
        inner = jnp.sum(probs * grad_probs, axis=-1, keepdims=True)
        grad_scores = (probs * (grad_probs - inner)).astype(jnp.bfloat16)
        grad_query = (
            jnp.einsum("gqk,kd->gqd", grad_scores, key_h, preferred_element_type=jnp.float32)
            * scale_factor
        )
        grad_key = (
            jnp.einsum("gqk,gqd->kd", grad_scores, query_h, preferred_element_type=jnp.float32)
            * scale_factor
        )
        grad_value = jnp.einsum(
            "gqk,gqd->kd", probs.astype(jnp.bfloat16), grad_h, preferred_element_type=jnp.float32
        )
        return (grad_query, grad_key, grad_value)

    return lax.map(head_block, (query_heads, key_heads, value_heads, grad_heads, lse_heads))


def local(
    tokens,
    segments,
    query_w,
    key_w,
    value_w,
    proj_w,
    attn_gain,
    gate_w,
    up_w,
    down_w,
    mlp_gain,
    cotangent,
):
    shards = lax.axis_size("shard")
    device_pos = lax.axis_index("shard")
    tok_count = tokens.shape[0]
    seq_length = tok_count * shards
    group = HEADS // KV_HEADS
    seg_all = lax.all_gather(segments, "shard", axis=0, tiled=True)
    positions = lax.dynamic_slice_in_dim(doc_positions(seg_all), device_pos * tok_count, tok_count)
    cos_table, sin_table = rope_tables(positions)
    query_index = device_pos * tok_count + jnp.arange(tok_count, dtype=jnp.int32)
    key_index = jnp.arange(seq_length, dtype=jnp.int32)
    allowed = (segments[:, None] == seg_all[None, :]) & (key_index[None, :] <= query_index[:, None])

    def fetch_attn():
        return (
            lax.all_gather(query_w, "shard", axis=0, tiled=True),
            lax.all_gather(key_w, "shard", axis=0, tiled=True),
            lax.all_gather(value_w, "shard", axis=0, tiled=True),
            lax.all_gather(proj_w, "shard", axis=0, tiled=True),
        )

    attn_full = fetch_attn()
    query_m, key_m, value_m, proj_m = attn_full
    inputs = tokens.astype(jnp.float32)
    normed, attn_rms = normalize(inputs, attn_gain)
    normed_b = normed.astype(jnp.bfloat16)
    queries = rotate(plain_dot(normed_b, query_m), cos_table, sin_table).astype(jnp.bfloat16)
    keys_own = rotate(plain_dot(normed_b, key_m), cos_table, sin_table).astype(jnp.bfloat16)
    values_own = plain_dot(normed_b, value_m).astype(jnp.bfloat16)
    keys_all, values_all = (
        lax.all_gather(keys_own, "shard", axis=0, tiled=True),
        lax.all_gather(values_own, "shard", axis=0, tiled=True),
    )
    query_heads = queries.reshape(tok_count, KV_HEADS, group, HEAD).transpose(1, 2, 0, 3)
    key_heads = keys_all.reshape(seq_length, KV_HEADS, HEAD).transpose(1, 0, 2)
    value_heads = values_all.reshape(seq_length, KV_HEADS, HEAD).transpose(1, 0, 2)
    mixed_heads, lse_heads = attend(query_heads, key_heads, value_heads, allowed)
    mixed_b = (
        mixed_heads.transpose(2, 0, 1, 3).reshape(tok_count, HEADS * HEAD).astype(jnp.bfloat16)
    )
    hidden = inputs + plain_dot(mixed_b, proj_m)
    mlp_full = (
        lax.all_gather(gate_w, "shard", axis=0, tiled=True),
        lax.all_gather(up_w, "shard", axis=0, tiled=True),
        lax.all_gather(down_w, "shard", axis=0, tiled=True),
    )
    gate_m, up_m, down_m = mlp_full
    normed_mlp, mlp_rms = normalize(hidden, mlp_gain)
    normed_mlp_b = normed_mlp.astype(jnp.bfloat16)
    gate_val = plain_dot(normed_mlp_b, gate_m)
    up_val = plain_dot(normed_mlp_b, up_m)
    sigm = jax.nn.sigmoid(gate_val)
    swish = gate_val * sigm
    activ_b = (swish * up_val).astype(jnp.bfloat16)
    result = hidden + plain_dot(activ_b, down_m)
    grad_down = lax.psum_scatter(
        dot_left(activ_b, cotangent).astype(jnp.bfloat16), "shard", scatter_dimension=0, tiled=True
    )
    grad_activ = dot_back(cotangent, down_m)
    grad_gate_b = (grad_activ * up_val * sigm * (1.0 + gate_val * (1.0 - sigm))).astype(
        jnp.bfloat16
    )
    grad_up_b = (grad_activ * swish).astype(jnp.bfloat16)
    grad_normed_mlp = dot_back(grad_gate_b, gate_m) + dot_back(grad_up_b, up_m)
    gate_up_b = jnp.concatenate([grad_gate_b, grad_up_b], axis=1)
    gate_up = lax.psum_scatter(
        dot_left(normed_mlp_b, gate_up_b).astype(jnp.bfloat16),
        "shard",
        scatter_dimension=0,
        tiled=True,
    ).astype(jnp.float32)
    grad_hidden_norm, grad_mlp_gain = norm_back(hidden, mlp_rms, mlp_gain, grad_normed_mlp)
    grad_hidden = cotangent.astype(jnp.float32) + grad_hidden_norm
    grad_hidden_b = grad_hidden.astype(jnp.bfloat16)
    attn_full = fetch_attn()
    query_m, key_m, value_m, proj_m = attn_full
    grad_mixed_b = dot_back(grad_hidden_b, proj_m).astype(jnp.bfloat16)
    grad_heads = grad_mixed_b.reshape(tok_count, KV_HEADS, group, HEAD).transpose(1, 2, 0, 3)
    grad_q_heads, grad_k_heads, grad_v_heads = attend_back(
        query_heads, key_heads, value_heads, grad_heads, lse_heads, allowed
    )
    grad_keys_all = grad_k_heads.transpose(1, 0, 2).reshape(seq_length, KV_HEADS * HEAD)
    grad_values_all = grad_v_heads.transpose(1, 0, 2).reshape(seq_length, KV_HEADS * HEAD)
    grad_keys, grad_values = (
        lax.psum_scatter(
            grad_keys_all.astype(jnp.bfloat16), "shard", scatter_dimension=0, tiled=True
        ).astype(jnp.float32),
        lax.psum_scatter(
            grad_values_all.astype(jnp.bfloat16), "shard", scatter_dimension=0, tiled=True
        ).astype(jnp.float32),
    )
    grad_queries = grad_q_heads.transpose(2, 0, 1, 3).reshape(tok_count, HEADS * HEAD)
    grad_query_b = rotate(grad_queries, cos_table, -sin_table).astype(jnp.bfloat16)
    grad_key_b = rotate(grad_keys, cos_table, -sin_table).astype(jnp.bfloat16)
    grad_value_b = grad_values.astype(jnp.bfloat16)
    grad_normed = (
        dot_back(grad_query_b, query_m)
        + dot_back(grad_key_b, key_m)
        + dot_back(grad_value_b, value_m)
    )
    attn_cols = jnp.concatenate([grad_query_b, grad_key_b, grad_value_b], axis=1)
    ffn_width = gate_w.shape[1]
    model_width = query_w.shape[1]
    kv_width = key_w.shape[1]
    left_part = dot_left(normed_b, attn_cols)
    right_part = dot_left(mixed_b, grad_hidden_b)
    attn_grads = lax.psum_scatter(
        jnp.concatenate([left_part, right_part], axis=1).astype(jnp.bfloat16),
        "shard",
        scatter_dimension=0,
        tiled=True,
    ).astype(jnp.float32)
    grad_gate = gate_up[:, :ffn_width]
    grad_up = gate_up[:, ffn_width:]
    grad_query = attn_grads[:, :model_width]
    grad_key = attn_grads[:, model_width : model_width + kv_width]
    grad_value = attn_grads[:, model_width + kv_width : model_width + 2 * kv_width]
    grad_proj = attn_grads[:, model_width + 2 * kv_width :]
    grad_inputs_norm, grad_attn_gain = norm_back(inputs, attn_rms, attn_gain, grad_normed)
    grad_tokens = grad_hidden + grad_inputs_norm
    gain_attn_part, gain_mlp_part = (
        lax.psum_scatter(grad_attn_gain, "shard", scatter_dimension=0, tiled=True),
        lax.psum_scatter(grad_mlp_gain, "shard", scatter_dimension=0, tiled=True),
    )
    summed = (
        lax.psum(grad_query.astype(jnp.bfloat16), "rep").astype(jnp.float32),
        lax.psum(grad_key.astype(jnp.bfloat16), "rep").astype(jnp.float32),
        lax.psum(grad_value.astype(jnp.bfloat16), "rep").astype(jnp.float32),
        lax.psum(grad_proj.astype(jnp.bfloat16), "rep").astype(jnp.float32),
        lax.psum(gain_attn_part.astype(jnp.bfloat16), "rep").astype(jnp.float32),
        lax.psum(grad_gate.astype(jnp.bfloat16), "rep").astype(jnp.float32),
        lax.psum(grad_up.astype(jnp.bfloat16), "rep").astype(jnp.float32),
        lax.psum(grad_down, "rep").astype(jnp.float32),
        lax.psum(gain_mlp_part.astype(jnp.bfloat16), "rep").astype(jnp.float32),
    )
    return (result, grad_tokens) + tuple(summed)


def solution(mesh):
    in_specs = (
        P(("rep", "shard"), None),
        P(("rep", "shard")),
        P("shard", None),
        P("shard", None),
        P("shard", None),
        P("shard", None),
        P(),
        P("shard", None),
        P("shard", None),
        P("shard", None),
        P(),
        P(("rep", "shard"), None),
    )
    out_specs = (
        P(("rep", "shard"), None),
        P(("rep", "shard"), None),
        P("shard", None),
        P("shard", None),
        P("shard", None),
        P("shard", None),
        P("shard"),
        P("shard", None),
        P("shard", None),
        P("shard", None),
        P("shard"),
    )
    return jax.shard_map(local, mesh=mesh, in_specs=in_specs, out_specs=out_specs, check_vma=False)
```

profile of v0, /device:TPU:0, one launch (start us, length us, event | category | flops | bytes accessed | tf_op | source)
XLA Modules:
  0.0 3718.4 jit_solution(14708828792219910539)
XLA Ops:
  10.9 37.0 all-gather.17.cloned.1.call-done
  47.9 3.4 convolution_convert_fusion.5
  52.0 8.0 all-gather
  62.8 22.3 all-gather.13.cloned.1.call-done
  85.1 2.6 fusion.86
  91.7 22.4 all-gather.19.cloned.1.call-done
  116.4 87.1 %all-gather.11.cloned.1.call-done = bf16[2048,2048]{1,0:T(8,128)(2,1)} async-done(((bf16[512,2048]{1,0:T(8,128)(2,1)}), bf16[2048,2048]{1,0:T(8,128)(2,1)}) %all-gather.11.cloned.1.call-update) | async-done | bytes 8388624 | tf_op jit(solution)/shard_map/all_gather | solution.py:151
  203.5 6.8 fusion.88
  210.8 21.5 all-gather.15.cloned.1.call-done
  232.3 47.9 %while.30 = (s32[]{:T(128)}, bf16[8,4,256,64]{2,3,1,0:T(8,128)(2,1)S(1)}, f32[8,4,256,1]{2,1,3,0:T(4,128)S(1)}, bf16[8,4,256,64]{2,3,1,0:T(8,128)(2,1)S(1)}, bf1...) while((s32[]{:T(128)}, ...), condition=%wide.region_6.7_spmd.clone.clone, body=%wide.region_3.6_spmd.clone.sunk.clone | while | flops 281803776 | bytes 14327913 | solution.py:90
  235.7 2.5 fusion.170
  241.7 2.5 fusion.170
  247.8 2.5 fusion.170
  253.8 2.5 fusion.170
  259.7 2.5 fusion.170
  265.7 2.5 fusion.170
  271.7 2.5 fusion.170
  277.7 2.5 fusion.170
  280.2 41.6 %all-gather.21.cloned.1.call-done = bf16[2048,2048]{1,0:T(8,128)(2,1)} async-done(((bf16[512,2048]{1,0:T(8,128)(2,1)}), bf16[2048,2048]{1,0:T(8,128)(2,1)}) %all-gather.21.cloned.1.call-update) | async-done | bytes 8388624 | tf_op jit(solution)/shard_map/all_gather | solution.py:154
  321.8 6.2 multiply_reduce_fusion.3
  328.3 292.5 %all-gather.23.cloned.1.call-done = bf16[2048,8192]{1,0:T(8,128)(2,1)} async-done(((bf16[512,8192]{1,0:T(8,128)(2,1)}), bf16[2048,8192]{1,0:T(8,128)(2,1)}) %all-gather.23.cloned.1.call-update) | async-done | bytes 33554448 | tf_op jit(solution)/shard_map/all_gather | solution.py:178
  620.8 21.7 fusion.93
  642.5 277.4 %all-gather.25.cloned.1.call-done = bf16[2048,8192]{1,0:T(8,128)(2,1)} async-done(((bf16[512,8192]{1,0:T(8,128)(2,1)}), bf16[2048,8192]{1,0:T(8,128)(2,1)}) %all-gather.25.cloned.1.call-update) | async-done | bytes 33554448 | tf_op jit(solution)/shard_map/all_gather | solution.py:179
  919.9 21.2 fusion.94
  941.1 277.9 %all-gather.27.cloned.1.call-done = bf16[8192,2048]{1,0:T(8,128)(2,1)} async-done(((bf16[2048,2048]{1,0:T(8,128)(2,1)}), bf16[8192,2048]{1,0:T(8,128)(2,1)}) %all-gather.27.cloned.1.call-update) | async-done | bytes 33554448 | tf_op jit(solution)/shard_map/all_gather | solution.py:180
  1219.0 23.9 multiply_convert_fusion.1
  1242.8 15.7 fusion.95
  1258.6 18.9 multiply_reduce_fusion.1
  1277.6 2.8 subtract_add_fusion
  1280.4 3.3 convolution_convert_fusion.4
  1285.3 97.3 %while.31 = (s32[]{:T(128)}, f32[8,4,256,64]{2,3,1,0:T(8,128)}, bf16[8,1024,64]{1,2,0:T(8,128)(2,1)}, bf16[8,1024,64]{1,2,0:T(8,128)(2,1)}, bf16[8,4,256,64]{2,3...) while((s32[]{:T(128)}, f32[8,4,256,64]{2,3,1,0:T(8,128)}, ...), condition=%wide.region_11.12_spmd.clone.clone, body=%wide.region_9.11_spmd.clone.sunk.clone | while | flops 687733760 | bytes 34249856 | solution.py:120
  1287.6 2.5 multiply_reduce_fusion.6
  1299.7 2.4 multiply_reduce_fusion.6
  1311.9 2.4 multiply_reduce_fusion.6
  1324.0 2.4 multiply_reduce_fusion.6
  1336.1 2.4 multiply_reduce_fusion.6
  1348.3 2.4 multiply_reduce_fusion.6
  1360.4 2.5 multiply_reduce_fusion.6
  1372.5 2.4 multiply_reduce_fusion.6
  1386.3 7.1 convolution_convert_fusion.3
  1393.4 17.0 reduce-scatter.7.cloned.1.call-done
  1411.5 29.8 reduce-scatter.9.cloned.1.call-done
  1441.4 8.1 convolution_convert_fusion.2
  1449.5 17.5 pad_maximum_fusion
  1467.1 31.1 convolution_convert_fusion
  1498.3 17.3 convolution_convert_fusion.1
  1517.5 137.5 %reduce-scatter.11.cloned.1.call-done = bf16[512,5120]{1,0:T(8,128)(2,1)} async-done(((bf16[2048,5120]{1,0:T(8,128)(2,1)}), bf16[512,5120]{1,0:T(8,128)(2,1)}) %reduce-scatter.11.cloned.1.call-update) | async-done | bytes 5242896 | tf_op jit(solution)/shard_map/reduce_scatter | solution.py:242
  1657.2 4.9 fusion.91
  1662.1 1113.8 %all-reduce.10.cloned.1.call-done = bf16[2048,16384]{1,0:T(8,128)(2,1)} async-done(((bf16[2048,16384]{1,0:T(8,128)(2,1)}), bf16[2048,16384]{1,0:T(8,128)(2,1)}) %all-reduce.10.cloned.1.call-update) | async-done | bytes 67108880
  2775.9 13.1 fusion.90
  2789.0 279.9 %reduce-scatter.13.cloned.1.call-done = bf16[2048,2048]{1,0:T(8,128)(2,1)} async-done(((bf16[8192,2048]{1,0:T(8,128)(2,1)}), bf16[2048,2048]{1,0:T(8,128)(2,1)}) %reduce-scatter.13.cloned.1.call-update) | async-done | bytes 8388624
  3068.9 7.6 fusion.96
  3076.5 18.2 convolution_add_fusion.3
  3094.8 3.1 convolution_add_fusion.1
  3097.9 2.5 fusion.72
  3100.4 15.0 all-reduce.4
  3115.6 14.9 all-reduce.5
  3131.7 3.5 fusion.69
  3135.2 532.2 %all-reduce.12.cloned.1.call-done = (bf16[512,2048]{1,0:T(8,128)(2,1)}, bf16[512,512]{1,0:T(8,128)(2,1)}, bf16[512,512]{1,0:T(8,128)(2,1)}, bf16[512,2048]{1,0:T...) async-done(((bf16[512,2048]{1,0:T(8,128)(2,1)}, bf16[512,512]{1,0:T(8,128)(2,1)}, bf16[512,512]{1,0:T(8,128)(2,1)}, ...) | async-done | bytes 30408720 | tf_op jit(solution)/shard_map/psum | solution.py:261
  3667.4 4.3 convert_element_type.161
  3673.9 2.5 convert_element_type.164
  3676.5 11.7 convert_element_type.168
  3688.2 11.7 convert_element_type.169
  3699.9 11.7 convert_element_type.171
  (216 shorter events, 132.6 us)
Async XLA Ops:
  7.2 40.7 %all-gather.17.cloned.1.call-start = ((), (), s32[]{:S(2)}) async-start(), calls=%async_computation.7 | async-start | bytes 2621440 | tf_op jit(solution)/shard_map/all_gather | solution.py:153
  7.9 44.0 %copy-start.19 = (s32[256]{0:T(256)S(1)}, s32[256]{0:T(256)}, u32[]{:S(2)}) copy-start(s32[256]{0:T(256)} %param.17) | copy-start | bytes 3076
  7.9 77.2 %all-gather.13.cloned.1.call-start = ((), (), s32[]{:S(2)}) async-start(), calls=%async_computation.5 | async-start | bytes 2621440 | tf_op jit(solution)/shard_map/all_gather | solution.py:152
  8.7 76.4 %copy-start = (bf16[256,2048]{1,0:T(8,128)(2,1)S(1)}, bf16[256,2048]{1,0:T(8,128)(2,1)}, u32[]{:S(2)}) copy-start(bf16[256,2048]{1,0:T(8,128)(2,1)} %param.16) | copy-start | bytes 3145732
  8.7 76.4 %copy-start.17 = (f32[2048]{0:T(1024)S(1)}, f32[2048]{0:T(1024)}, u32[]{:S(2)}) copy-start(f32[2048]{0:T(1024)} %param.22) | copy-start | bytes 24580
  8.7 105.5 %all-gather.19.cloned.1.call-start = ((), (), s32[]{:S(2)}) async-start(), calls=%async_computation.8 | async-start | bytes 1310720 | tf_op jit(solution)/shard_map/all_gather | solution.py:167
  10.9 192.6 %copy-start.21 = (f32[256]{0:T(256)}, f32[256]{0:T(256)S(1)}, u32[]{:S(2)}) copy-start(f32[256]{0:T(256)S(1)} %get-tuple-element.242) | copy-start | bytes 3076
  51.3 152.2 %all-gather.11.cloned.1.call-start = ((), (), s32[]{:S(2)}) async-start(), calls=%async_computation.4 | async-start | bytes 10485760 | tf_op jit(solution)/shard_map/all_gather | solution.py:151
  51.9 180.4 %all-gather.15.cloned.1.call-start = ((), (), s32[]{:S(2)}) async-start(), calls=%async_computation.6 | async-start | bytes 1310720 | tf_op jit(solution)/shard_map/all_gather | solution.py:166
  62.8 147.6 %copy-start.12 = (f32[256,32]{0,1:T(8,128)}, f32[256,32]{0,1:T(8,128)S(1)}, u32[]{:S(2)}) copy-start(f32[256,32]{0,1:T(8,128)S(1)} %get-tuple-element.240) | copy-start | bytes 98308
  88.5 233.3 %all-gather.21.cloned.1.call-start = ((), (), s32[]{:S(2)}) async-start(), calls=%async_computation.9 | async-start | bytes 10485760 | tf_op jit(solution)/shard_map/all_gather | solution.py:154
  89.1 531.7 %all-gather.23.cloned.1.call-start = ((), (), s32[]{:S(2)}) async-start(), calls=%async_computation.10 | async-start | bytes 41943040 | tf_op jit(solution)/shard_map/all_gather | solution.py:178
  89.9 830.0 %all-gather.25.cloned.1.call-start = ((), (), s32[]{:S(2)}) async-start(), calls=%async_computation.11 | async-start | bytes 41943040 | tf_op jit(solution)/shard_map/all_gather | solution.py:179
  90.6 1128.4 %all-gather.27.cloned.1.call-start = ((), (), s32[]{:S(2)}) async-start(), calls=%async_computation.12 | async-start | bytes 41943040 | tf_op jit(solution)/shard_map/all_gather | solution.py:180
  91.3 1319.1 %reduce-scatter.7.cloned.1.call-start = ((), (), s32[]{:S(2)}) async-start(), calls=%async_computation.13 | async-start | bytes 1310720 | tf_op jit(solution)/shard_map/reduce_scatter | solution.py:220
  280.2 41.6 %copy-start.4 = (bf16[8,4,256,64]{2,3,1,0:T(8,128)(2,1)}, bf16[8,4,256,64]{2,3,1,0:T(8,128)(2,1)S(1)}, u32[]{:S(2)}) copy-start(bf16[8,4,256,64]{2,3,1,0:T(8,128)(2,1)S(1)} %get-tuple-element.103) | copy-start | bytes 3145732
  280.2 41.6 %copy-start.5 = (bf16[8,4,256,64]{2,3,1,0:T(8,128)(2,1)}, bf16[8,4,256,64]{2,3,1,0:T(8,128)(2,1)S(1)}, u32[]{:S(2)}) copy-start(bf16[8,4,256,64]{2,3,1,0:T(8,128)(2,1)S(1)} %get-tuple-element.548) | copy-start | bytes 3145732
  321.8 6.2 copy-start.20
  328.0 930.6 %copy-start.2 = (f32[256,2048]{1,0:T(8,128)}, f32[256,2048]{1,0:T(8,128)S(1)}, u32[]{:S(2)}) copy-start(f32[256,2048]{1,0:T(8,128)S(1)} %get-tuple-element.246) | copy-start | bytes 6291460
  328.3 591.6 %copy-start.7 = (bf16[256,2048]{1,0:T(8,128)(2,1)}, bf16[256,2048]{1,0:T(8,128)(2,1)S(1)}, u32[]{:S(2)}) copy-start(bf16[256,2048]{1,0:T(8,128)(2,1)S(1)} %multiply_convert_fusion.4) | copy-start | bytes 3145732
  1258.6 21.8 slice-start
  1258.6 18.9 copy-start.8
  1258.6 21.8 slice-start.1
  1285.3 98.1 %copy-start.13 = (f32[256,32]{0,1:T(8,128)S(1)}, f32[256,32]{0,1:T(8,128)}, u32[]{:S(2)}) copy-start(f32[256,32]{0,1:T(8,128)} %copy-done.12) | copy-start | bytes 98308
  1285.3 98.1 %copy-start.16 = (f32[256,32]{0,1:T(8,128)S(1)}, f32[256,32]{0,1:T(8,128)}, u32[]{:S(2)}) copy-start(f32[256,32]{0,1:T(8,128)} %get-tuple-element.238) | copy-start | bytes 98308
  1382.6 58.8 %reduce-scatter.9.cloned.1.call-start = ((), (), s32[]{:S(2)}) async-start(), calls=%async_computation.14 | async-start | bytes 1310720 | tf_op jit(solution)/shard_map/reduce_scatter | solution.py:223
  1383.3 271.7 %reduce-scatter.11.cloned.1.call-start = ((), (), s32[]{:S(2)}) async-start(), calls=%async_computation.15 | async-start | bytes 26214400 | tf_op jit(solution)/shard_map/reduce_scatter | solution.py:242
  1386.3 55.0 %copy-start.1 = (bf16[256,2048]{1,0:T(8,128)(2,1)S(1)}, bf16[256,2048]{1,0:T(8,128)(2,1)}, u32[]{:S(2)}) copy-start(bf16[256,2048]{1,0:T(8,128)(2,1)} %param.16) | copy-start | bytes 3145732
  1386.3 55.0 %copy-start.18 = (f32[2048]{0:T(1024)S(1)}, f32[2048]{0:T(1024)}, u32[]{:S(2)}) copy-start(f32[2048]{0:T(1024)} %param.22) | copy-start | bytes 24580
  1386.3 55.0 %copy-start.22 = (f32[256]{0:T(256)S(1)}, f32[256]{0:T(256)}, u32[]{:S(2)}) copy-start(f32[256]{0:T(256)} %copy-done.21) | copy-start | bytes 3076
  1467.0 1308.9 %all-reduce.10.cloned.1.call-start = ((), (), s32[]{:S(2)}) async-start(), calls=%async_computation.16 | async-start | bytes 134217728
  1498.2 1570.7 %reduce-scatter.13.cloned.1.call-start = ((), (), s32[]{:S(2)}) async-start(), calls=%async_computation.17 | async-start | bytes 41943040
  1515.6 0.7 copy-start.25
  1515.7 2151.7 %all-reduce.12.cloned.1.call-start = ((), (), s32[]{:S(2)}) async-start(), calls=%async_computation.18 | async-start | bytes 60817408 | tf_op jit(solution)/shard_map/psum | solution.py:261
  3068.9 7.6 copy-start.3
  3068.9 7.6 copy-start.6
  3094.7 3.1 copy-start.10
  3094.8 3.2 copy-start.11
  3097.9 2.5 copy-start.23
  3097.9 33.8 copy-start.24
  3667.4 4.3 copy-start.15
  3667.4 5.4 copy-start.14
  3667.4 6.5 copy-start.9
Sparse Core Ops, SparseCore 0:
  9.9 38.0 all-gather.16
  49.7 35.2 all-gather.12
  87.5 26.6 all-gather.18
  115.9 87.5 all-gather.10
  205.8 26.4 all-gather.14
  234.0 87.7 all-gather.20
  323.6 297.1 all-gather.22
  622.6 297.2 all-gather.24
  921.7 297.2 all-gather.26
  1382.7 27.6 reduce-scatter.6
  1413.6 27.7 reduce-scatter.8
  1467.1 187.8 reduce-scatter.10
  1658.9 1116.9 all-reduce.9
  2778.8 290.0 reduce-scatter.12
  3073.7 593.6 all-reduce.11
where the time goes:
time: 3720 us
  waiting for transfers between devices  3200 us (86%)
  matrix products  337 us (9%)
  other arithmetic  105 us (3%)
  blocking collectives  38 us (1%)
    unnamed x17, waiting for transfers between devices  1400 us
    psum x1, waiting for transfers between devices, local(): lax.psum(grad_query.astype(jnp.bfloat16), 'rep').astype(jnp.float32)  532 us
    all_gather x1, waiting for transfers between devices, local(): lax.all_gather(gate_w, 'shard', axis=0, tiled=True)  293 us
    all_gather x1, waiting for transfers between devices, local(): lax.all_gather(down_w, 'shard', axis=0, tiled=True)  278 us
    all_gather x1, waiting for transfers between devices, local(): lax.all_gather(up_w, 'shard', axis=0, tiled=True)  277 us
    reduce_scatter x1, waiting for transfers between devices, local(): lax.psum_scatter(jnp.concatenate([left_part, right_part], axis=1).astype(...  137 us
    all_gather x1, waiting for transfers between devices, fetch_attn(): lax.all_gather(query_w, 'shard', axis=0, tiled=True)  87.1 us
    dot_general x7, matrix products, plain_dot(): return jnp.dot(left, right, preferred_element_type=jnp.float32)  80.2 us
  transfers between devices with their start and end apart: 15, of which 15 were waited for; matrix products, arithmetic and copies ran while one was open for 6% of the time, Pallas kernels for 0%

commit v1 on v0

v1 whole, which is shorter than its diff:
```python
import functools
import math

import jax
import jax.numpy as jnp
from jax import lax
from jax.experimental import pallas as pl
from jax.experimental.pallas import tpu as pltpu
from jax.sharding import PartitionSpec as P

HEADS = 32
KV_HEADS = 8
HEAD = 64
GROUP = HEADS // KV_HEADS
SCALE = 1.0 / math.sqrt(HEAD)
TILE = 256
NEG = -1e30
MIB = 1024 * 1024

epsilon = 1e-05
rope_base = 500000.0
F32 = jnp.float32
BF16 = jnp.bfloat16


def dot(left, right, dims):
    return lax.dot_general(left, right, (dims, ((), ())), preferred_element_type=F32)


NN = ((1,), (0,))
NT = ((1,), (1,))
TN = ((0,), (0,))
TT = ((0,), (1,))


MESH = pl.DeviceIdType.MESH


def place():
    return lax.axis_index("rep"), lax.axis_index("shard")


def remote(src, dst, sends, recvs, index, rep, shard):
    return pltpu.make_async_remote_copy(
        src_ref=src,
        dst_ref=dst,
        send_sem=sends.at[index],
        recv_sem=recvs.at[index],
        device_id=(rep, shard),
        device_id_type=MESH,
    )


def greet(partners):
    barrier = pltpu.get_barrier_semaphore()
    for partner in partners:
        pl.semaphore_signal(barrier, inc=1, device_id=partner, device_id_type=MESH)
    pl.semaphore_wait(barrier, len(partners))


def plane_partners(rep, me, shards):
    return [(rep, me ^ step) for step in range(1, shards)]


class Spread:
    def __init__(self, shards, own, full, columns, sends, recvs, local_sem):
        rep, me = place()
        quarter = rep % 4
        count = own.shape[0]
        part = count // 4
        own_rows = pl.ds(pl.multiple_of(quarter * part, part), part)

        def at(shard, which):
            return full.at[pl.ds(pl.multiple_of(shard * count + which * part, part), part), :]

        def piece(shard):
            return own.at[own_rows, :] if columns is None else own.at[own_rows, columns(shard)]

        self.first, self.core, self.layer, self.last = [], [], [], []
        n = shards - 1
        for i in range(n):
            peer = me ^ (i + 1)
            self.first.append(remote(piece(peer), at(me, quarter), sends, recvs, i, rep, peer))
            mine = at(peer, quarter)
            self.core.append(remote(mine, mine, sends, recvs, n + i, rep ^ 1, me))
            self.layer.append(remote(mine, mine, sends, recvs, 2 * n + i, rep ^ 2, me))
            theirs = at(peer, quarter ^ 2)
            self.last.append(remote(theirs, theirs, sends, recvs, 3 * n + i, rep ^ 1, me))
        kept = own if columns is None else own.at[:, columns(me)]
        self.kept = pltpu.make_async_copy(
            kept, full.at[pl.ds(pl.multiple_of(me * count, count), count), :], local_sem
        )

    def start(self):
        for copy in self.first:
            copy.start()
        self.kept.start()

    def hand_on(self):
        for i, copy in enumerate(self.first):
            copy.wait_recv()
            self.layer[i].start()
            self.core[i].start()

    def hand_on_last(self):
        for i, copy in enumerate(self.layer):
            copy.wait_recv()
            self.last[i].start()

    def finish(self):
        for copy in self.core + self.last:
            copy.wait_recv()
        for copy in self.first + self.core + self.layer + self.last:
            copy.wait_send()
        self.kept.wait()

    @staticmethod
    def semaphores(shards):
        n = 4 * (shards - 1)
        return [
            pltpu.SemaphoreType.DMA((n,)),
            pltpu.SemaphoreType.DMA((n,)),
            pltpu.SemaphoreType.DMA,
        ]


class Gather:
    def __init__(self, shards, own, full, sends, recvs, local_sem=None):
        rep, me = place()
        count = own.shape[0]
        half = count // 2

        def at(shard, start, size):
            return full.at[pl.ds(pl.multiple_of(shard * count + start, half), size), :]

        self.direct, self.passed, self.kept = [], [], None
        if shards == 4:
            for i, (step, start) in enumerate(((1, 0), (2, half), (1, half), (2, 0))):
                self.direct.append(
                    remote(
                        own.at[pl.ds(start, half), :], at(me, start, half),
                        sends, recvs, i, rep, me ^ step,
                    )
                )
            for i, (step, start) in enumerate(((1, 0), (2, half))):
                came = at(me ^ step, start, half)
                self.passed.append(remote(came, came, sends, recvs, 4 + i, rep, me ^ step ^ 3))
        else:
            for i in range(shards - 1):
                self.direct.append(
                    remote(own, at(me, 0, count), sends, recvs, i, rep, me ^ (i + 1))
                )
        if local_sem is not None:
            self.kept = pltpu.make_async_copy(own, at(me, 0, count), local_sem)

    def start(self):
        for copy in self.direct:
            copy.start()
        if self.kept is not None:
            self.kept.start()

    def hand_on(self):
        for i, copy in enumerate(self.passed):
            self.direct[i].wait_recv()
            copy.start()

    def finish(self):
        for copy in self.direct[len(self.passed) :] + self.passed:
            copy.wait_recv()
        for copy in self.direct + self.passed:
            copy.wait_send()
        if self.kept is not None:
            self.kept.wait()

    @staticmethod
    def semaphores(shards):
        n = max(6, shards - 1)
        return [
            pltpu.SemaphoreType.DMA((n,)),
            pltpu.SemaphoreType.DMA((n,)),
            pltpu.SemaphoreType.DMA,
        ]


def column_block(part):
    return lambda shard: pl.ds(pl.multiple_of(shard * part, part), part)


def pair_partners(rep, me):
    return [(rep ^ 1, me), (rep ^ 2, me)]


ANY = pl.BlockSpec(memory_space=pl.ANY)
IN_VMEM = pl.BlockSpec(memory_space=pltpu.VMEM)


def first_kernel(shards, part, tokens, seg, qkv, tokens_all, seg_all, qkv_m, *sems):
    rep, me = place()
    greet(plane_partners(rep, me, shards) + pair_partners(rep, me))
    weight = Spread(shards, qkv, qkv_m, column_block(part), *sems[:3])
    rows = Gather(shards, tokens, tokens_all, *sems[3:6])
    seg_send, seg_recv, seg_local = sems[6:]
    segs = [
        remote(seg, seg_all.at[me], seg_send, seg_recv, i, rep, me ^ (i + 1))
        for i in range(shards - 1)
    ]
    weight.start()
    for copy in segs:
        copy.start()
    rows.start()
    own_seg = pltpu.make_async_copy(seg, seg_all.at[me], seg_local)
    own_seg.start()
    weight.hand_on()
    rows.hand_on()
    weight.hand_on_last()
    weight.finish()
    rows.finish()
    for copy in segs:
        copy.wait()
    own_seg.wait()


def first(tokens, seg, qkv_w, shards):
    rows, width = tokens.shape
    part = qkv_w.shape[1] // shards
    n = shards - 1
    return pl.pallas_call(
        functools.partial(first_kernel, shards, part),
        in_specs=[ANY] * 3,
        out_specs=[ANY] * 3,
        out_shape=[
            jax.ShapeDtypeStruct((shards * rows, width), tokens.dtype),
            jax.ShapeDtypeStruct((shards,) + seg.shape, seg.dtype),
            jax.ShapeDtypeStruct((shards * qkv_w.shape[0], part), qkv_w.dtype),
        ],
        scratch_shapes=Spread.semaphores(shards)
        + Gather.semaphores(shards)
        + [pltpu.SemaphoreType.DMA((n,)), pltpu.SemaphoreType.DMA((n,)), pltpu.SemaphoreType.DMA],
        compiler_params=pltpu.CompilerParams(
            collective_id=0, has_side_effects=True, vmem_limit_bytes=40 * MIB
        ),
        name="first",
    )(tokens, seg, qkv_w)


def inverse_rms(values):
    return lax.rsqrt(jnp.mean(values * values, axis=-1, keepdims=True) + epsilon)


def doc_positions(seg_ids):
    index = jnp.arange(seg_ids.shape[0], dtype=jnp.int32)
    fresh = (index == 0) | (seg_ids != jnp.roll(seg_ids, 1))
    begins = lax.cummax(jnp.where(fresh, index, jnp.zeros_like(index)), axis=0)
    return index - begins


def rope_tables(positions):
    freqs = rope_base ** (-(jnp.arange(HEAD // 2, dtype=F32) * (2.0 / HEAD)))
    angles = freqs[:, None] * positions.astype(F32)[None, :]
    return (jnp.cos(angles), jnp.sin(angles))


def rotate(values, cos_t, sin_t):
    shaped = values.reshape(-1, 2, HEAD // 2, values.shape[1])
    first, second = shaped[:, 0], shaped[:, 1]
    turned = jnp.stack(
        [first * cos_t - second * sin_t, second * cos_t + first * sin_t], axis=1
    )
    return turned.reshape(values.shape)


def side_by_side(ref, start):
    return jnp.concatenate(
        [ref[h * HEAD : (h + 1) * HEAD, pl.ds(start, TILE)] for h in range(GROUP)], axis=1
    )


def block_bias(seg_col_ref, seg_row_ref, key_at, query_at):
    same = seg_col_ref[pl.ds(key_at, TILE), :] == seg_row_ref[:, pl.ds(query_at, TILE)]
    key_index = key_at + lax.broadcasted_iota(jnp.int32, (TILE, TILE), 0)
    query_index = query_at + lax.broadcasted_iota(jnp.int32, (TILE, TILE), 1)
    bias = jnp.where(same & (key_index <= query_index), 0.0, NEG).astype(F32)
    return jnp.concatenate([bias] * GROUP, axis=1)


def attend_kernel(
    shards, ffn_part, seg_col, seg_row, q_ref, k_ref, v_ref, cot, proj_w, gate_w, up_w,
    out_ref, lse_ref, cot_all, proj_m, gate_m, up_m, *sems,
):
    block = pl.program_id(1)
    at = pl.program_id(0) * pl.num_programs(1) + block
    steps = pl.num_programs(0) * pl.num_programs(1)
    rep, me = place()
    gate = Spread(shards, gate_w, gate_m, column_block(ffn_part), *sems[:3])
    up = Spread(shards, up_w, up_m, column_block(ffn_part), *sems[3:6])
    proj = Spread(shards, proj_w, proj_m, None, *sems[6:9])
    cots = Gather(shards, cot, cot_all, *sems[9:12])

    @pl.when(at == 0)
    def _():
        greet(plane_partners(rep, me, shards) + pair_partners(rep, me))
        proj.start()
        gate.start()
        up.start()
        cots.start()

    query_at = pl.multiple_of(block * TILE, TILE)
    queries = side_by_side(q_ref, query_at)
    wide = GROUP * TILE

    def step(c, carry):
        top, total, acc = carry
        key_at = pl.multiple_of(c * TILE, TILE)
        scores = dot(k_ref[0, pl.ds(key_at, TILE), :], queries, NN)
        scores = scores + block_bias(seg_col, seg_row, key_at, query_at)
        new_top = jnp.maximum(top, jnp.max(scores, axis=0, keepdims=True))
        expo = jnp.exp(scores - new_top)
        fade = jnp.exp(top - new_top)
        total = total * fade + jnp.sum(expo, axis=0, keepdims=True)
        acc = acc * fade + dot(v_ref[:, pl.ds(key_at, TILE)], expo.astype(BF16), NN)
        return new_top, total, acc

    start = (
        jnp.full((1, wide), NEG, F32),
        jnp.zeros((1, wide), F32),
        jnp.zeros((HEAD, wide), F32),
    )
    carry = step(block, start)
    top, total, acc = lax.fori_loop(0, block, step, carry)
    mixed = (acc / total).astype(BF16)
    lse = top + jnp.log(total)
    for h in range(GROUP):
        out_ref[h * HEAD : (h + 1) * HEAD, :] = mixed[:, h * TILE : (h + 1) * TILE]
        lse_ref[0, h : h + 1, :] = lse[:, h * TILE : (h + 1) * TILE]

    @pl.when(at == steps // 2)
    def _():
        proj.hand_on()

    @pl.when(at == steps - 1)
    def _():
        gate.hand_on()
        proj.hand_on_last()
        up.hand_on()
        cots.hand_on()
        gate.hand_on_last()
        up.hand_on_last()
        for transfer in (proj, gate, up, cots):
            transfer.finish()


def attend(q_t, k, v_t, seg, cot, proj_w, gate_w, up_w, shards):
    kv_heads, length, _ = k.shape
    blocks = length // TILE
    rows = GROUP * HEAD
    width = cot.shape[1]
    part = gate_w.shape[1] // shards
    return pl.pallas_call(
        functools.partial(attend_kernel, shards, part),
        grid=(kv_heads, blocks),
        in_specs=[
            pl.BlockSpec((length, 1), lambda g, n: (0, 0)),
            pl.BlockSpec((1, length), lambda g, n: (0, 0)),
            pl.BlockSpec((rows, length), lambda g, n: (g, 0)),
            pl.BlockSpec((1, length, HEAD), lambda g, n: (g, 0, 0)),
            pl.BlockSpec((HEAD, length), lambda g, n: (g, 0)),
        ]
        + [ANY] * 4,
        out_specs=[
            pl.BlockSpec((rows, TILE), lambda g, n: (g, n)),
            pl.BlockSpec((1, GROUP, TILE), lambda g, n: (g, 0, n)),
        ]
        + [ANY] * 4,
        out_shape=[
            jax.ShapeDtypeStruct(q_t.shape, BF16),
            jax.ShapeDtypeStruct((kv_heads, GROUP, length), F32),
            jax.ShapeDtypeStruct((length, width), BF16),
            jax.ShapeDtypeStruct((shards * proj_w.shape[0], width), BF16),
            jax.ShapeDtypeStruct((width, part), BF16),
            jax.ShapeDtypeStruct((width, part), BF16),
        ],
        scratch_shapes=3 * Spread.semaphores(shards) + Gather.semaphores(shards),
        compiler_params=pltpu.CompilerParams(
            collective_id=1, has_side_effects=True, vmem_limit_bytes=40 * MIB
        ),
        name="attend",
    )(seg[:, None], seg[None, :], q_t, k, v_t, cot, proj_w, gate_w, up_w)


def hidden_kernel(
    shards, mixed_t, proj_m, tokens, gain, hidden_ref, rms_ref, normed_all,
    mixed_own, normed, mix_send, mix_recv, gather_send, gather_recv, local_sem,
):
    rep, me = place()
    part, _ = mixed_t.shape
    count = tokens.shape[0]
    greet(plane_partners(rep, me, shards))

    def columns(shard):
        return mixed_t.at[:, pl.ds(pl.multiple_of(shard * count, count), count)]

    copies = [
        remote(columns(me ^ (i + 1)), mixed_own.at[i], mix_send, mix_recv, i, rep, me ^ (i + 1))
        for i in range(shards - 1)
    ]
    for copy in copies:
        copy.start()

    def product(block, shard):
        rows = proj_m[pl.ds(pl.multiple_of(shard * part, part), part), :]
        return dot(block, rows, TN)

    hidden_ref[...] = tokens[...].astype(F32) + product(
        mixed_t[:, pl.ds(pl.multiple_of(me * count, count), count)], me
    )
    for i, copy in enumerate(copies):
        copy.wait_recv()
        hidden_ref[...] += product(mixed_own[i], me ^ (i + 1))
    hidden = hidden_ref[...]
    rms = lax.rsqrt(jnp.mean(hidden * hidden, axis=-1, keepdims=True) + epsilon)
    rms_ref[...] = rms
    normed[...] = (hidden * rms * gain[...]).astype(BF16)
    gather = Gather(shards, normed, normed_all, gather_send, gather_recv, local_sem)
    gather.start()
    for copy in copies:
        copy.wait_send()
    gather.hand_on()
    gather.finish()


def hidden_layer(mixed_t, proj_m, tokens, gain, shards):
    part, length = mixed_t.shape
    count, width = tokens.shape
    n = shards - 1
    return pl.pallas_call(
        functools.partial(hidden_kernel, shards),
        in_specs=[IN_VMEM] * 4,
        out_specs=[IN_VMEM, IN_VMEM, ANY],
        out_shape=[
            jax.ShapeDtypeStruct((count, width), F32),
            jax.ShapeDtypeStruct((count, 1), F32),
            jax.ShapeDtypeStruct((length, width), BF16),
        ],
        scratch_shapes=[
            pltpu.VMEM((n, part, count), BF16),
            pltpu.VMEM((count, width), BF16),
            pltpu.SemaphoreType.DMA((n,)),
            pltpu.SemaphoreType.DMA((n,)),
        ]
        + Gather.semaphores(shards),
        compiler_params=pltpu.CompilerParams(
            collective_id=2, has_side_effects=True, vmem_limit_bytes=40 * MIB
        ),
        name="hidden",
    )(mixed_t, proj_m, tokens, gain[None, :])


def ffn_kernel(x_ref, cot_ref, gate_w, up_w, down_w, activ_ref, dgate_ref, dup_ref):
    def rows_of(m, _):
        here = pl.ds(pl.multiple_of(m * 256, 256), 256)
        x = x_ref[here, :]
        gate = dot(x, gate_w[...], NN)
        up = dot(x, up_w[...], NN)
        grad_activ = dot(cot_ref[here, :], down_w[...], NT)
        sigm = jax.nn.sigmoid(gate)
        swish = gate * sigm
        activ_ref[here, :] = (swish * up).astype(BF16)
        dup_ref[here, :] = (grad_activ * swish).astype(BF16)
        dgate_ref[here, :] = (
            grad_activ * up * sigm * (1.0 + gate * (1.0 - sigm))
        ).astype(BF16)
        return 0

    lax.fori_loop(0, x_ref.shape[0] // 256, rows_of, 0)


def ffn(x, cot, gate_w, up_w, down_w):
    length, width = x.shape
    part = gate_w.shape[1]
    tile = 256
    whole = pl.BlockSpec((length, width), lambda n: (0, 0))
    out = pl.BlockSpec((length, tile), lambda n: (0, n))
    return pl.pallas_call(
        ffn_kernel,
        grid=(part // tile,),
        in_specs=[
            whole,
            whole,
            pl.BlockSpec((width, tile), lambda n: (0, n)),
            pl.BlockSpec((width, tile), lambda n: (0, n)),
            pl.BlockSpec((tile, width), lambda n: (n, 0)),
        ],
        out_specs=[out] * 3,
        out_shape=[jax.ShapeDtypeStruct((length, part), BF16)] * 3,
        compiler_params=pltpu.CompilerParams(vmem_limit_bytes=56 * MIB),
        cost_estimate=pl.CostEstimate(
            flops=6 * length * width * part,
            bytes_accessed=2 * (2 * length * width + 3 * width * part + 3 * length * part),
            transcendentals=length * part,
        ),
        name="ffn",
    )(x, cot, gate_w, up_w, down_w)


def split_rows(ref, index, size):
    return ref.at[pl.ds(pl.multiple_of(index * size, size), size), :]


class Plan:
    def __init__(self, shards, reps, length, width, ffn_part, q_part, kv_part):
        self.shards, self.reps, self.length, self.width = shards, reps, length, width
        self.ffn_part, self.q_part, self.kv_part = ffn_part, q_part, kv_part
        self.layers = reps // 2
        self.half = self.layers // 2
        self.rows = width // 2
        self.own = width // shards
        self.block = self.own // 2
        self.proj_half = q_part // 2
        self.proj_blocks = self.rows // self.proj_half
        counts = [
            width // TILE, ffn_part // TILE, ffn_part // TILE,
            width // TILE // self.proj_blocks, q_part // TILE, 1,
        ]
        self.starts = [sum(counts[:i]) for i in range(7)]
        self.chunks = self.starts[6]
        lag = 1
        self.lag = lag
        self.meet = 1 + lag * self.half
        self.spread = 1 + lag * (self.layers - 1)
        self.hand = self.spread + lag
        self.slots = self.chunks + self.hand + 1
        self.mine_ring = 2 + lag * (self.half - 1)
        self.sum_ring = lag + 2


KEPT, CAME = 0, 1


def backward_kernel(
    plan, activ, dgate, dup, x, cot_all, back_part, res_part, hidden, cot, tokens, proj_w,
    qkv_m, normed,
    mlp_rms, mlp_gain, attn_gain, seg_col, seg_row, cos_ref, sin_ref, lse_ref, q_ref, mixed_ref,
    k_ref, kt_ref, v_ref,
    f_down, f_gate, f_up, f_proj, f_q, f_kv, result_ref, tokens_out, gains_out,
    swapped, from_outer, from_middle, totals, back_land, res_land, norm_land, norm_part,
    left_a, left_b, right, proj_v, qkv_v, hidden_v, cot_v, tokens_v, row_sum, land_v,
    mine, theirs, swap_v, outer_v, middle_v, sums, total_v,
    grad_hidden, gh_own, gh_all, g_t, back_t, dk_acc, dv_acc,
    gain_part, gain_land, gain_sum, gain_reps,
    load_sem, right_sem, small_sem, swap_send, swap_recv, in_send, outer_recv, middle_recv,
    out_send, total_recv, total_store, cross_recv, cross_send, keep_sem, pass_send, pass_recv,
    back_send, back_recv, res_send, res_recv, norm_send, norm_recv,
    gather_send, gather_recv, gather_local, gain_send, gain_recv, rep_send, rep_recv,
):
    p = plan
    shards, reps, n = p.shards, p.reps, p.shards - 1
    rep, me = place()
    core, layer = rep % 2, rep // 2
    upper = layer >= p.half
    depth = jnp.where(upper, p.layers - 1 - layer, layer)
    inward = jnp.where(upper, rep - 2, rep + 2)
    outward = jnp.where(upper, rep + 2, rep - 2)
    is_middle = depth == p.half - 1
    count = cot.shape[0]
    down_at, gate_at, up_at, proj_at, q_at, kv_at, end_at = p.starts
    half_rows = p.ffn_part // 2

    greet(plane_partners(rep, me, shards) + [(rep ^ i, me) for i in range(1, reps)])

    def load(src, dst, i):
        return pltpu.make_async_copy(src, dst, load_sem.at[i])

    load_activ = load(activ, left_a.at[:, pl.ds(0, p.ffn_part)], 0)
    load_x = load(x, left_b, 1)
    load_normed = load(normed, left_a.at[:, pl.ds(0, p.width)], 2)
    load_proj = load(proj_w, proj_v, 3)
    load_qkv = load(qkv_m, qkv_v, 4)
    load_hidden = load(hidden, hidden_v, 5)
    load_cot = load(cot, cot_v, 6)
    load_tokens = load(tokens, tokens_v, 7)

    def load_right(t):
        slot = right.at[t % 2]

        def copies(action):
            def tile(ref, first):
                at = pl.ds(pl.multiple_of((t - first) * TILE, TILE), TILE)
                return pltpu.make_async_copy(ref.at[:, at], slot, right_sem.at[t % 2])

            @pl.when(t < gate_at)
            def _():
                action(tile(cot_all, down_at))

            @pl.when((t >= gate_at) & (t < up_at))
            def _():
                action(tile(dgate, gate_at))

            @pl.when((t >= up_at) & (t < proj_at))
            def _():
                action(tile(dup, up_at))

        return copies

    def scatter(part, land, sends, recvs):
        return [
            remote(split_rows(part, me ^ (i + 1), count), land.at[i], sends, recvs, i, rep, me ^ (i + 1))
            for i in range(n)
        ]

    back_rows = scatter(back_part, back_land, back_send, back_recv)
    res_rows = scatter(res_part, res_land, res_send, res_recv)
    norm_rows = scatter(norm_part, norm_land, norm_send, norm_recv)

    def fetch_rows(copies, part, land):
        for copy in copies:
            copy.wait_recv()
        pieces = [split_rows(part, me, count)] + [land.at[i] for i in range(n)]
        loads = [
            pltpu.make_async_copy(piece, land_v.at[i % 2], small_sem.at[i % 2])
            for i, piece in enumerate(pieces)
        ]
        loads[0].start()
        for i, piece in enumerate(loads):
            if i + 1 < len(loads):
                loads[i + 1].start()
            piece.wait()

            def strip(here, i=i):
                value = land_v[i % 2, here, :].astype(F32)
                row_sum[here, :] = value if i == 0 else row_sum[here, :] + value

            strips(strip)

    STRIP = 32

    def strips(body):
        def go(i, carry):
            body(pl.ds(pl.multiple_of(i * STRIP, STRIP), STRIP))
            return carry

        lax.fori_loop(0, count // STRIP, go, 0)

    def norm_strip(here, values, rms, gain, row):
        grad_in = row_sum[here, :]
        weighted = grad_in * gain
        inner = jnp.mean(weighted * values, axis=-1, keepdims=True)
        gain_part[row : row + 1, :] += jnp.sum(grad_in * values * rms, axis=0, keepdims=True)
        return rms * weighted - values * (rms * rms * rms) * inner

    gather = Gather(shards, gh_own, gh_all, gather_send, gather_recv, gather_local)

    def hidden_back():
        load_hidden.wait()
        load_cot.wait()
        fetch_rows(back_rows, back_part, back_land)
        gain_part[...] = jnp.zeros_like(gain_part)

        def strip(here):
            grad = cot_v[here, :].astype(F32) + norm_strip(
                here, hidden_v[here, :], mlp_rms[here, :], mlp_gain[...], 1
            )
            grad_hidden[here, :] = grad
            gh_own[here, :] = grad.astype(BF16)

        strips(strip)
        gather.start()

    def finish_result():
        fetch_rows(res_rows, res_part, res_land)

        def strip(here):
            result_ref[here, :] = hidden_v[here, :] + row_sum[here, :]

        strips(strip)

    def mixed_back():
        gather.finish()
        load_proj.wait()

        def go(i, carry):
            here = pl.ds(pl.multiple_of(i * TILE, TILE), TILE)
            g_t[:, here] = dot(proj_v[...], gh_all[here, :], NT).astype(BF16)
            return carry

        lax.fori_loop(0, p.length // TILE, go, 0)

    blocks = p.length // TILE
    rows = GROUP * HEAD
    wide = GROUP * TILE
    mid = HEAD // 2

    def attention_unit(unit):
        g, block = unit // blocks, unit % blocks
        query_at = pl.multiple_of(block * TILE, TILE)
        here_q = pl.ds(query_at, TILE)

        def beside(ref):
            return jnp.concatenate(
                [
                    ref[pl.ds(pl.multiple_of(g * rows + h * HEAD, HEAD), HEAD), here_q]
                    for h in range(GROUP)
                ],
                axis=1,
            )

        queries, grads, mixed = beside(q_ref), beside(g_t), beside(mixed_ref)
        lse = jnp.concatenate([lse_ref[g, h : h + 1, here_q] for h in range(GROUP)], axis=1)
        inner = jnp.sum(grads.astype(F32) * mixed.astype(F32), axis=0, keepdims=True)

        @pl.when(block == 0)
        def _():
            dk_acc[...] = jnp.zeros_like(dk_acc)
            dv_acc[...] = jnp.zeros_like(dv_acc)

        def step(c, acc):
            key_at = pl.multiple_of(c * TILE, TILE)
            here = pl.ds(key_at, TILE)
            scores = dot(k_ref[g, here, :], queries, NN)
            scores = scores + block_bias(seg_col, seg_row, key_at, query_at)
            probs = jnp.exp(scores - lse)
            grad_probs = dot(v_ref[g, here, :], grads, NN)
            grad_scores = (probs * (grad_probs - inner)).astype(BF16)
            dv_acc[:, here] += dot(grads, probs.astype(BF16), NT)
            dk_acc[:, here] += dot(queries, grad_scores, NT)
            key_rows = pl.ds(pl.multiple_of(g * HEAD, HEAD), HEAD)
            return acc + dot(kt_ref[key_rows, here], grad_scores, NN)

        acc = lax.fori_loop(0, block + 1, step, jnp.zeros((HEAD, wide), F32))
        cos, sin = cos_ref[:, here_q], sin_ref[:, here_q]
        for h in range(GROUP):
            grad = acc[:, h * TILE : (h + 1) * TILE] * SCALE
            first, second = grad[:mid], grad[mid:]
            at = pl.multiple_of(g * rows + h * HEAD, HEAD)
            back_t[pl.ds(at, mid), here_q] = (first * cos + second * sin).astype(BF16)
            back_t[pl.ds(at + mid, mid), here_q] = (second * cos - first * sin).astype(BF16)

        @pl.when(block == blocks - 1)
        def _():
            cos, sin = cos_ref[...], sin_ref[...]
            first, second = dk_acc[:mid, :], dk_acc[mid:, :]
            at = pl.multiple_of(p.q_part + g * HEAD, HEAD)
            back_t[pl.ds(at, mid), :] = (first * cos + second * sin).astype(BF16)
            back_t[pl.ds(at + mid, mid), :] = (second * cos - first * sin).astype(BF16)
            at = pl.multiple_of(p.q_part + p.kv_part + g * HEAD, HEAD)
            back_t[pl.ds(at, HEAD), :] = dv_acc[...].astype(BF16)

    def normed_back():
        load_qkv.wait()

        stores = [
            pltpu.make_async_copy(
                land_v.at[i % 2], norm_part.at[pl.ds(i * count, count), :], small_sem.at[i % 2]
            )
            for i in range(shards)
        ]
        for i, store in enumerate(stores):
            if i >= 2:
                stores[i - 2].wait()
            here = pl.ds(i * count, count)
            land_v[i % 2] = dot(back_t[:, here].T, qkv_v[...], NT).astype(BF16)
            store.start()
        for store in stores[-2:]:
            store.wait()
        for copy in norm_rows:
            copy.start()

    gain_cols = p.width // shards

    def gain_slice(shard):
        return pl.ds(pl.multiple_of(shard * gain_cols, gain_cols), gain_cols)

    gain_plane = [
        remote(
            gain_part.at[:, gain_slice(me ^ (i + 1))], gain_land.at[me],
            gain_send, gain_recv, i, rep, me ^ (i + 1),
        )
        for i in range(n)
    ]
    gain_all = [
        remote(gain_sum, gain_reps.at[rep], rep_send, rep_recv, i, rep ^ (i + 1), me)
        for i in range(reps - 1)
    ]

    def tokens_back():
        load_tokens.wait()
        fetch_rows(norm_rows, norm_part, norm_land)

        def strip(here):
            values = tokens_v[here, :].astype(F32)
            rms = lax.rsqrt(jnp.mean(values * values, axis=-1, keepdims=True) + epsilon)
            tokens_out[here, :] = grad_hidden[here, :] + norm_strip(
                here, values, rms, attn_gain[...], 0
            )

        strips(strip)
        gain_land[me] = gain_part[:, gain_slice(me)]
        for copy in gain_plane:
            copy.start()

    def gains_plane():
        for copy in gain_plane:
            copy.wait_recv()
        total = gain_land[0]
        for s in range(1, shards):
            total = total + gain_land[s]
        gain_sum[...] = total
        gain_reps[rep] = total
        for copy in gain_all:
            copy.start()

    def gains_reps():
        for copy in gain_all:
            copy.wait_recv()
        total = gain_reps[0]
        for r in range(1, reps):
            total = total + gain_reps[r]
        gains_out[...] = total

    def swap(j):
        return remote(theirs.at[j % 2], swapped.at[j], swap_send, swap_recv, 0, rep ^ 1, me)

    def swap_copy(j):
        return pltpu.make_async_remote_copy(
            src_ref=theirs.at[j % 2], dst_ref=swapped.at[j],
            send_sem=swap_send.at[j % 2], recv_sem=swap_recv.at[j],
            device_id=(rep ^ 1, me), device_id_type=MESH,
        )

    def store_chunk(slot, other_slot, at, size, product, columns=TILE):
        here = pl.ds(pl.multiple_of(at, size), size)
        mine[slot, here, :columns] = product(core).astype(BF16)
        theirs[other_slot, here, :columns] = product(1 - core).astype(BF16)

    def make(t):
        slot, other = t % p.mine_ring, t % 2

        @pl.when(t >= 2)
        def _():
            swap_copy(t - 2).wait_send()

        @pl.when(t < proj_at)
        def _():
            load_right(t)(lambda copy: copy.wait())

        @pl.when(t + 1 < proj_at)
        def _():
            load_right(t + 1)(lambda copy: copy.start())

        @pl.when(t < gate_at)
        def _():
            size = min(TILE, half_rows)

            def go(i, carry):
                def product(which):
                    at = pl.multiple_of(which * half_rows + i * size, size)
                    return dot(left_a[:, pl.ds(at, size)], right[t % 2], TN)

                store_chunk(slot, other, i * size, size, product)
                return carry

            lax.fori_loop(0, half_rows // size, go, 0)

        def wide_chunk(left, factor, columns):
            def go(s, carry):
                def product(which):
                    at = pl.multiple_of(s * p.own + which * p.block, p.block)
                    return dot(left[:, pl.ds(at, p.block)], factor(), TN)

                store_chunk(slot, other, s * p.block, p.block, product, columns)
                return carry

            lax.fori_loop(0, shards, go, 0)

        @pl.when((t >= gate_at) & (t < proj_at))
        def _():
            wide_chunk(left_b, lambda: right[t % 2], TILE)

        @pl.when((t >= proj_at) & (t < q_at))
        def _():
            def go(i, carry):
                at = pl.multiple_of(((t - proj_at) * p.proj_blocks + i) * TILE, TILE)

                def product(which):
                    part = pl.ds(pl.multiple_of(which * p.proj_half, p.proj_half), p.proj_half)
                    return dot(mixed_ref[part, :], gh_all[:, pl.ds(at, TILE)], NN)

                store_chunk(slot, other, i * p.proj_half, p.proj_half, product)
                return carry

            lax.fori_loop(0, p.proj_blocks, go, 0)

        @pl.when((t >= q_at) & (t < kv_at))
        def _():
            at = pl.multiple_of((t - q_at) * TILE, TILE)
            right[t % 2] = back_t[pl.ds(at, TILE), :].T
            wide_chunk(left_a, lambda: right[t % 2], TILE)

        @pl.when(t == kv_at)
        def _():
            columns = 2 * p.kv_part
            right[t % 2, :, :columns] = back_t[p.q_part :, :].T
            wide_chunk(left_a, lambda: right[t % 2, :, :columns], columns)

        swap_copy(t).start()

    def inward_copies(j):
        common = dict(
            src_ref=sums.at[j % p.sum_ring], send_sem=in_send.at[j % p.sum_ring],
            device_id=(inward, me), device_id_type=MESH,
        )
        to_layer = pltpu.make_async_remote_copy(
            dst_ref=from_outer.at[j], recv_sem=outer_recv.at[j], **common
        )
        to_middle = pltpu.make_async_remote_copy(
            dst_ref=from_middle.at[j], recv_sem=middle_recv.at[j], **common
        )
        return to_layer, to_middle

    def outward_copy(src, j):
        return pltpu.make_async_remote_copy(
            src_ref=src, dst_ref=totals.at[j], send_sem=out_send.at[j % 2],
            recv_sem=total_recv.at[j], device_id=(outward, me), device_id_type=MESH,
        )

    def add_rows(body):
        def go(i, carry):
            body(pl.ds(pl.multiple_of(i * TILE, TILE), TILE))
            return carry

        lax.fori_loop(0, p.rows // TILE, go, 0)

    def send_inward(j):
        @pl.when((j >= 0) & (j < p.chunks))
        def _():
            swap_copy(j).wait_recv()
            first = pltpu.make_async_copy(swapped.at[j], swap_v, small_sem.at[2])
            second = pltpu.make_async_copy(from_outer.at[j], outer_v, small_sem.at[3])
            first.start()

            @pl.when(depth > 0)
            def _():
                inward_copies(j)[0].wait_recv()
                second.start()

            @pl.when(j >= p.sum_ring)
            def _():
                inward_copies(j - p.sum_ring)[0].wait_send()

            first.wait()
            ours = mine.at[j % p.mine_ring]
            total = sums.at[j % p.sum_ring]

            @pl.when(depth > 0)
            def _():
                second.wait()

                def add(here):
                    total[here, :] = (
                        ours[here, :].astype(F32)
                        + swap_v[here, :].astype(F32)
                        + outer_v[here, :].astype(F32)
                    ).astype(BF16)

                add_rows(add)

            @pl.when(depth == 0)
            def _():
                def add(here):
                    total[here, :] = (
                        ours[here, :].astype(F32) + swap_v[here, :].astype(F32)
                    ).astype(BF16)

                add_rows(add)

            to_layer, to_middle = inward_copies(j)

            @pl.when(is_middle)
            def _():
                to_middle.start()

            @pl.when(jnp.logical_not(is_middle))
            def _():
                to_layer.start()

    def store_total(j):
        return pltpu.make_async_copy(total_v.at[j % 2], totals.at[j], total_store.at[j % 2])

    def meet_in_middle(j):
        @pl.when(is_middle & (j >= 0) & (j < p.chunks))
        def _():
            inward_copies(j)[1].wait_recv()
            fetch = pltpu.make_async_copy(from_middle.at[j], middle_v, small_sem.at[4])
            fetch.start()

            if p.half > 1:

                @pl.when(j >= 2)
                def _():
                    outward_copy(total_v.at[j % 2], j - 2).wait_send()

            fetch.wait()
            out, held = total_v.at[j % 2], sums.at[j % p.sum_ring]

            def add(here):
                out[here, :] = (
                    held[here, :].astype(F32) + middle_v[here, :].astype(F32)
                ).astype(BF16)

            add_rows(add)
            if p.half > 1:
                outward_copy(out, j).start()
            store_total(j).start()
            store_total(j).wait()

    def send_outward(j):
        @pl.when(jnp.logical_not(is_middle) & (j >= 0) & (j < p.chunks))
        def _():
            outward_copy(totals.at[j], j).wait_recv()

            @pl.when(depth > 0)
            def _():
                @pl.when(j >= 2)
                def _():
                    outward_copy(totals.at[j], j - 2).wait_send()

                outward_copy(totals.at[j], j).start()

    def put_down(blocks_of, sem):
        for src, dst in blocks_of:
            pltpu.make_async_copy(src, dst, keep_sem.at[sem]).start()
            remote_pass(src, dst, sem).start()

    def remote_pass(src, dst, sem):
        return pltpu.make_async_remote_copy(
            src_ref=src, dst_ref=dst, send_sem=pass_send.at[sem], recv_sem=pass_recv.at[sem],
            device_id=(rep ^ 1, me), device_id_type=MESH,
        )

    def window(full, shard, part, tile, columns=TILE):
        at = pl.multiple_of(shard * part + tile * columns, columns)
        return full.at[pl.ds(pl.multiple_of(core * p.block, p.block), p.block), pl.ds(at, columns)]

    WIDE = (
        (gate_at, up_at, f_gate, p.ffn_part, 1, TILE),
        (up_at, proj_at, f_up, p.ffn_part, 2, TILE),
        (q_at, kv_at, f_q, p.q_part, 4, TILE),
        (kv_at, end_at, f_kv, 2 * p.kv_part, 5, 2 * p.kv_part),
    )

    def spread_total(j):
        @pl.when((j >= 0) & (j < gate_at))
        def _():
            at = pl.ds(pl.multiple_of(j * TILE, TILE), TILE)
            here = pl.ds(pl.multiple_of(core * half_rows, half_rows), half_rows)
            put_down([(totals.at[j, pl.ds(0, half_rows), :], f_down.at[here, at])], 0)

        @pl.when((j >= proj_at) & (j < q_at))
        def _():
            here = pl.ds(pl.multiple_of(core * p.proj_half, p.proj_half), p.proj_half)
            pairs = []
            for i in range(p.proj_blocks):
                at = pl.multiple_of(((j - proj_at) * p.proj_blocks + i) * TILE, TILE)
                src = totals.at[j, pl.ds(i * p.proj_half, p.proj_half), :]
                pairs.append((src, f_proj.at[here, pl.ds(at, TILE)]))
            put_down(pairs, 3)

        for first, last, full, part, sem, columns in WIDE:

            @pl.when((j >= first) & (j < last))
            def _():
                def block(shard):
                    at = pl.ds(pl.multiple_of(shard * p.block, p.block), p.block)
                    return totals.at[j, at, pl.ds(0, columns)]

                place_here = window(full, me, part, j - first, columns)
                for i in range(n):
                    pltpu.make_async_remote_copy(
                        src_ref=block(me ^ (i + 1)), dst_ref=place_here,
                        send_sem=cross_send.at[sem], recv_sem=cross_recv.at[j],
                        device_id=(rep, me ^ (i + 1)), device_id_type=MESH,
                    ).start()
                put_down([(block(me), place_here)], sem)

    def pass_on(j):
        for first, last, full, part, sem, columns in WIDE:

            @pl.when((j >= first) & (j < last))
            def _():
                came = totals.at[j, pl.ds(0, n * p.block), pl.ds(0, columns)]
                pltpu.make_async_copy(came, came, cross_recv.at[j]).wait()
                for i in range(n):
                    here = window(full, me ^ (i + 1), part, j - first, columns)
                    remote_pass(here, here, sem).start()

    load_activ.start()
    load_right(0)(lambda copy: copy.start())
    for copy in back_rows:
        copy.start()
    for copy in (load_x, load_hidden, load_cot, load_proj, load_qkv, load_tokens):
        copy.start()
    load_activ.wait()

    units = (p.length // TILE) * (p.kv_part // HEAD)
    rows_slot, pass_slot, mixed_slot = 4, 6, 8
    unit_slot = mixed_slot + 1
    per_slot = 2
    last_unit_slot = unit_slot + (units + per_slot - 1) // per_slot
    result_slot = last_unit_slot
    norm_slot = last_unit_slot
    tokens_slot = norm_slot + 5
    gain_slot = tokens_slot + 1
    rep_slot = gain_slot + 1
    assert proj_at > mixed_slot and q_at > norm_slot and rep_slot < p.slots

    def slot(t, carry):
        send_inward(t - 1 - p.lag * depth)
        meet_in_middle(t - p.meet)
        send_outward(t - p.spread + p.lag * depth)
        spread_total(t - p.spread)
        pass_on(t - p.hand)

        @pl.when(t == gate_at)
        def _():
            load_x.wait()
            load_normed.start()

        @pl.when(t == q_at)
        def _():
            load_normed.wait()

        @pl.when(t < p.chunks)
        def _():
            make(t)

        def at(when, action):
            @pl.when(t == when)
            def _():
                action()

        at(rows_slot, hidden_back)
        at(pass_slot, gather.hand_on)
        at(mixed_slot, mixed_back)

        @pl.when((t >= unit_slot) & (t < last_unit_slot))
        def _():
            def go(i, c):
                attention_unit((t - unit_slot) * per_slot + i)
                return c

            lax.fori_loop(0, per_slot, go, 0)

        def start_result():
            for copy in res_rows:
                copy.start()

        at(unit_slot, start_result)
        at(result_slot, finish_result)
        at(norm_slot, normed_back)
        at(tokens_slot, tokens_back)
        at(gain_slot, gains_plane)
        at(rep_slot, gains_reps)
        return carry

    lax.fori_loop(0, p.slots, slot, 0)

    for j in range(max(0, p.chunks - 2), p.chunks):
        swap_copy(j).wait_send()
    for j in range(max(0, p.chunks - p.sum_ring), p.chunks):
        inward_copies(j)[0].wait_send()
    if p.half > 1:

        @pl.when(depth > 0)
        def _():
            for j in range(max(0, p.chunks - 2), p.chunks):
                outward_copy(total_v.at[j % 2], j).wait_send()

    for copies in (back_rows, res_rows, norm_rows, gain_plane, gain_all):
        for copy in copies:
            copy.wait_send()

    def settle(ref, sem):
        pltpu.make_async_copy(ref, ref, sem).wait()

    for sem, full in ((0, f_down), (3, f_proj)):
        part = full.at[pl.ds(0, full.shape[0] // 2), :]
        settle(part, keep_sem.at[sem])
        settle(part, pass_send.at[sem])
        settle(part, pass_recv.at[sem])
    for _, _, full, part, sem, _ in WIDE:
        here = full.at[pl.ds(0, p.block), :]
        settle(here, pass_send.at[sem])
        settle(here, pass_recv.at[sem])
        settle(full.at[pl.ds(0, p.block), pl.ds(0, part)], keep_sem.at[sem])
        settle(full.at[pl.ds(0, p.block), pl.ds(0, n * part)], cross_send.at[sem])


def backward(
    shards, reps, activ, dgate, dup, x, cot_all, back_part, res_part, hidden, cot, tokens, proj_w,
    qkv_m, normed, mlp_rms, mlp_gain, attn_gain, seg, cos_t, sin_t, lse, q_t, mixed_t, k, k_t, v,
):
    length, width = x.shape
    count = cot.shape[0]
    ffn_part = activ.shape[1]
    q_part, kv_part = q_t.shape[0], k_t.shape[0]
    n = shards - 1
    p = Plan(shards, reps, length, width, ffn_part, q_part, kv_part)
    shape = jax.ShapeDtypeStruct
    own = width // shards
    chunk = (p.rows, TILE)
    dma = pltpu.SemaphoreType.DMA
    lefts = max(ffn_part, width)
    return pl.pallas_call(
        functools.partial(backward_kernel, p),
        in_specs=[ANY] * 13 + [IN_VMEM] * 13,
        out_specs=[ANY] * 6 + [IN_VMEM] * 3 + [ANY] * 8,
        out_shape=[
            shape((ffn_part, width), BF16),
            shape((own, shards * ffn_part), BF16),
            shape((own, shards * ffn_part), BF16),
            shape((q_part, width), BF16),
            shape((own, shards * q_part), BF16),
            shape((own, shards * 2 * kv_part), BF16),
            shape((count, width), F32),
            shape((count, width), F32),
            shape((8, width // shards), F32),
        ]
        + [shape((p.chunks,) + chunk, BF16)] * 4
        + [shape((n, count, width), BF16)] * 3
        + [shape((length, width), BF16)],
        scratch_shapes=[
            pltpu.VMEM((length, lefts), BF16),
            pltpu.VMEM((length, width), BF16),
            pltpu.VMEM((2, length, TILE), BF16),
            pltpu.VMEM(proj_w.shape, BF16),
            pltpu.VMEM(qkv_m.shape, BF16),
            pltpu.VMEM((count, width), F32),
            pltpu.VMEM((count, width), BF16),
            pltpu.VMEM((count, width), BF16),
            pltpu.VMEM((count, width), F32),
            pltpu.VMEM((2, count, width), BF16),
            pltpu.VMEM((p.mine_ring,) + chunk, BF16),
            pltpu.VMEM((2,) + chunk, BF16),
            pltpu.VMEM(chunk, BF16),
            pltpu.VMEM(chunk, BF16),
            pltpu.VMEM(chunk, BF16),
            pltpu.VMEM((p.sum_ring,) + chunk, BF16),
            pltpu.VMEM((2,) + chunk, BF16),
            pltpu.VMEM((count, width), F32),
            pltpu.VMEM((count, width), BF16),
            pltpu.VMEM((length, width), BF16),
            pltpu.VMEM((q_part, length), BF16),
            pltpu.VMEM((q_part + 2 * kv_part, length), BF16),
            pltpu.VMEM((HEAD, length), F32),
            pltpu.VMEM((HEAD, length), F32),
            pltpu.VMEM((8, width), F32),
            pltpu.VMEM((shards, 8, own), F32),
            pltpu.VMEM((8, own), F32),
            pltpu.VMEM((reps, 8, own), F32),
            dma((8,)), dma((2,)), dma((5,)), dma((2,)), dma((p.chunks,)), dma((p.sum_ring,)),
            dma((p.chunks,)), dma((p.chunks,)), dma((2,)), dma((p.chunks,)), dma((2,)),
            dma((p.chunks,)), dma((6,)), dma((6,)), dma((6,)), dma((6,)),
            dma((n,)), dma((n,)), dma((n,)), dma((n,)), dma((n,)), dma((n,)),
        ]
        + Gather.semaphores(shards)
        + [dma((n,)), dma((n,)), dma((reps - 1,)), dma((reps - 1,))],
        compiler_params=pltpu.CompilerParams(
            collective_id=3, has_side_effects=True, vmem_limit_bytes=62 * MIB
        ),
        name="backward",
    )(
        activ, dgate, dup, x, cot_all, back_part, res_part, hidden, cot, tokens, proj_w,
        qkv_m, normed, mlp_rms, mlp_gain[None, :], attn_gain[None, :], seg[:, None], seg[None, :],
        cos_t, sin_t, lse, q_t, mixed_t, k, k_t, v,
    )[:9]


def local(
    tokens, segments, query_w, key_w, value_w, proj_w, attn_gain,
    gate_w, up_w, down_w, mlp_gain, cotangent,
):
    shards = lax.axis_size("shard")
    reps = lax.axis_size("rep")
    tok_count, width = tokens.shape
    kv_part = key_w.shape[1] // shards
    q_part = query_w.shape[1] // shards
    length = tok_count * shards

    qkv_w = jnp.concatenate(
        [
            w[:, s * (w.shape[1] // shards) : (s + 1) * (w.shape[1] // shards)]
            for s in range(shards)
            for w in (query_w, key_w, value_w)
        ],
        axis=1,
    )
    tokens_all, seg, qkv_m = first(tokens, segments[None, :], qkv_w, shards)
    seg = seg.reshape(length)

    cos_t, sin_t = rope_tables(doc_positions(seg))
    inputs_all = tokens_all.astype(F32)
    normed = (inputs_all * inverse_rms(inputs_all) * attn_gain).astype(BF16)
    qkv_t = dot(qkv_m, normed, TT)
    q_t = (rotate(qkv_t[:q_part], cos_t, sin_t).astype(BF16).astype(F32) * SCALE).astype(BF16)
    k_t = rotate(qkv_t[q_part : q_part + kv_part], cos_t, sin_t).astype(BF16)
    v_t = qkv_t[q_part + kv_part :].astype(BF16)
    k = k_t.reshape(-1, HEAD, length).transpose(0, 2, 1)
    v = v_t.reshape(-1, HEAD, length).transpose(0, 2, 1)
    mixed_t, lse, cot_all, proj_m, gate_m, up_m = attend(
        q_t, k, v_t, seg, cotangent, proj_w, gate_w, up_w, shards
    )
    hidden, mlp_rms, normed_mlp = hidden_layer(mixed_t, proj_m, tokens, mlp_gain, shards)

    activ, dgate, dup = ffn(normed_mlp, cot_all, gate_m, up_m, down_w)
    back_part = (dot(dgate, gate_m, NT) + dot(dup, up_m, NT)).astype(BF16)
    res_part = dot(activ, down_w, NN).astype(BF16)
    down, gate, up, proj, query, kv, result, grad_tokens, gains = backward(
        shards, reps, activ, dgate, dup, normed_mlp, cot_all, back_part, res_part, hidden,
        cotangent, tokens, proj_w, qkv_m, normed, mlp_rms, mlp_gain, attn_gain, seg,
        cos_t, sin_t, lse, q_t, mixed_t, k, k_t, v,
    )

    def every_other(first):
        parts = [
            kv[:, (2 * s + first) * kv_part : (2 * s + first + 1) * kv_part] for s in range(shards)
        ]
        return jnp.concatenate(parts, axis=1).astype(F32)

    return (
        result, grad_tokens, query.astype(F32), every_other(0), every_other(1), proj.astype(F32),
        gains[0], gate.astype(F32), up.astype(F32), down.astype(F32), gains[1],
    )


def solution(mesh):
    rows = P(("rep", "shard"), None)
    held = P("shard", None)
    in_specs = (
        rows, P(("rep", "shard")), held, held, held, held, P(), held, held, held, P(), rows,
    )
    out_specs = (
        rows, rows, held, held, held, held, P("shard"), held, held, held, P("shard"),
    )
    return jax.shard_map(local, mesh=mesh, in_specs=in_specs, out_specs=out_specs, check_vma=False)
```

time: 3720 us -> 851 us (0.23)
  waiting for transfers between devices: 3200 us -> 0 us
  Pallas kernels: 0 us -> 714 us
  matrix products: 337 us -> 46.8 us
  other arithmetic: 105 us -> 50.4 us
  blocking collectives: 38 us -> 0 us
    unnamed x17 -> x0, waiting for transfers between devices: 1400 us -> none
    all_gather x9 -> x0, waiting for transfers between devices: 1080 us -> none  [the longest x1 293 us: local(): lax.all_gather(gate_w, 'shard', axis=0, tiled=True)]
    pallas_call x0 -> x5, Pallas kernels: none -> 714 us  [the longest x1 444 us: backward(): pl.pallas_call(functools.partial(backward_kernel, p), in_specs=[ANY] * 13...]
    psum x1 -> x0, waiting for transfers between devices: 532 us -> none  [local(): lax.psum(grad_query.astype(jnp.bfloat16), 'rep').astype(jnp.float32)]
    dot_general x74 -> x4, matrix products: 337 us -> 46.8 us  [dot(): lax.dot_general(left, right, (dims, ((), ())), preferred_element_type=F32)]
    reduce_scatter x3 -> x0, waiting for transfers between devices: 184 us -> none  [the longest x1 137 us: local(): lax.psum_scatter(jnp.concatenate([left_part, right_part], axis=1).astype(...]
  transfers between devices with their start and end apart: 15 -> 0, of which waited for: 15 -> 0; matrix products, arithmetic and copies ran while one was open for 6% -> 0% of each run, Pallas kernels for 0% -> 0%
where the time goes in v1:
time: 851 us; the launch traced here: 847 us
  Pallas kernels  714 us (84%)
  other arithmetic  50.4 us (6%)
  matrix products  46.8 us (5%)
  local copies, waits for them, and re-layouts  35 us (4%)
    pallas_call x1, Pallas kernels, backward(): pl.pallas_call(functools.partial(backward_kernel, p), in_specs=[ANY] * 13...  444 us
    pallas_call x1, Pallas kernels, attend(): pl.pallas_call(functools.partial(attend_kernel, shards, part), grid=(kv_h...  131 us
    pallas_call x1, Pallas kernels, hidden_layer(): pl.pallas_call(functools.partial(hidden_kernel, shards), in_specs=[IN_VME...  52.9 us
    pallas_call x1, Pallas kernels, first(): pl.pallas_call(functools.partial(first_kernel, shards, part), in_specs=[A...  47.6 us
    dot_general x4, matrix products, dot(): lax.dot_general(left, right, (dims, ((), ())), preferred_element_type=F32)  46.8 us
    pallas_call x1, Pallas kernels, ffn(): pl.pallas_call(ffn_kernel, grid=(part // tile,), in_specs=[whole, whole,...  38.5 us
    unnamed x79, local copies, waits for them, and re-layouts  27.4 us

profile of v1, /device:TPU:0, one launch (start us, length us, event | category | flops | bytes accessed | tf_op | source)
XLA Modules:
  0.0 847.1 jit_solution(2883989845044406796)
XLA Ops:
  0.6 0.0 copy-start.29
  0.7 0.0 copy-start.28
  0.7 0.0 copy-start.2
  0.7 1.2 slice_dynamic-update-slice_fusion.3
  1.9 0.9 slice_dynamic-update-slice_fusion.11
  2.9 0.9 slice_dynamic-update-slice_fusion.10
  3.8 1.1 slice_dynamic-update-slice_fusion.2
  5.0 0.9 slice_dynamic-update-slice_fusion.9
  5.9 0.9 slice_dynamic-update-slice_fusion.8
  6.9 1.1 slice_dynamic-update-slice_fusion.1
  8.1 1.1 slice_dynamic-update-slice_fusion
  9.2 0.1 slice_dynamic-update-slice_fusion.5
  9.3 0.0 copy-start.30
  9.4 47.6 %first.1 = (bf16[1024,2048]{1,0:T(8,128)(2,1)S(1)}, s32[4,1,256]{2,1,0:T(1,128)S(1)}, bf16[2048,768]{1,0:T(8,128)(2,1)S(1)}) custom-call(bf16[256,2048]{1,0:T(8,128)(2,1)S(1)} %copy-done.2, s32[1,256]{1,0:T(1,128)S(1)} %bitcast.49, bf16[512,3072]{1,0:T(8,128)(2,1)S(1)} %slice_dynamic-update-slice_fusion.4.qkv), custom_call_target="tpu_custom_call" | custom-call | tf_op jit(solution)/shard_map/first/pallas_call | solution.py:227
  57.0 0.0 copy-start
  57.0 2.0 copy-done
  59.0 1.6 copy-done.11
  60.6 0.6 slice.117
  61.2 0.7 fusion.5
  61.9 0.3 reduce-window.9
  62.2 0.1 slice.119
  62.3 0.1 slice_reduce_fusion
  62.5 0.1 fusion.4
  62.5 3.2 fusion
  65.8 3.0 fusion.2.normed
  68.8 0.5 multiply_cosine_fusion
  69.4 0.2 copy.25.seg_col
  69.6 6.4 fusion.10
  76.0 0.0 copy-start.18
  76.1 1.7 copy-done.18
  77.7 1.0 copy.26
  78.8 1.6 slice-done.1
  80.4 0.3 subtract_convert_fusion
  80.7 0.2 multiply_convert_fusion
  80.9 0.0 copy-start.3
  81.0 0.1 multiply_subtract_fusion
  81.1 1.1 copy.24
  82.2 1.6 copy-done.4
  83.8 1.0 copy-done.6
  84.8 1.2 copy-done.9
  86.0 130.5 %attend.1 = (bf16[512,1024]{1,0:T(8,128)(2,1)S(1)}, f32[2,4,1024]{2,1,0:T(4,128)S(1)}, bf16[1024,2048]{1,0:T(8,128)(2,1)S(1)}, bf16[2048,2048]{1,0:T(8,128)(2,1)...) custom-call(s32[1024,1]{1,0:T(8,128)S(1)} %copy.25.seg_col, s32[1,1024]{1,0:T(1,128)S(1)} %bitcast.45, ...), custom_call_target="tpu_custom_call" | custom-call | tf_op jit(solution)/shard_map/attend/pallas_call | solution.py:358
  216.6 0.0 copy-start.7
  216.6 2.0 copy-done.7
  218.6 52.9 %hidden.1 = (f32[256,2048]{1,0:T(8,128)S(1)}, f32[256,1]{1,0:T(8,128)S(1)}, bf16[1024,2048]{1,0:T(8,128)(2,1)S(1)}) custom-call(bf16[512,1024]{1,0:T(8,128)(2,1)S(1)} %get-tuple-element.38.mixed_t.mixed_ref, bf16[2048,2048]{1,0:T(8,128)(2,1)} %get-tuple-element.39.proj_m, bf16[256,2048]{1,0:T(8,128)(2,1)S(1)} %copy-done.2, f32[1,2048]{1,0:T(1,128)S(1)} %bitcast.48), custom_call_target="tpu_custom_call" | custom-call | tf_op jit(solution)/shard_map/hidden/pallas_call | solution.py:435
  271.5 0.0 copy-start.8
  271.5 2.0 copy-done.8
  273.5 1.3 copy-done.12
  274.8 0.7 copy-done.13
  275.5 38.5 %ffn.1 = (bf16[1024,2048]{1,0:T(8,128)(2,1)}, bf16[1024,2048]{1,0:T(8,128)(2,1)}, bf16[1024,2048]{1,0:T(8,128)(2,1)}) custom-call(bf16[1024,2048]{1,0:T(8,128)(2,1)} %copy-done.8, bf16[1024,2048]{1,0:T(8,128)(2,1)} %copy-done.7, bf16[2048,2048]{1,0:T(8,128)(2,1)} %get-tuple-element.42.gate_w, bf16[2048,2048]{1,0:T(8,128)(2,1)} %get-tuple-element.43.up_w, ...), custom_call_target="tpu_custom_call" | custom-call | flops 25769803776 | bytes 46137344 | tf_op jit(solution)/shard_map/ffn/pallas_call | solution.py:483
  314.0 14.9 %fusion.11 = f32[1024,2048]{1,0:T(8,128)} fusion(bf16[1024,2048]{1,0:T(8,128)(2,1)} %get-tuple-element.45.dgate, bf16[2048,2048]{1,0:T(8,128)(2,1)} %get-tuple-element.42.gate_w), kind=kOutput, calls=%fused_computation.44 | convolution fusion | flops 8589934592 | bytes 20971520 | tf_op jit(solution)/shard_map/dot_general | solution.py:27
  328.9 15.1 %add_convert_fusion.back_part = bf16[1024,2048]{1,0:T(8,128)(2,1)} fusion(f32[1024,2048]{1,0:T(8,128)} %fusion.11, bf16[1024,2048]{1,0:T(8,128)(2,1)S(1)} %copy-done.20, bf16[2048,2048]{1,0:T(8,128)(2,1)} %get-tuple-element.43.up_w), kind=kOutput, calls=%fused_computation.5 | convolution fusion | flops 8594128896 | bytes 25165824 | tf_op jit(solution)/shard_map/dot_general | solution.py:27
  344.0 10.4 %convolution_convert_fusion.res_part = bf16[1024,2048]{1,0:T(8,128)(2,1)} fusion(bf16[1024,2048]{1,0:T(8,128)(2,1)S(1)} %copy-done.19, bf16[2048,2048]{1,0:T(8,128)(2,1)S(1)} %bitcast.59), kind=kOutput, calls=%fused_computation.6 | convolution fusion | flops 8592031744 | bytes 16777216 | tf_op jit(solution)/shard_map/dot_general | solution.py:27
  354.4 444.3 %backward.1 = (bf16[2048,2048]{1,0:T(8,128)(2,1)}, bf16[512,8192]{1,0:T(8,128)(2,1)}, bf16[512,8192]{1,0:T(8,128)(2,1)}, bf16[512,2048]{1,0:T(8,128)(2,1)}, bf16...) custom-call(bf16[1024,2048]{1,0:T(8,128)(2,1)} %get-tuple-element.44, ...), custom_call_target="tpu_custom_call" | custom-call | tf_op jit(solution)/shard_map/backward/pallas_call | solution.py:1212
  798.7 1.5 fusion.9
  800.2 1.4 fusion.8
  801.6 1.5 maximum_convert_fusion.1
  803.0 2.5 convert_element_type.70
  805.6 2.5 convert_element_type.73
  808.1 11.7 %convert_element_type.74 = f32[512,8192]{1,0:T(8,128)} convert(bf16[512,8192]{1,0:T(8,128)(2,1)} %get-tuple-element.56) | non-fusion elementwise | flops 4194304 | bytes 25165824 | tf_op jit(solution)/shard_map/convert_element_type | solution.py:1330
  819.8 11.7 %convert_element_type.75 = f32[512,8192]{1,0:T(8,128)} convert(bf16[512,8192]{1,0:T(8,128)(2,1)} %get-tuple-element.57) | non-fusion elementwise | flops 4194304 | bytes 25165824 | tf_op jit(solution)/shard_map/convert_element_type | solution.py:1330
  831.6 11.8 %convert_element_type.76 = f32[2048,2048]{1,0:T(8,128)} convert(bf16[2048,2048]{1,0:T(8,128)(2,1)} %get-tuple-element.58) | non-fusion elementwise | flops 4194304 | bytes 25165824 | tf_op jit(solution)/shard_map/convert_element_type | solution.py:1330
  843.4 1.3 copy.41
  844.7 1.0 copy-done.26
  845.8 1.3 copy.42
  (58 shorter events, 0.3 us)
Async XLA Ops:
  0.6 7.4 copy-start.29
  0.7 7.3 copy-start.28
  0.7 8.7 %copy-start.2 = (bf16[256,2048]{1,0:T(8,128)(2,1)S(1)}, bf16[256,2048]{1,0:T(8,128)(2,1)}, u32[]{:S(2)}) copy-start(bf16[256,2048]{1,0:T(8,128)(2,1)} %tokens.5) | copy-start | bytes 3145732
  0.7 8.7 %copy-start.17 = (s32[256]{0:T(256)S(1)}, s32[256]{0:T(256)}, u32[]{:S(2)}) copy-start(s32[256]{0:T(256)} %param.13) | copy-start | bytes 3076
  9.3 56.4 %copy-start.30 = (f32[2048]{0:T(1024)S(1)}, f32[2048]{0:T(1024)}, u32[]{:S(2)}) copy-start(f32[2048]{0:T(1024)} %param.18) | copy-start | bytes 24580
  57.0 2.0 copy-start
  59.0 1.6 copy-start.11
  60.6 21.5 %copy-start.14 = (s32[4,1,256]{2,1,0:T(1,128)}, s32[4,1,256]{2,1,0:T(1,128)S(1)}, u32[]{:S(2)}) copy-start(s32[4,1,256]{2,1,0:T(1,128)S(1)} %get-tuple-element.35) | copy-start | bytes 12292
  62.3 3.5 copy-start.1
  69.4 11.6 %copy-start.22 = (f32[32,1024]{1,0:T(8,128)}, f32[32,1024]{1,0:T(8,128)S(1)}, u32[]{:S(2)}) copy-start(f32[32,1024]{1,0:T(8,128)S(1)} %get-tuple-element.73.cos_ref) | copy-start | bytes 393220
  69.4 11.6 %copy-start.23 = (f32[32,1024]{1,0:T(8,128)}, f32[32,1024]{1,0:T(8,128)S(1)}, u32[]{:S(2)}) copy-start(f32[32,1024]{1,0:T(8,128)S(1)} %get-tuple-element.74.sin_ref) | copy-start | bytes 393220
  69.6 12.5 %copy-start.5 = (s32[1024,1]{1,0:T(8,128)}, s32[1024,1]{1,0:T(8,128)S(1)}, u32[]{:S(2)}) copy-start(s32[1024,1]{1,0:T(8,128)S(1)} %copy.25.seg_col) | copy-start | bytes 12292
  76.0 1.7 copy-start.18
  78.8 1.6 slice-start.1
  78.8 2.2 slice-start
  80.9 135.6 %copy-start.3 = (bf16[8,2,32,1024]{3,2,1,0:T(8,128)(2,1)}, bf16[8,2,32,1024]{3,2,1,0:T(8,128)(2,1)S(1)}, u32[]{:S(2)}) copy-start(bf16[8,2,32,1024]{3,2,1,0:T(8,128)(2,1)S(1)} %multiply_convert_fusion) | copy-start | bytes 3145732
  81.1 135.5 %copy-start.21 = (bf16[2,2,32,1024]{3,2,1,0:T(8,128)(2,1)}, bf16[2,2,32,1024]{3,2,1,0:T(8,128)(2,1)S(1)}, u32[]{:S(2)}) copy-start(bf16[2,2,32,1024]{3,2,1,0:T(8,128)(2,1)S(1)} %maximum_convert_fusion) | copy-start | bytes 786436
  82.2 1.6 copy-start.4
  83.8 1.0 copy-start.6
  84.8 1.2 copy-start.9
  86.0 132.6 %copy-start.16 = (f32[2048]{0:T(1024)S(1)}, f32[2048]{0:T(1024)}, u32[]{:S(2)}) copy-start(f32[2048]{0:T(1024)} %param.22) | copy-start | bytes 24580
  216.6 2.0 copy-start.7
  218.6 52.9 %copy-start.10 = (bf16[512,1024]{1,0:T(8,128)(2,1)}, bf16[512,1024]{1,0:T(8,128)(2,1)S(1)}, u32[]{:S(2)}) copy-start(bf16[512,1024]{1,0:T(8,128)(2,1)S(1)} %get-tuple-element.38.mixed_t.mixed_ref) | copy-start | bytes 3145732
  218.6 52.9 %copy-start.15 = (f32[2,4,1024]{2,1,0:T(4,128)}, f32[2,4,1024]{2,1,0:T(4,128)S(1)}, u32[]{:S(2)}) copy-start(f32[2,4,1024]{2,1,0:T(4,128)S(1)} %get-tuple-element.49.lse_ref) | copy-start | bytes 98308
  271.5 2.0 copy-start.8
  273.5 1.3 copy-start.12
  274.8 0.7 copy-start.13
  275.5 68.5 %slice-start.2 = ((s8[8388608]{0:T(1024)(128)(4,1)}), s8[4194304]{0:T(1024)(128)(4,1)S(1)}, s32[]{:S(2)}) async-start(s8[8388608]{0:T(1024)(128)(4,1)} %bitcast.58), calls=%async_computation.2 | async-start | bytes 8388608
  314.0 14.9 %copy-start.20 = (bf16[1024,2048]{1,0:T(8,128)(2,1)S(1)}, bf16[1024,2048]{1,0:T(8,128)(2,1)}, u32[]{:S(2)}) copy-start(bf16[1024,2048]{1,0:T(8,128)(2,1)} %get-tuple-element.46.dup) | copy-start | bytes 12582916
  314.0 30.0 %slice-start.3 = ((s8[8388608]{0:T(1024)(128)(4,1)}), s8[4194304]{0:T(1024)(128)(4,1)S(1)}, s32[]{:S(2)}) async-start(s8[8388608]{0:T(1024)(128)(4,1)} %bitcast.58), calls=%async_computation.3 | async-start | bytes 8388608
  328.9 15.2 %copy-start.19 = (bf16[1024,2048]{1,0:T(8,128)(2,1)S(1)}, bf16[1024,2048]{1,0:T(8,128)(2,1)}, u32[]{:S(2)}) copy-start(bf16[1024,2048]{1,0:T(8,128)(2,1)} %get-tuple-element.44.activ) | copy-start | bytes 12582916
  798.7 4.3 copy-start.25
  801.5 4.0 copy-start.24
  831.6 11.8 %copy-start.27 = (f32[256,2048]{1,0:T(8,128)S(1)}, f32[256,2048]{1,0:T(8,128)}, u32[]{:S(2)}) copy-start(f32[256,2048]{1,0:T(8,128)} %get-tuple-element.88) | copy-start | bytes 6291460
  843.4 2.3 copy-start.26

commit v2 on v1

v2 whole, which is shorter than its diff:
```python
import functools
import math

import jax
import jax.numpy as jnp
from jax import lax
from jax.experimental import pallas as pl
from jax.experimental.pallas import tpu as pltpu
from jax.sharding import PartitionSpec as P

HEADS = 32
KV_HEADS = 8
HEAD = 64
GROUP = HEADS // KV_HEADS
SCALE = 1.0 / math.sqrt(HEAD)
TILE = 256
NEG = -1e30
MIB = 1024 * 1024

epsilon = 1e-05
rope_base = 500000.0
F32 = jnp.float32
BF16 = jnp.bfloat16


def dot(left, right, dims):
    return lax.dot_general(left, right, (dims, ((), ())), preferred_element_type=F32)


NN = ((1,), (0,))
NT = ((1,), (1,))
TN = ((0,), (0,))
TT = ((0,), (1,))


MESH = pl.DeviceIdType.MESH


def place():
    return lax.axis_index("rep"), lax.axis_index("shard")


def remote(src, dst, sends, recvs, index, rep, shard):
    return pltpu.make_async_remote_copy(
        src_ref=src,
        dst_ref=dst,
        send_sem=sends.at[index],
        recv_sem=recvs.at[index],
        device_id=(rep, shard),
        device_id_type=MESH,
    )


def greet(partners):
    barrier = pltpu.get_barrier_semaphore()
    for partner in partners:
        pl.semaphore_signal(barrier, inc=1, device_id=partner, device_id_type=MESH)
    pl.semaphore_wait(barrier, len(partners))


def plane_partners(rep, me, shards):
    return [(rep, me ^ step) for step in range(1, shards)]


class Spread:
    def __init__(self, shards, own, full, columns, sends, recvs, held=None, held_sem=None):
        rep, me = place()
        quarter = rep % 4
        count = own.shape[0]
        part = count // 4
        own_rows = pl.ds(pl.multiple_of(quarter * part, part), part)

        def at(shard, which):
            return full.at[pl.ds(pl.multiple_of(shard * count + which * part, part), part), :]

        def piece(shard):
            return own.at[own_rows, :] if columns is None else own.at[own_rows, columns(shard)]

        self.first, self.core, self.layer, self.last = [], [], [], []
        n = shards - 1
        for i in range(n):
            peer = me ^ (i + 1)
            self.first.append(remote(piece(peer), at(me, quarter), sends, recvs, i, rep, peer))
            mine = at(peer, quarter)
            self.core.append(remote(mine, mine, sends, recvs, n + i, rep ^ 1, me))
            self.layer.append(remote(mine, mine, sends, recvs, 2 * n + i, rep ^ 2, me))
            theirs = at(peer, quarter ^ 2)
            self.last.append(remote(theirs, theirs, sends, recvs, 3 * n + i, rep ^ 1, me))
        self.take = self.keep = None
        if held is not None:
            kept = full.at[pl.ds(pl.multiple_of(me * count, count), count), :]
            self.take = pltpu.make_async_copy(own.at[:, columns(me)], held, held_sem.at[0])
            self.keep = pltpu.make_async_copy(held, kept, held_sem.at[1])

    def start(self):
        for copy in self.first:
            copy.start()
        if self.take is not None:
            self.take.start()

    def hand_on(self):
        if self.take is not None:
            self.take.wait()
            self.keep.start()
        for i, copy in enumerate(self.first):
            copy.wait_recv()
            self.layer[i].start()
            self.core[i].start()

    def hand_on_last(self):
        for i, copy in enumerate(self.layer):
            copy.wait_recv()
            self.last[i].start()

    def finish(self):
        for copy in self.core + self.last:
            copy.wait_recv()
        for copy in self.first + self.core + self.layer + self.last:
            copy.wait_send()
        if self.keep is not None:
            self.keep.wait()

    @staticmethod
    def semaphores(shards):
        n = 4 * (shards - 1)
        return [pltpu.SemaphoreType.DMA((n,)), pltpu.SemaphoreType.DMA((n,))]


class Gather:
    def __init__(self, shards, own, full, sends, recvs, local_sem=None):
        rep, me = place()
        count = own.shape[0]
        half = count // 2

        def at(shard, start, size):
            return full.at[pl.ds(pl.multiple_of(shard * count + start, half), size), :]

        self.direct, self.passed, self.kept = [], [], None
        if shards == 4:
            for i, (step, start) in enumerate(((1, 0), (2, half), (1, half), (2, 0))):
                self.direct.append(
                    remote(
                        own.at[pl.ds(start, half), :], at(me, start, half),
                        sends, recvs, i, rep, me ^ step,
                    )
                )
            for i, (step, start) in enumerate(((1, 0), (2, half))):
                came = at(me ^ step, start, half)
                self.passed.append(remote(came, came, sends, recvs, 4 + i, rep, me ^ step ^ 3))
        else:
            for i in range(shards - 1):
                self.direct.append(
                    remote(own, at(me, 0, count), sends, recvs, i, rep, me ^ (i + 1))
                )
        if local_sem is not None:
            self.kept = pltpu.make_async_copy(own, at(me, 0, count), local_sem)

    def start(self):
        for copy in self.direct:
            copy.start()
        if self.kept is not None:
            self.kept.start()

    def hand_on(self):
        for i, copy in enumerate(self.passed):
            self.direct[i].wait_recv()
            copy.start()

    def finish(self):
        for copy in self.direct[len(self.passed) :] + self.passed:
            copy.wait_recv()
        for copy in self.direct + self.passed:
            copy.wait_send()
        if self.kept is not None:
            self.kept.wait()

    @staticmethod
    def semaphores(shards):
        n = max(6, shards - 1)
        return [
            pltpu.SemaphoreType.DMA((n,)),
            pltpu.SemaphoreType.DMA((n,)),
            pltpu.SemaphoreType.DMA,
        ]


def split_rows(ref, index, size):
    return ref.at[pl.ds(pl.multiple_of(index * size, size), size), :]


def column_block(part):
    return lambda shard: pl.ds(pl.multiple_of(shard * part, part), part)


def pair_partners(rep, me):
    return [(rep ^ 1, me), (rep ^ 2, me)]


ANY = pl.BlockSpec(memory_space=pl.ANY)
IN_VMEM = pl.BlockSpec(memory_space=pltpu.VMEM)


def first_kernel(shards, parts, tokens, seg, *refs):
    rep, me = place()
    count = len(parts)
    weights, (tokens_all, seg_all, qkv_m, tokens_v) = refs[:count], refs[count : count + 4]
    held, held_sem, sems = refs[count + 4 : 2 * count + 4], refs[2 * count + 4], refs[2 * count + 5 :]
    take = pltpu.make_async_copy(tokens, tokens_v, held_sem.at[count, 0])
    take.start()
    greet(plane_partners(rep, me, shards) + pair_partners(rep, me))
    at, spreads = 0, []
    for weight, part, i in zip(weights, parts, range(count)):
        full = qkv_m.at[:, pl.ds(at, part)]
        spreads.append(
            Spread(
                shards, weight, full, column_block(part), *sems[2 * i : 2 * i + 2],
                held[i], held_sem.at[i],
            )
        )
        at += part
    sems = sems[2 * count :]
    rows = Gather(shards, tokens_v, tokens_all, *sems[:3])
    seg_send, seg_recv, seg_local = sems[3:]
    segs = [
        remote(seg, seg_all.at[me], seg_send, seg_recv, i, rep, me ^ (i + 1))
        for i in range(shards - 1)
    ]
    for spread in spreads:
        spread.start()
    for copy in segs:
        copy.start()
    take.wait()
    rows.start()
    own_seg = pltpu.make_async_copy(seg, seg_all.at[me], seg_local)
    own_seg.start()
    for spread in spreads:
        spread.hand_on()
    rows.hand_on()
    for spread in spreads:
        spread.hand_on_last()
    for spread in spreads:
        spread.finish()
    rows.finish()
    for copy in segs:
        copy.wait()
    own_seg.wait()


def first(tokens, seg, weights, shards):
    rows, width = tokens.shape
    parts = [w.shape[1] // shards for w in weights]
    n = shards - 1
    return pl.pallas_call(
        functools.partial(first_kernel, shards, parts),
        in_specs=[ANY] * (2 + len(weights)),
        out_specs=[ANY] * 3,
        out_shape=[
            jax.ShapeDtypeStruct((shards * rows, width), tokens.dtype),
            jax.ShapeDtypeStruct((shards,) + seg.shape, seg.dtype),
            jax.ShapeDtypeStruct((width, sum(parts)), BF16),
        ],
        scratch_shapes=[pltpu.VMEM(tokens.shape, BF16)]
        + [pltpu.VMEM((w.shape[0], part), BF16) for w, part in zip(weights, parts)]
        + [pltpu.SemaphoreType.DMA((len(weights) + 1, 2))]
        + len(weights) * Spread.semaphores(shards)
        + Gather.semaphores(shards)
        + [pltpu.SemaphoreType.DMA((n,)), pltpu.SemaphoreType.DMA((n,)), pltpu.SemaphoreType.DMA],
        compiler_params=pltpu.CompilerParams(
            collective_id=0, has_side_effects=True, vmem_limit_bytes=40 * MIB
        ),
        name="first",
    )(tokens, seg, *weights)


def doc_positions(seg_ids):
    index = jnp.arange(seg_ids.shape[0], dtype=jnp.int32)
    fresh = (index == 0) | (seg_ids != jnp.roll(seg_ids, 1))
    begins = lax.cummax(jnp.where(fresh, index, jnp.zeros_like(index)), axis=0)
    return index - begins


def rope_tables(positions):
    freqs = rope_base ** (-(jnp.arange(HEAD // 2, dtype=F32) * (2.0 / HEAD)))
    angles = freqs[:, None] * positions.astype(F32)[None, :]
    return (jnp.cos(angles), jnp.sin(angles))


def side_by_side(ref, group, here):
    rows = GROUP * HEAD
    return jnp.concatenate(
        [
            ref[pl.ds(pl.multiple_of(group * rows + h * HEAD, HEAD), HEAD), here]
            for h in range(GROUP)
        ],
        axis=1,
    )


def block_bias(seg_col_ref, seg_row_ref, key_at, query_at):
    same = seg_col_ref[pl.ds(key_at, TILE), :] == seg_row_ref[:, pl.ds(query_at, TILE)]
    key_index = key_at + lax.broadcasted_iota(jnp.int32, (TILE, TILE), 0)
    query_index = query_at + lax.broadcasted_iota(jnp.int32, (TILE, TILE), 1)
    bias = jnp.where(same & (key_index <= query_index), 0.0, NEG).astype(F32)
    return jnp.concatenate([bias] * GROUP, axis=1)


def attend_kernel(
    shards, ffn_part, early, tokens, qkv_m, cot, proj_w, gate_w, up_w, gain, seg_col, seg_row,
    cos_ref, sin_ref,
    normed_out, cot_all, proj_m, gate_m, up_m, q_ref, k_ref, kt_ref, v_ref, out_ref, lse_ref,
    tokens_v, normed_v, qkv_v, turned_v, vt_ref, cot_v, load_sem, store_sem, qkv_sem, *sems,
):
    rep, me = place()
    length, width = tokens.shape
    kv_heads = k_ref.shape[0]
    q_part, kv_part = q_ref.shape[0], kt_ref.shape[0]
    blocks = length // TILE

    def first_tiles(shard):
        return pl.ds(pl.multiple_of(shard * ffn_part, ffn_part), early)

    proj = Spread(shards, proj_w, proj_m, None, *sems[:2])
    gate = Spread(shards, gate_w, gate_m, first_tiles, *sems[2:4])
    up = Spread(shards, up_w, up_m, first_tiles, *sems[4:6])
    cots = Gather(shards, cot_v, cot_all, *sems[6:9])

    def block_rows(i):
        return pl.ds(pl.multiple_of(i * TILE, TILE), TILE)

    def load(i):
        return pltpu.make_async_copy(tokens.at[block_rows(i), :], tokens_v.at[i % 2], load_sem.at[i % 2])

    def store(i):
        return pltpu.make_async_copy(
            normed_v.at[i % 2], normed_out.at[block_rows(i), :], store_sem.at[i % 2]
        )

    weights = pltpu.make_async_copy(qkv_m, qkv_v, qkv_sem.at[0])
    take = pltpu.make_async_copy(cot, cot_v, qkv_sem.at[1])
    take.start()
    weights.start()
    load(0).start()
    greet(plane_partners(rep, me, shards) + pair_partners(rep, me))
    proj.start()
    gate.start()
    up.start()
    take.wait()
    cots.start()
    weights.wait()

    def turn_weights(i, carry):
        turned_v[:, block_rows(i)] = qkv_v[block_rows(i), :].T
        return carry

    lax.fori_loop(0, width // TILE, turn_weights, 0)

    half = HEAD // 2

    def project(i, carry):
        here = block_rows(i)

        @pl.when(i + 1 < blocks)
        def _():
            load(i + 1).start()

        load(i).wait()

        @pl.when(i >= 2)
        def _():
            store(i - 2).wait()

        values = tokens_v[i % 2].astype(F32)
        rms = lax.rsqrt(jnp.mean(values * values, axis=-1, keepdims=True) + epsilon)
        normed_v[i % 2] = (values * rms * gain[...]).astype(BF16)
        store(i).start()
        heads = dot(turned_v[...], normed_v[i % 2], NT)
        cos, sin = cos_ref[:, here], sin_ref[:, here]

        def turned(at):
            first, second = heads[at : at + half], heads[at + half : at + HEAD]
            return (
                (first * cos - second * sin).astype(BF16),
                (second * cos + first * sin).astype(BF16),
            )

        for at in range(0, q_part, HEAD):
            first, second = turned(at)
            q_ref[at : at + half, here] = (first.astype(F32) * SCALE).astype(BF16)
            q_ref[at + half : at + HEAD, here] = (second.astype(F32) * SCALE).astype(BF16)
        for g in range(kv_heads):
            at = g * HEAD
            first, second = turned(q_part + at)
            kt_ref[at : at + half, here] = first
            kt_ref[at + half : at + HEAD, here] = second
            vt_ref[at : at + HEAD, here] = heads[
                q_part + kv_part + at : q_part + kv_part + at + HEAD
            ].astype(BF16)
            k_ref[g, here, :] = kt_ref[at : at + HEAD, here].T
            v_ref[g, here, :] = vt_ref[at : at + HEAD, here].T
        return carry

    lax.fori_loop(0, blocks, project, 0)
    for i in range(max(0, blocks - 2), blocks):
        store(i).wait()
    proj.hand_on()
    gate.hand_on()
    wide = GROUP * TILE

    def unit(at, carry_out):
        g, block = at // blocks, at % blocks
        query_at = pl.multiple_of(block * TILE, TILE)
        here = pl.ds(query_at, TILE)
        queries = side_by_side(q_ref, g, here)
        value_rows = pl.ds(pl.multiple_of(g * HEAD, HEAD), HEAD)

        def step(c, carry):
            top, total, acc = carry
            key_at = pl.multiple_of(c * TILE, TILE)
            keys = pl.ds(key_at, TILE)
            scores = dot(k_ref[g, keys, :], queries, NN)
            scores = scores + block_bias(seg_col, seg_row, key_at, query_at)
            new_top = jnp.maximum(top, jnp.max(scores, axis=0, keepdims=True))
            expo = jnp.exp(scores - new_top)
            fade = jnp.exp(top - new_top)
            total = total * fade + jnp.sum(expo, axis=0, keepdims=True)
            acc = acc * fade + dot(vt_ref[value_rows, keys], expo.astype(BF16), NN)
            return new_top, total, acc

        start = (
            jnp.full((1, wide), NEG, F32),
            jnp.zeros((1, wide), F32),
            jnp.zeros((HEAD, wide), F32),
        )
        top, total, acc = lax.fori_loop(0, block, step, step(block, start))
        mixed = (acc / total).astype(BF16)
        lse = top + jnp.log(total)
        for h in range(GROUP):
            at_row = pl.multiple_of(g * GROUP * HEAD + h * HEAD, HEAD)
            out_ref[pl.ds(at_row, HEAD), here] = mixed[:, h * TILE : (h + 1) * TILE]
            lse_ref[g, h : h + 1, here] = lse[:, h * TILE : (h + 1) * TILE]
        return carry_out

    units = kv_heads * blocks
    lax.fori_loop(0, units // 2, unit, 0)
    up.hand_on()
    proj.hand_on_last()
    gate.hand_on_last()
    lax.fori_loop(units // 2, units, unit, 0)
    up.hand_on_last()
    cots.hand_on()
    for transfer in (proj, gate, up, cots):
        transfer.finish()


def attend(
    tokens_all, qkv_m, cot, proj_w, gate_w, up_w, gain, seg, cos_t, sin_t, q_part, kv_part,
    early, shards,
):
    length, width = tokens_all.shape
    kv_heads = kv_part // HEAD
    part = gate_w.shape[1] // shards
    shape = jax.ShapeDtypeStruct
    dma = pltpu.SemaphoreType.DMA
    return pl.pallas_call(
        functools.partial(attend_kernel, shards, part, early),
        in_specs=[ANY] * 6 + [IN_VMEM] * 5,
        out_specs=[ANY] * 5 + [IN_VMEM] * 6,
        out_shape=[
            shape((length, width), BF16),
            shape((length, width), BF16),
            shape((shards * proj_w.shape[0], width), BF16),
            shape((width, early), BF16),
            shape((width, early), BF16),
            shape((q_part, length), BF16),
            shape((kv_heads, length, HEAD), BF16),
            shape((kv_part, length), BF16),
            shape((kv_heads, length, HEAD), BF16),
            shape((q_part, length), BF16),
            shape((kv_heads, GROUP, length), F32),
        ],
        scratch_shapes=[
            pltpu.VMEM((2, TILE, width), BF16),
            pltpu.VMEM((2, TILE, width), BF16),
            pltpu.VMEM(qkv_m.shape, BF16),
            pltpu.VMEM(qkv_m.shape[::-1], BF16),
            pltpu.VMEM((kv_part, length), BF16),
            pltpu.VMEM(cot.shape, BF16),
            dma((2,)), dma((2,)), dma((2,)),
        ]
        + 3 * Spread.semaphores(shards)
        + Gather.semaphores(shards),
        compiler_params=pltpu.CompilerParams(
            collective_id=1, has_side_effects=True, vmem_limit_bytes=48 * MIB
        ),
        name="attend",
    )(
        tokens_all, qkv_m, cot, proj_w, gate_w, up_w, gain[None, :], seg[:, None], seg[None, :],
        cos_t, sin_t,
    )


def hidden_kernel(
    shards, mixed_t, proj_m, proj_w, tokens, gain, hidden_ref, rms_ref, normed_all,
    proj_v, mixed_own, normed, proj_sem, mix_send, mix_recv, gather_send, gather_recv, local_sem,
):
    rep, me = place()
    part, _ = mixed_t.shape
    count = tokens.shape[0]
    rows = [
        pltpu.make_async_copy(
            split_rows(proj_m, me ^ i, part) if i else proj_w,
            split_rows(proj_v, me ^ i, part),
            proj_sem.at[i],
        )
        for i in range(shards)
    ]
    for copy in rows:
        copy.start()
    greet(plane_partners(rep, me, shards))

    def columns(shard):
        return mixed_t.at[:, pl.ds(pl.multiple_of(shard * count, count), count)]

    copies = [
        remote(columns(me ^ (i + 1)), mixed_own.at[i], mix_send, mix_recv, i, rep, me ^ (i + 1))
        for i in range(shards - 1)
    ]
    for copy in copies:
        copy.start()

    def product(block, i):
        rows[i].wait()
        return dot(block, split_rows(proj_v, me ^ i, part)[...], TN)

    hidden_ref[...] = tokens[...].astype(F32) + product(
        mixed_t[:, pl.ds(pl.multiple_of(me * count, count), count)], 0
    )
    for i, copy in enumerate(copies):
        copy.wait_recv()
        hidden_ref[...] += product(mixed_own[i], i + 1)
    hidden = hidden_ref[...]
    rms = lax.rsqrt(jnp.mean(hidden * hidden, axis=-1, keepdims=True) + epsilon)
    rms_ref[...] = rms
    normed[...] = (hidden * rms * gain[...]).astype(BF16)
    gather = Gather(shards, normed, normed_all, gather_send, gather_recv, local_sem)
    gather.start()
    for copy in copies:
        copy.wait_send()
    gather.hand_on()
    gather.finish()


def hidden_layer(mixed_t, proj_m, proj_w, tokens, gain, shards):
    part, length = mixed_t.shape
    count, width = tokens.shape
    n = shards - 1
    return pl.pallas_call(
        functools.partial(hidden_kernel, shards),
        in_specs=[IN_VMEM, ANY, ANY, IN_VMEM, IN_VMEM],
        out_specs=[IN_VMEM, IN_VMEM, ANY],
        out_shape=[
            jax.ShapeDtypeStruct((count, width), F32),
            jax.ShapeDtypeStruct((count, 1), F32),
            jax.ShapeDtypeStruct((length, width), BF16),
        ],
        scratch_shapes=[
            pltpu.VMEM(proj_m.shape, BF16),
            pltpu.VMEM((n, part, count), BF16),
            pltpu.VMEM((count, width), BF16),
            pltpu.SemaphoreType.DMA((shards,)),
            pltpu.SemaphoreType.DMA((n,)),
            pltpu.SemaphoreType.DMA((n,)),
        ]
        + Gather.semaphores(shards),
        compiler_params=pltpu.CompilerParams(
            collective_id=2, has_side_effects=True, vmem_limit_bytes=40 * MIB
        ),
        name="hidden",
    )(mixed_t, proj_m, proj_w, tokens, gain[None, :])


class Plan:
    def __init__(self, shards, reps, length, width, ffn_part, q_part, kv_part):
        self.shards, self.reps, self.length, self.width = shards, reps, length, width
        self.ffn_part, self.q_part, self.kv_part = ffn_part, q_part, kv_part
        self.layers = reps // 2
        self.half = self.layers // 2
        self.rows = width // 2
        self.own = width // shards
        self.block = self.own // 2
        self.proj_half = q_part // 2
        self.proj_blocks = self.rows // self.proj_half
        self.tiles = ffn_part // TILE
        self.out_tiles = width // TILE
        per_slot = 4
        self.back_slot = self.tiles
        self.send_slot = self.back_slot + self.out_tiles // per_slot - 1
        self.rows_slot = self.send_slot + 4
        self.pass_slot = self.rows_slot + 2
        self.mixed_slot = self.rows_slot + 4
        self.unit_slot = self.mixed_slot + 1
        self.per_slot = per_slot
        self.units = (length // TILE) * (kv_part // HEAD)
        self.norm_slot = self.unit_slot + self.units // 2
        self.tokens_slot = self.norm_slot + 5
        self.gain_slot = self.tokens_slot + 1
        self.rep_slot = self.gain_slot + 1
        proj = width // TILE // self.proj_blocks
        self.ffn_end = 3 * self.tiles
        self.proj_at = max(self.ffn_end, self.norm_slot)
        self.q_at = max(self.proj_at + proj, self.norm_slot + 1)
        assert self.q_at == self.proj_at + proj
        self.kv_at = self.q_at + q_part // TILE
        self.chunks = self.kv_at + 1
        self.res_slot = max(self.ffn_end + 1, self.norm_slot + 1)
        self.result_slot = self.res_slot + self.out_tiles // 2 + 3
        lag = 3 if self.layers <= 4 else 1
        self.lag = lag
        self.meet = 1 + lag * self.half
        self.spread = 1 + lag * (self.layers - 1)
        self.hand = self.spread + lag
        self.slots = max(self.chunks + self.hand, self.rep_slot, self.result_slot) + 1
        self.mine_ring = 2 + lag * (self.half - 1)
        self.sum_ring = lag + 2


def backward_kernel(
    plan, early, x, cot_all, gate_w, up_w, gate_e, up_e, down_w, hidden, tokens, proj_w, qkv_m,
    normed,
    mlp_rms, mlp_gain, attn_gain, seg_col, seg_row, cos_ref, sin_ref, lse_ref, q_ref, mixed_ref,
    k_ref, kt_ref, v_ref,
    f_down, f_gate, f_up, f_proj, f_q, f_kv, result_ref, tokens_out, gains_out,
    swapped, from_outer, from_middle, totals, back_land, res_land, norm_land, norm_part,
    gate_m, up_m, activ, dgate, dup, back_part, res_part,
    left_a, left_b, right, gate_v, up_v, down_v, back_v, tile_v, both, proj_v, qkv_v, hidden_v,
    row_sum, land_v,
    mine, theirs, swap_v, outer_v, middle_v, sums, total_v,
    grad_hidden, gh_own, g_t, back_t, dk_acc, dv_acc,
    gain_part, gain_land, gain_sum, gain_reps,
    load_sem, right_sem, small_sem, swap_send, swap_recv, in_send, outer_recv, middle_recv,
    out_send, total_recv, total_store, cross_recv, cross_send, pass_send, pass_recv,
    back_send, back_recv, res_send, res_recv, norm_send, norm_recv,
    gather_send, gather_recv, gather_local, gain_send, gain_recv, rep_send, rep_recv,
    tile_send, tile_recv, tile_pass, tile_passed, down_sem, back_sem, tile_sem,
):
    p = plan
    shards, reps, n = p.shards, p.reps, p.shards - 1
    rep, me = place()
    core, layer = rep % 2, rep // 2
    upper = layer >= p.half
    depth = jnp.where(upper, p.layers - 1 - layer, layer)
    inward = jnp.where(upper, rep - 2, rep + 2)
    outward = jnp.where(upper, rep + 2, rep - 2)
    is_middle = depth == p.half - 1
    count = tokens.shape[0]
    ffn_end, proj_at, q_at, kv_at, end_at = p.ffn_end, p.proj_at, p.q_at, p.kv_at, p.chunks
    gh_all = both.at[:, pl.ds(0, p.width)]

    def columns(index, size=TILE):
        return pl.ds(pl.multiple_of(index * size, size), size)

    def load(src, dst, i):
        return pltpu.make_async_copy(src, dst, load_sem.at[i])

    load_cot = load(cot_all, left_a, 0)
    load_x = load(x, left_b, 1)
    load_normed = load(normed, left_a, 2)
    load_proj = load(proj_w, proj_v, 3)
    load_qkv = load(qkv_m, qkv_v, 4)
    load_hidden = load(hidden, hidden_v, 5)
    load_activ = load(activ, left_b.at[:, pl.ds(0, p.ffn_part)], 6)
    load_tokens = load(tokens, gh_own, 7)
    first_tile = early // TILE

    def tile_bytes(tile, sem):
        piece = gate_m.at[pl.ds(0, 2 * n * p.block), pl.ds(0, TILE)]
        return pltpu.make_async_copy(piece, piece, sem.at[tile])

    def send_tile(tile):
        rows = columns(core, p.block)
        into = pl.ds(pl.multiple_of(me * p.own + core * p.block, p.block), p.block)
        for weight, full in ((gate_w, gate_m), (up_w, up_m)):
            for i in range(n):
                peer = me ^ (i + 1)
                at = pl.ds(pl.multiple_of(peer * p.ffn_part + tile * TILE, TILE), TILE)
                pltpu.make_async_remote_copy(
                    src_ref=weight.at[rows, at], dst_ref=full.at[into, columns(tile)],
                    send_sem=tile_send.at[tile], recv_sem=tile_recv.at[tile],
                    device_id=(rep, peer), device_id_type=MESH,
                ).start()

    def pass_tile(tile):
        tile_bytes(tile, tile_recv).wait()
        for full in (gate_m, up_m):
            for i in range(n):
                peer = me ^ (i + 1)
                at = pl.ds(pl.multiple_of(peer * p.own + core * p.block, p.block), p.block)
                piece = full.at[at, columns(tile)]
                pltpu.make_async_remote_copy(
                    src_ref=piece, dst_ref=piece,
                    send_sem=tile_pass.at[tile], recv_sem=tile_passed.at[tile],
                    device_id=(rep ^ 1, me), device_id_type=MESH,
                ).start()

    def load_down(tile):
        return pltpu.make_async_copy(down_w.at[columns(tile), :], down_v, down_sem.at[0])

    def load_tile(tile):
        @pl.when(tile >= first_tile)
        def _():
            tile_bytes(tile, tile_passed).wait()

        own_at = pl.ds(pl.multiple_of(me * p.ffn_part + tile * TILE, TILE), TILE)
        held_rows = [pl.ds(pl.multiple_of((me ^ i) * p.own, p.own), p.own) for i in range(shards)]
        for i, (weight, tiles, full, held) in enumerate(
            ((gate_w, gate_e, gate_m, gate_v), (up_w, up_e, up_m, up_v))
        ):
            sem = down_sem.at[i + 1]
            pltpu.make_async_copy(weight.at[:, own_at], held.at[held_rows[0], :], sem).start()
            for rows in held_rows[1:]:

                @pl.when(tile < first_tile)
                def _(rows=rows, tiles=tiles, held=held, sem=sem):
                    src = tiles.at[rows, columns(tile)]
                    pltpu.make_async_copy(src, held.at[rows, :], sem).start()

                @pl.when(tile >= first_tile)
                def _(rows=rows, full=full, held=held, sem=sem):
                    src = full.at[rows, columns(tile)]
                    pltpu.make_async_copy(src, held.at[rows, :], sem).start()

        load_down(tile).start()

    def store_tile(tile):
        dup_columns = pl.ds(pl.multiple_of(p.ffn_part + tile * TILE, TILE), TILE)
        return [
            pltpu.make_async_copy(src, dst.at[:, columns(tile)], tile_sem.at[i])
            for i, (src, dst) in enumerate(
                (
                    (tile_v.at[tile % 2], activ),
                    (both.at[:, columns(tile)], dgate),
                    (both.at[:, dup_columns], dup),
                )
            )
        ]

    def stored(tile):
        for copy in store_tile(tile):
            copy.wait()

    def ffn_tile(tile):
        for i, held in enumerate((gate_v, up_v)):
            pltpu.make_async_copy(held, held, down_sem.at[i + 1]).wait()
        load_down(tile).wait()
        dup_columns = pl.ds(pl.multiple_of(p.ffn_part + tile * TILE, TILE), TILE)

        def go(i, carry):
            here = columns(i)
            rows = left_b[here, :]
            gate = dot(rows, gate_v[...], NN)
            up = dot(rows, up_v[...], NN)
            grad_activ = dot(left_a[here, :], down_v[...], NT)
            sigm = jax.nn.sigmoid(gate)
            swish = gate * sigm
            tile_v[tile % 2, here, :] = (swish * up).astype(BF16)
            both[here, columns(tile)] = (
                grad_activ * up * sigm * (1.0 + gate * (1.0 - sigm))
            ).astype(BF16)
            both[here, dup_columns] = (grad_activ * swish).astype(BF16)
            return carry

        lax.fori_loop(0, p.length // TILE, go, 0)

        @pl.when(tile >= 2)
        def _():
            stored(tile - 1)

        for copy in store_tile(tile):
            copy.start()

        @pl.when(tile == 0)
        def _():
            stored(0)

        @pl.when(tile + 1 < p.tiles)
        def _():
            load_tile(tile + 1)

    def load_back(tile):
        slot = tile % 2
        per_shard = p.own // TILE
        for i, (weight, tiles, full) in enumerate(
            ((gate_w, gate_e, gate_m), (up_w, up_e, up_m))
        ):
            sem, at = back_sem.at[slot, i], i * p.ffn_part

            @pl.when(tile // per_shard == me)
            def _(weight=weight, sem=sem, at=at):
                src = weight.at[columns(tile - me * per_shard), columns(me, p.ffn_part)]
                pltpu.make_async_copy(src, back_v.at[slot, :, pl.ds(at, p.ffn_part)], sem).start()

            @pl.when(tile // per_shard != me)
            def _(tiles=tiles, full=full, sem=sem, at=at):
                into = back_v.at[slot, :, pl.ds(at, early)]
                pltpu.make_async_copy(tiles.at[columns(tile), :], into, sem).start()
                rest = p.ffn_part - early
                into = back_v.at[slot, :, pl.ds(at + early, rest)]
                src = full.at[columns(tile), pl.ds(early, rest)]
                pltpu.make_async_copy(src, into, sem).start()

    def wait_back(tile):
        slot = tile % 2
        for i in range(2):
            half = back_v.at[slot, :, pl.ds(i * p.ffn_part, p.ffn_part)]
            pltpu.make_async_copy(half, half, back_sem.at[slot, i]).wait()

    def back_tiles(first):
        def store(tile):
            return pltpu.make_async_copy(
                tile_v.at[tile % 2], back_part.at[:, columns(tile)], tile_sem.at[tile % 2]
            )

        @pl.when(first == 0)
        def _():
            stored(p.tiles - 1)
            load_back(0)

        def tile_go(k, carry):
            tile = first + k
            wait_back(tile)

            @pl.when(tile + 1 < p.out_tiles)
            def _():
                load_back(tile + 1)

            @pl.when(k >= 2)
            def _():
                store(tile - 2).wait()

            def go(i, c):
                here = columns(i)
                tile_v[tile % 2, here, :] = dot(both[here, :], back_v[tile % 2], NT).astype(BF16)
                return c

            lax.fori_loop(0, p.length // TILE, go, 0)
            store(tile).start()
            return carry

        lax.fori_loop(0, p.per_slot, tile_go, 0)
        for k in range(max(0, p.per_slot - 2), p.per_slot):
            store(first + k).wait()

    def load_res(tile):
        def copies(action):
            for i, held in enumerate((gate_v, up_v)):

                @pl.when(tile % 2 == i)
                def _(i=i, held=held):
                    action(
                        pltpu.make_async_copy(
                            down_w.at[:, columns(tile)], held.at[pl.ds(0, p.ffn_part), :], back_sem.at[i, 0]
                        )
                    )

        return copies

    def res_tiles(first):
        def store(tile):
            return pltpu.make_async_copy(
                tile_v.at[tile % 2], res_part.at[:, columns(tile)], tile_sem.at[tile % 2]
            )

        for k, held in enumerate((gate_v, up_v)):
            tile = first + k
            load_res(tile)(lambda copy: copy.wait())

            @pl.when(tile + 1 < p.out_tiles)
            def _(tile=tile):
                load_res(tile + 1)(lambda copy: copy.start())

            def go(i, c, k=k, held=held):
                here = columns(i)
                tile_v[k, here, :] = dot(
                    left_b[here, : p.ffn_part], held[: p.ffn_part, :], NN
                ).astype(BF16)
                return c

            lax.fori_loop(0, p.length // TILE, go, 0)
            store(tile).start()
        store(first).wait()
        store(first + 1).wait()

    def load_right(t):
        slot = right.at[t % 2]
        tile, kind = t // 3, t % 3

        def copies(action):
            for i, ref in enumerate((activ, dgate, dup)):

                @pl.when((t < ffn_end) & (kind == i))
                def _(ref=ref):
                    action(
                        pltpu.make_async_copy(
                            ref.at[:, columns(tile)], slot, right_sem.at[t % 2]
                        )
                    )

        return copies

    def scatter(part, land, sends, recvs):
        return [
            remote(split_rows(part, me ^ (i + 1), count), land.at[i], sends, recvs, i, rep, me ^ (i + 1))
            for i in range(n)
        ]

    back_rows = scatter(back_part, back_land, back_send, back_recv)
    res_rows = scatter(res_part, res_land, res_send, res_recv)
    norm_rows = scatter(norm_part, norm_land, norm_send, norm_recv)

    def fetch_rows(copies, part, land):
        for copy in copies:
            copy.wait_recv()
        pieces = [split_rows(part, me, count)] + [land.at[i] for i in range(n)]
        loads = [
            pltpu.make_async_copy(piece, land_v.at[i % 2], small_sem.at[i % 2])
            for i, piece in enumerate(pieces)
        ]
        loads[0].start()
        for i, piece in enumerate(loads):
            if i + 1 < len(loads):
                loads[i + 1].start()
            piece.wait()

            def strip(here, i=i):
                value = land_v[i % 2, here, :].astype(F32)
                row_sum[here, :] = value if i == 0 else row_sum[here, :] + value

            strips(strip)

    STRIP = 32

    def strips(body):
        def go(i, carry):
            body(pl.ds(pl.multiple_of(i * STRIP, STRIP), STRIP))
            return carry

        lax.fori_loop(0, count // STRIP, go, 0)

    def norm_strip(here, values, rms, gain, row):
        grad_in = row_sum[here, :]
        weighted = grad_in * gain
        inner = jnp.mean(weighted * values, axis=-1, keepdims=True)
        gain_part[row : row + 1, :] += jnp.sum(grad_in * values * rms, axis=0, keepdims=True)
        return rms * weighted - values * (rms * rms * rms) * inner

    gather = Gather(shards, gh_own, gh_all, gather_send, gather_recv, gather_local)

    def hidden_back():
        load_hidden.wait()
        fetch_rows(back_rows, back_part, back_land)
        gain_part[...] = jnp.zeros_like(gain_part)

        def strip(here):
            own = pl.ds(pl.multiple_of(me * count, count) + here.start, STRIP)
            grad = left_a[own, :].astype(F32) + norm_strip(
                here, hidden_v[here, :], mlp_rms[here, :], mlp_gain[...], 1
            )
            grad_hidden[here, :] = grad
            gh_own[here, :] = grad.astype(BF16)

        strips(strip)
        gather.start()

    def finish_result():
        fetch_rows(res_rows, res_part, res_land)

        def strip(here):
            row_sum[here, :] = hidden_v[here, :] + row_sum[here, :]

        strips(strip)
        store_result = pltpu.make_async_copy(row_sum, result_ref, small_sem.at[0])
        store_result.start()
        store_result.wait()

    def mixed_back():
        gather.finish()
        load_proj.wait()

        def go(i, carry):
            here = pl.ds(pl.multiple_of(i * TILE, TILE), TILE)
            g_t[:, here] = dot(proj_v[...], both[here, : p.width], NT).astype(BF16)
            return carry

        lax.fori_loop(0, p.length // TILE, go, 0)

    blocks = p.length // TILE
    rows = GROUP * HEAD
    wide = GROUP * TILE
    mid = HEAD // 2

    def attention_unit(unit):
        g, block = unit // blocks, unit % blocks
        query_at = pl.multiple_of(block * TILE, TILE)
        here_q = pl.ds(query_at, TILE)

        queries = side_by_side(q_ref, g, here_q)
        grads = side_by_side(g_t, g, here_q)
        mixed = side_by_side(mixed_ref, g, here_q)
        lse = jnp.concatenate([lse_ref[g, h : h + 1, here_q] for h in range(GROUP)], axis=1)
        inner = jnp.sum(grads.astype(F32) * mixed.astype(F32), axis=0, keepdims=True)

        @pl.when(block == 0)
        def _():
            dk_acc[...] = jnp.zeros_like(dk_acc)
            dv_acc[...] = jnp.zeros_like(dv_acc)

        def step(c, acc):
            key_at = pl.multiple_of(c * TILE, TILE)
            here = pl.ds(key_at, TILE)
            scores = dot(k_ref[g, here, :], queries, NN)
            scores = scores + block_bias(seg_col, seg_row, key_at, query_at)
            probs = jnp.exp(scores - lse)
            grad_probs = dot(v_ref[g, here, :], grads, NN)
            grad_scores = (probs * (grad_probs - inner)).astype(BF16)
            dv_acc[:, here] += dot(grads, probs.astype(BF16), NT)
            dk_acc[:, here] += dot(queries, grad_scores, NT)
            key_rows = pl.ds(pl.multiple_of(g * HEAD, HEAD), HEAD)
            return acc + dot(kt_ref[key_rows, here], grad_scores, NN)

        acc = lax.fori_loop(0, block + 1, step, jnp.zeros((HEAD, wide), F32))
        cos, sin = cos_ref[:, here_q], sin_ref[:, here_q]
        for h in range(GROUP):
            grad = acc[:, h * TILE : (h + 1) * TILE] * SCALE
            first, second = grad[:mid], grad[mid:]
            at = pl.multiple_of(g * rows + h * HEAD, HEAD)
            back_t[pl.ds(at, mid), here_q] = (first * cos + second * sin).astype(BF16)
            back_t[pl.ds(at + mid, mid), here_q] = (second * cos - first * sin).astype(BF16)

        @pl.when(block == blocks - 1)
        def _():
            cos, sin = cos_ref[...], sin_ref[...]
            first, second = dk_acc[:mid, :], dk_acc[mid:, :]
            at = pl.multiple_of(p.q_part + g * HEAD, HEAD)
            back_t[pl.ds(at, mid), :] = (first * cos + second * sin).astype(BF16)
            back_t[pl.ds(at + mid, mid), :] = (second * cos - first * sin).astype(BF16)
            at = pl.multiple_of(p.q_part + p.kv_part + g * HEAD, HEAD)
            back_t[pl.ds(at, HEAD), :] = dv_acc[...].astype(BF16)

    def normed_back():
        load_qkv.wait()

        stores = [
            pltpu.make_async_copy(
                land_v.at[i % 2], norm_part.at[pl.ds(i * count, count), :], small_sem.at[i % 2]
            )
            for i in range(shards)
        ]
        for i, store in enumerate(stores):
            if i >= 2:
                stores[i - 2].wait()
            here = pl.ds(i * count, count)
            land_v[i % 2] = dot(back_t[:, here].T, qkv_v[...], NT).astype(BF16)
            store.start()
        for store in stores[-2:]:
            store.wait()
        for copy in norm_rows:
            copy.start()

    gain_cols = p.width // shards

    def gain_slice(shard):
        return pl.ds(pl.multiple_of(shard * gain_cols, gain_cols), gain_cols)

    gain_plane = [
        remote(
            gain_part.at[:, gain_slice(me ^ (i + 1))], gain_land.at[me],
            gain_send, gain_recv, i, rep, me ^ (i + 1),
        )
        for i in range(n)
    ]
    gain_all = [
        remote(gain_sum, gain_reps.at[rep], rep_send, rep_recv, i, rep ^ (i + 1), me)
        for i in range(reps - 1)
    ]

    def tokens_back():
        load_tokens.start()
        load_tokens.wait()
        fetch_rows(norm_rows, norm_part, norm_land)

        def strip(here):
            values = gh_own[here, :].astype(F32)
            rms = lax.rsqrt(jnp.mean(values * values, axis=-1, keepdims=True) + epsilon)
            grad_hidden[here, :] += norm_strip(here, values, rms, attn_gain[...], 0)

        strips(strip)
        store_tokens = pltpu.make_async_copy(grad_hidden, tokens_out, small_sem.at[0])
        store_tokens.start()
        store_tokens.wait()
        gain_land[me] = gain_part[:, gain_slice(me)]
        for copy in gain_plane:
            copy.start()

    def gains_plane():
        for copy in gain_plane:
            copy.wait_recv()
        total = gain_land[0]
        for s in range(1, shards):
            total = total + gain_land[s]
        gain_sum[...] = total
        gain_reps[rep] = total
        for copy in gain_all:
            copy.start()

    def gains_reps():
        for copy in gain_all:
            copy.wait_recv()
        total = gain_reps[0]
        for r in range(1, reps):
            total = total + gain_reps[r]
        gains_out[...] = total

    def swap_copy(j):
        return pltpu.make_async_remote_copy(
            src_ref=theirs.at[j % 2], dst_ref=swapped.at[j],
            send_sem=swap_send.at[j % 2], recv_sem=swap_recv.at[j],
            device_id=(rep ^ 1, me), device_id_type=MESH,
        )

    def store_chunk(slot, other_slot, at, size, product, columns=TILE):
        here = pl.ds(pl.multiple_of(at, size), size)
        mine[slot, here, :columns] = product(core).astype(BF16)
        theirs[other_slot, here, :columns] = product(1 - core).astype(BF16)

    def make(t):
        slot, other = t % p.mine_ring, t % 2

        @pl.when(t >= 2)
        def _():
            swap_copy(t - 2).wait_send()

        @pl.when(t == 0)
        def _():
            load_right(0)(lambda copy: copy.start())

        load_right(t)(lambda copy: copy.wait())

        @pl.when(t + 1 < ffn_end)
        def _():
            load_right(t + 1)(lambda copy: copy.start())

        @pl.when((t < ffn_end) & (t % 3 == 0))
        def _():
            left = right[t % 2].T

            def go(i, carry):
                def product(which):
                    at = pl.multiple_of(which * p.rows + i * TILE, TILE)
                    return dot(left, left_a[:, pl.ds(at, TILE)], NN)

                store_chunk(slot, other, i * TILE, TILE, product)
                return carry

            lax.fori_loop(0, p.rows // TILE, go, 0)

        def wide_chunk(left, factor, columns):
            def go(s, carry):
                def product(which):
                    at = pl.multiple_of(s * p.own + which * p.block, p.block)
                    return dot(factor, left[:, pl.ds(at, p.block)], NN).T

                store_chunk(slot, other, s * p.block, p.block, product, columns)
                return carry

            lax.fori_loop(0, shards, go, 0)

        @pl.when((t < ffn_end) & (t % 3 > 0))
        def _():
            wide_chunk(left_b, right[t % 2].T, TILE)

        @pl.when((t >= proj_at) & (t < q_at))
        def _():
            def go(i, carry):
                at = columns((t - proj_at) * p.proj_blocks + i)

                def product(which):
                    part = columns(which, p.proj_half)
                    return dot(mixed_ref[part, :], both[:, at], NN)

                store_chunk(slot, other, i * p.proj_half, p.proj_half, product)
                return carry

            lax.fori_loop(0, p.proj_blocks, go, 0)

        @pl.when((t >= q_at) & (t < kv_at))
        def _():
            wide_chunk(left_a, back_t[columns(t - q_at), :], TILE)

        @pl.when(t == kv_at)
        def _():
            wide_chunk(left_a, back_t[p.q_part :, :], 2 * p.kv_part)

        swap_copy(t).start()

    def inward_copies(j):
        common = dict(
            src_ref=sums.at[j % p.sum_ring], send_sem=in_send.at[j % p.sum_ring],
            device_id=(inward, me), device_id_type=MESH,
        )
        to_layer = pltpu.make_async_remote_copy(
            dst_ref=from_outer.at[j], recv_sem=outer_recv.at[j], **common
        )
        to_middle = pltpu.make_async_remote_copy(
            dst_ref=from_middle.at[j], recv_sem=middle_recv.at[j], **common
        )
        return to_layer, to_middle

    def total_places(j, action):
        @pl.when(is_chunk(j, 0))
        def _():
            action(
                [
                    (
                        i * TILE, TILE, TILE,
                        f_down.at[
                            columns(j // 3),
                            pl.ds(pl.multiple_of(core * p.rows + i * TILE, TILE), TILE),
                        ],
                    )
                    for i in range(p.rows // TILE)
                ]
            )

        @pl.when((j >= proj_at) & (j < q_at))
        def _():
            action(
                [
                    (
                        i * p.proj_half, p.proj_half, TILE,
                        f_proj.at[
                            columns(core, p.proj_half),
                            columns((j - proj_at) * p.proj_blocks + i),
                        ],
                    )
                    for i in range(p.proj_blocks)
                ]
            )

        for when, full, part, tile, sem, wide_by in wide_kinds(j):

            @pl.when(when)
            def _(full=full, part=part, tile=tile, wide_by=wide_by):
                blocks = []
                for i in range(shards):
                    at = pl.multiple_of((me ^ i) * p.block, p.block)
                    place_there = totals.at[j, pl.ds(at, p.block), pl.ds(0, wide_by)]
                    if i == 0:
                        place_there = window(full, me, part, tile, wide_by)
                    blocks.append((at, p.block, wide_by, place_there))
                action(blocks)

    def chunk_bytes(j, sem):
        @pl.when(j == kv_at)
        def _():
            whole = totals.at[0, :, pl.ds(0, 2 * p.kv_part)]
            pltpu.make_async_copy(whole, whole, sem).wait()

        @pl.when(j != kv_at)
        def _():
            whole = totals.at[0]
            pltpu.make_async_copy(whole, whole, sem).wait()

    def send_total(src, dst, j):
        return pltpu.make_async_remote_copy(
            src_ref=src, dst_ref=dst, send_sem=out_send.at[j % 2],
            recv_sem=total_recv.at[j], device_id=(outward, me), device_id_type=MESH,
        )

    def add_rows(body):
        def go(i, carry):
            body(pl.ds(pl.multiple_of(i * TILE, TILE), TILE))
            return carry

        lax.fori_loop(0, p.rows // TILE, go, 0)

    def load_swapped(j):
        return pltpu.make_async_copy(swapped.at[j], swap_v, small_sem.at[2])

    def load_outer(j):
        return pltpu.make_async_copy(from_outer.at[j], outer_v, small_sem.at[3])

    def load_middle(j):
        return pltpu.make_async_copy(from_middle.at[j], middle_v, small_sem.at[4])

    def valid(j):
        return (j >= 0) & (j < p.chunks)

    def take_inward(j):
        @pl.when(valid(j))
        def _():
            swap_copy(j).wait_recv()
            load_swapped(j).start()

            @pl.when(depth > 0)
            def _():
                inward_copies(j)[0].wait_recv()
                load_outer(j).start()

    def send_inward(j):
        @pl.when(valid(j))
        def _():
            @pl.when(j >= p.sum_ring)
            def _():
                inward_copies(j - p.sum_ring)[0].wait_send()

            load_swapped(j).wait()
            ours = mine.at[j % p.mine_ring]
            total = sums.at[j % p.sum_ring]

            @pl.when(depth > 0)
            def _():
                load_outer(j).wait()

                def add(here):
                    total[here, :] = (
                        ours[here, :].astype(F32)
                        + swap_v[here, :].astype(F32)
                        + outer_v[here, :].astype(F32)
                    ).astype(BF16)

                add_rows(add)

            @pl.when(depth == 0)
            def _():
                def add(here):
                    total[here, :] = (
                        ours[here, :].astype(F32) + swap_v[here, :].astype(F32)
                    ).astype(BF16)

                add_rows(add)

            to_layer, to_middle = inward_copies(j)

            @pl.when(is_middle)
            def _():
                to_middle.start()

            @pl.when(jnp.logical_not(is_middle))
            def _():
                to_layer.start()

    def take_middle(j):
        @pl.when(is_middle & valid(j))
        def _():
            inward_copies(j)[1].wait_recv()
            load_middle(j).start()

        @pl.when(is_middle & valid(j - 1))
        def _():
            chunk_bytes(j - 1, total_store.at[0])

    def meet_in_middle(j):
        @pl.when(is_middle & valid(j))
        def _():
            if p.half > 1:

                @pl.when(j >= 2)
                def _():
                    chunk_bytes(j - 2, out_send.at[j % 2])

            load_middle(j).wait()
            out, held = total_v.at[j % 2], sums.at[j % p.sum_ring]

            def add(here):
                out[here, :] = (
                    held[here, :].astype(F32) + middle_v[here, :].astype(F32)
                ).astype(BF16)

            add_rows(add)

            def put(blocks):
                for at, size, wide_by, dst in blocks:
                    src = out.at[pl.ds(at, size), pl.ds(0, wide_by)]
                    if p.half > 1:
                        send_total(src, dst, j).start()
                    pltpu.make_async_copy(src, dst, total_store.at[0]).start()

            total_places(j, put)

    def send_outward(j):
        @pl.when(jnp.logical_not(is_middle) & valid(j))
        def _():
            chunk_bytes(j, total_recv.at[j])

            if p.half > 2:

                @pl.when(depth > 0)
                def _():
                    @pl.when(j >= 2)
                    def _():
                        chunk_bytes(j - 2, out_send.at[j % 2])

                    def put(blocks):
                        for _, _, _, dst in blocks:
                            send_total(dst, dst, j).start()

                    total_places(j, put)

    def remote_pass(src, dst, sem):
        return pltpu.make_async_remote_copy(
            src_ref=src, dst_ref=dst, send_sem=pass_send.at[sem], recv_sem=pass_recv.at[sem],
            device_id=(rep ^ 1, me), device_id_type=MESH,
        )

    def window(full, shard, part, tile, columns=TILE):
        at = pl.multiple_of(shard * part + tile * columns, columns)
        return full.at[pl.ds(pl.multiple_of(core * p.block, p.block), p.block), pl.ds(at, columns)]

    def is_chunk(j, kind):
        return (j >= 0) & (j < ffn_end) & (j % 3 == kind)

    def wide_kinds(j):
        return (
            (is_chunk(j, 1), f_gate, p.ffn_part, j // 3, 1, TILE),
            (is_chunk(j, 2), f_up, p.ffn_part, j // 3, 2, TILE),
            ((j >= q_at) & (j < kv_at), f_q, p.q_part, j - q_at, 4, TILE),
            (j == kv_at, f_kv, 2 * p.kv_part, 0, 5, 2 * p.kv_part),
        )

    def spread_total(j):
        for kind, sem in ((is_chunk(j, 0), 0), ((j >= proj_at) & (j < q_at), 3)):

            @pl.when(kind)
            def _(sem=sem):
                def put(blocks):
                    for _, _, _, dst in blocks:
                        remote_pass(dst, dst, sem).start()

                total_places(j, put)

        for when, full, part, tile, sem, wide_by in wide_kinds(j):

            @pl.when(when)
            def _(full=full, part=part, tile=tile, sem=sem, wide_by=wide_by):
                place_here = window(full, me, part, tile, wide_by)
                for i in range(n):
                    at = columns(me ^ (i + 1), p.block)
                    pltpu.make_async_remote_copy(
                        src_ref=totals.at[j, at, pl.ds(0, wide_by)], dst_ref=place_here,
                        send_sem=cross_send.at[sem], recv_sem=cross_recv.at[j],
                        device_id=(rep, me ^ (i + 1)), device_id_type=MESH,
                    ).start()
                remote_pass(place_here, place_here, sem).start()

    def pass_on(j):
        for when, full, part, tile, sem, wide_by in wide_kinds(j):

            @pl.when(when)
            def _(full=full, part=part, tile=tile, sem=sem, wide_by=wide_by):
                came = totals.at[j, pl.ds(0, n * p.block), pl.ds(0, wide_by)]
                pltpu.make_async_copy(came, came, cross_recv.at[j]).wait()
                for i in range(n):
                    here = window(full, me ^ (i + 1), part, tile, wide_by)
                    remote_pass(here, here, sem).start()

    for copy in (load_x, load_cot):
        copy.start()
    load_tile(0)
    greet(plane_partners(rep, me, shards) + [(rep ^ i, me) for i in range(1, reps)])
    ahead = 3
    for tile in range(first_tile, min(first_tile + ahead, p.tiles)):
        send_tile(tile)
    for copy in (load_hidden, load_proj, load_qkv):
        copy.start()
    for copy in (load_x, load_cot):
        copy.wait()

    def slot(t, carry):
        take_inward(t - 1 - p.lag * depth)
        take_middle(t - p.meet)
        send_outward(t - p.spread + p.lag * depth)
        spread_total(t - p.spread)
        pass_on(t - p.hand)

        @pl.when(t + first_tile + ahead < p.tiles)
        def _():
            send_tile(t + first_tile + ahead)

        @pl.when(t < p.tiles)
        def _():
            ffn_tile(t)

        @pl.when((t >= p.back_slot) & (t <= p.send_slot))
        def _():
            back_tiles((t - p.back_slot) * p.per_slot)

        @pl.when(t == ffn_end)
        def _():
            load_normed.start()
            load_activ.start()

        @pl.when(t == q_at)
        def _():
            load_normed.wait()

        @pl.when(t < p.chunks)
        def _():
            make(t)

        def at(when, action):
            @pl.when(t == when)
            def _():
                action()

        def start_rows(copies):
            for copy in copies:
                copy.start()

        @pl.when((t + 2 >= first_tile) & (t + 2 < p.tiles))
        def _():
            pass_tile(t + 2)

        send_inward(t - 1 - p.lag * depth)
        meet_in_middle(t - p.meet)
        at(p.send_slot, lambda: start_rows(back_rows))
        at(p.rows_slot, hidden_back)
        at(p.pass_slot, gather.hand_on)
        at(p.mixed_slot, mixed_back)

        @pl.when((t >= p.unit_slot) & (t < p.norm_slot))
        def _():
            def go(i, c):
                attention_unit((t - p.unit_slot) * 2 + i)
                return c

            lax.fori_loop(0, 2, go, 0)

        at(p.norm_slot, normed_back)
        at(p.tokens_slot, tokens_back)
        at(p.gain_slot, gains_plane)
        at(p.rep_slot, gains_reps)

        @pl.when((t >= p.res_slot) & (t < p.res_slot + p.out_tiles // 2))
        def _():
            @pl.when(t == p.res_slot)
            def _():
                load_activ.wait()
                load_res(0)(lambda copy: copy.start())

            res_tiles((t - p.res_slot) * 2)

        at(p.res_slot + p.out_tiles // 2 - 1, lambda: start_rows(res_rows))
        at(p.result_slot, finish_result)
        return carry

    lax.fori_loop(0, p.slots, slot, 0)

    for j in range(max(0, p.chunks - 2), p.chunks):
        swap_copy(j).wait_send()
    for j in range(max(0, p.chunks - p.sum_ring), p.chunks):
        inward_copies(j)[0].wait_send()
    if p.half > 1:

        @pl.when(depth > 0)
        def _():
            for j in range(max(0, p.chunks - 2), p.chunks):
                chunk_bytes(j, out_send.at[j % 2])

    for copies in (back_rows, res_rows, norm_rows, gain_plane, gain_all):
        for copy in copies:
            copy.wait_send()

    def settle(ref, sem):
        pltpu.make_async_copy(ref, ref, sem).wait()

    for tile in range(first_tile, p.tiles):
        tile_bytes(tile, tile_send).wait()
        tile_bytes(tile, tile_pass).wait()
    for sem, part in (
        (0, f_down.at[:, pl.ds(0, p.rows)]),
        (3, f_proj.at[pl.ds(0, p.proj_half), :]),
    ):
        settle(part, pass_send.at[sem])
        settle(part, pass_recv.at[sem])
    for _, full, part, _, sem, _ in wide_kinds(0):
        here = full.at[pl.ds(0, p.block), :]
        settle(here, pass_send.at[sem])
        settle(here, pass_recv.at[sem])
        settle(full.at[pl.ds(0, p.block), pl.ds(0, n * part)], cross_send.at[sem])


def backward(
    shards, reps, x, cot_all, gate_w, up_w, gate_e, up_e, down_w, hidden, tokens, proj_w,
    qkv_m, normed, mlp_rms, mlp_gain, attn_gain, seg, cos_t, sin_t, lse, q_t, mixed_t, k, k_t, v,
):
    length, width = x.shape
    count = tokens.shape[0]
    ffn_part = down_w.shape[0]
    q_part, kv_part = q_t.shape[0], k_t.shape[0]
    n = shards - 1
    p = Plan(shards, reps, length, width, ffn_part, q_part, kv_part)
    shape = jax.ShapeDtypeStruct
    own = width // shards
    chunk = (p.rows, TILE)
    dma = pltpu.SemaphoreType.DMA
    return pl.pallas_call(
        functools.partial(backward_kernel, p, gate_e.shape[1]),
        in_specs=[ANY] * 12 + [IN_VMEM] * 13,
        out_specs=[ANY] * 8 + [IN_VMEM] + [ANY] * 15,
        out_shape=[
            shape((ffn_part, width), BF16),
            shape((own, shards * ffn_part), BF16),
            shape((own, shards * ffn_part), BF16),
            shape((q_part, width), BF16),
            shape((own, shards * q_part), BF16),
            shape((own, shards * 2 * kv_part), BF16),
            shape((count, width), F32),
            shape((count, width), F32),
            shape((8, width // shards), F32),
        ]
        + [shape((p.chunks,) + chunk, BF16)] * 4
        + [shape((n, count, width), BF16)] * 3
        + [shape((length, width), BF16)]
        + [shape((width, ffn_part), BF16)] * 2
        + [shape((length, ffn_part), BF16)] * 3
        + [shape((length, width), BF16)] * 2,
        scratch_shapes=[
            pltpu.VMEM((length, width), BF16),
            pltpu.VMEM((length, width), BF16),
            pltpu.VMEM((2, length, TILE), BF16),
            pltpu.VMEM((width, TILE), BF16),
            pltpu.VMEM((width, TILE), BF16),
            pltpu.VMEM((TILE, width), BF16),
            pltpu.VMEM((2, TILE, 2 * ffn_part), BF16),
            pltpu.VMEM((2, length, TILE), BF16),
            pltpu.VMEM((length, 2 * ffn_part), BF16),
            pltpu.VMEM(proj_w.shape, BF16),
            pltpu.VMEM(qkv_m.shape, BF16),
            pltpu.VMEM((count, width), F32),
            pltpu.VMEM((count, width), F32),
            pltpu.VMEM((2, count, width), BF16),
            pltpu.VMEM((p.mine_ring,) + chunk, BF16),
            pltpu.VMEM((2,) + chunk, BF16),
            pltpu.VMEM(chunk, BF16),
            pltpu.VMEM(chunk, BF16),
            pltpu.VMEM(chunk, BF16),
            pltpu.VMEM((p.sum_ring,) + chunk, BF16),
            pltpu.VMEM((2,) + chunk, BF16),
            pltpu.VMEM((count, width), F32),
            pltpu.VMEM((count, width), BF16),
            pltpu.VMEM((q_part, length), BF16),
            pltpu.VMEM((q_part + 2 * kv_part, length), BF16),
            pltpu.VMEM((HEAD, length), F32),
            pltpu.VMEM((HEAD, length), F32),
            pltpu.VMEM((8, width), F32),
            pltpu.VMEM((shards, 8, own), F32),
            pltpu.VMEM((8, own), F32),
            pltpu.VMEM((reps, 8, own), F32),
            dma((12,)), dma((2,)), dma((5,)), dma((2,)), dma((p.chunks,)), dma((p.sum_ring,)),
            dma((p.chunks,)), dma((p.chunks,)), dma((2,)), dma((p.chunks,)), dma((2,)),
            dma((p.chunks,)), dma((6,)), dma((6,)), dma((6,)),
            dma((n,)), dma((n,)), dma((n,)), dma((n,)), dma((n,)), dma((n,)),
        ]
        + Gather.semaphores(shards)
        + [dma((n,)), dma((n,)), dma((reps - 1,)), dma((reps - 1,))]
        + [dma((p.tiles,))] * 4
        + [dma((3,)), dma((2, 2)), dma((3,))],
        compiler_params=pltpu.CompilerParams(
            collective_id=3, has_side_effects=True, vmem_limit_bytes=63 * MIB + MIB // 2
        ),
        name="backward",
    )(
        x, cot_all, gate_w, up_w, gate_e, up_e, down_w, hidden, tokens, proj_w,
        qkv_m, normed, mlp_rms, mlp_gain[None, :], attn_gain[None, :], seg[:, None], seg[None, :],
        cos_t, sin_t, lse, q_t, mixed_t, k, k_t, v,
    )[:9]


def local(
    tokens, segments, query_w, key_w, value_w, proj_w, attn_gain,
    gate_w, up_w, down_w, mlp_gain, cotangent,
):
    shards = lax.axis_size("shard")
    reps = lax.axis_size("rep")
    tok_count, width = tokens.shape
    kv_part = key_w.shape[1] // shards
    q_part = query_w.shape[1] // shards
    length = tok_count * shards

    if kv_part % 128:
        kv_w = jnp.concatenate(
            [
                w[:, s * kv_part : (s + 1) * kv_part]
                for s in range(shards)
                for w in (key_w, value_w)
            ],
            axis=1,
        )
        weights = (query_w, kv_w)
    else:
        weights = (query_w, key_w, value_w)
    tokens_all, seg, qkv_m = first(tokens, segments[None, :], weights, shards)
    seg = seg.reshape(length)
    cos_t, sin_t = rope_tables(doc_positions(seg))
    early = min(2 * TILE, down_w.shape[0] // 2)
    normed, cot_all, proj_m, gate_e, up_e, q_t, k, k_t, v, mixed_t, lse = attend(
        tokens_all, qkv_m, cotangent, proj_w, gate_w, up_w, attn_gain, seg, cos_t, sin_t,
        q_part, kv_part, early, shards,
    )
    hidden, mlp_rms, normed_mlp = hidden_layer(mixed_t, proj_m, proj_w, tokens, mlp_gain, shards)
    down, gate, up, proj, query, kv, result, grad_tokens, gains = backward(
        shards, reps, normed_mlp, cot_all, gate_w, up_w, gate_e, up_e, down_w, hidden, tokens,
        proj_w, qkv_m, normed, mlp_rms, mlp_gain, attn_gain, seg, cos_t, sin_t, lse, q_t,
        mixed_t, k, k_t, v,
    )

    def every_other(first):
        parts = [
            kv[:, (2 * s + first) * kv_part : (2 * s + first + 1) * kv_part] for s in range(shards)
        ]
        return jnp.concatenate(parts, axis=1).astype(F32)

    return (
        result, grad_tokens, query.astype(F32), every_other(0), every_other(1), proj.astype(F32),
        gains[0], gate.astype(F32), up.astype(F32), down.astype(F32), gains[1],
    )


def solution(mesh):
    rows = P(("rep", "shard"), None)
    held = P("shard", None)
    in_specs = (
        rows, P(("rep", "shard")), held, held, held, held, P(), held, held, held, P(), rows,
    )
    out_specs = (
        rows, rows, held, held, held, held, P("shard"), held, held, held, P("shard"),
    )
    return jax.shard_map(local, mesh=mesh, in_specs=in_specs, out_specs=out_specs, check_vma=False)
```

time: 851 us -> 688 us (0.81)
  Pallas kernels: 714 us -> 621 us
  matrix products: 46.8 us -> 0 us
  local copies, waits for them, and re-layouts: 35 us -> 21.8 us
    pallas_call x4 -> x3, Pallas kernels: 661 us -> 577 us  [the longest x1 450 us: backward(): pl.pallas_call(functools.partial(backward_kernel, p, gate_e.shape[1]), in...]
    dot_general x4 -> x0, matrix products: 46.8 us -> none  [dot(): lax.dot_general(left, right, (dims, ((), ())), preferred_element_type=F32)]
    unnamed x79 -> x60, local copies, waits for them, and re-layouts: 27.4 us -> 17.9 us
where the time goes in v2:
time: 688 us; the launch traced here: 687 us
  Pallas kernels  621 us (90%)
  other arithmetic  43.5 us (6%)
  local copies, waits for them, and re-layouts  21.8 us (3%)
    pallas_call x1, Pallas kernels, backward(): pl.pallas_call(functools.partial(backward_kernel, p, gate_e.shape[1]), in...  450 us
    pallas_call x1, Pallas kernels, attend(): pl.pallas_call(functools.partial(attend_kernel, shards, part, early), in_...  78.1 us
    pallas_call x1, Pallas kernels, first(): pl.pallas_call(functools.partial(first_kernel, shards, parts), in_specs=[...  48.1 us
    pallas_call x1, Pallas kernels, hidden_layer(): pl.pallas_call(functools.partial(hidden_kernel, shards), in_specs=[IN_VME...  44.6 us
    unnamed x60, local copies, waits for them, and re-layouts  17.9 us

profile of v2, /device:TPU:0, one launch (start us, length us, event | category | flops | bytes accessed | tf_op | source)
XLA Modules:
  0.0 687.3 jit_solution(8202891587570564002)
XLA Ops:
  0.7 0.0 copy-start.2
  0.7 1.2 copy-done.2
  1.9 1.6 copy-done.9
  3.5 1.0 copy-done.16
  4.5 1.0 copy-done.17
  5.6 0.7 copy-done.24
  6.2 48.1 %first.1 = (bf16[1024,2048]{1,0:T(8,128)(2,1)S(1)}, s32[4,1,256]{2,1,0:T(1,128)S(1)}, bf16[2048,768]{1,0:T(8,128)(2,1)S(1)}) custom-call(bf16[256,2048]{1,0:T(8,128)(2,1)S(1)} %copy-done.2, s32[1,256]{1,0:T(1,128)S(1)} %bitcast.30, bf16[512,2048]{1,0:T(8,128)(2,1)S(1)} %copy-done.9, bf16[512,512]{1,0:T(8,128)(2,1)S(1)} %copy-done.16, ...), custom_call_target="tpu_custom_call" | custom-call | tf_op jit(solution)/shard_map/first/pallas_call | solution.py:253
  54.4 0.0 copy-start.1
  54.4 1.7 copy-done.1
  56.1 2.0 copy-done.6
  58.1 0.6 slice.45
  58.7 0.7 fusion.2
  59.4 0.3 reduce-window.9
  59.7 0.1 slice.47
  59.8 0.1 slice_reduce_fusion
  59.9 0.1 fusion.1
  60.0 0.5 multiply_sine_fusion
  60.5 0.0 copy-start.10
  60.5 0.0 copy-start.11
  60.5 0.2 copy.23.seg_col
  60.7 0.0 copy-done.12
  60.8 0.0 copy-done.21
  60.8 0.0 copy-start.4
  60.8 0.0 copy-start
  60.8 0.0 copy-start.3
  60.8 0.0 copy-start.22
  60.8 78.1 %attend.1 = (bf16[1024,2048]{1,0:T(8,128)(2,1)}, bf16[1024,2048]{1,0:T(8,128)(2,1)}, bf16[2048,2048]{1,0:T(8,128)(2,1)}, bf16[2048,512]{1,0:T(8,128)(2,1)}, bf16...) custom-call(bf16[1024,2048]{1,0:T(8,128)(2,1)} %copy-done.6, ...), custom_call_target="tpu_custom_call" | custom-call | tf_op jit(solution)/shard_map/attend/pallas_call | solution.py:464
  138.9 0.0 copy-done.20
  139.0 0.0 copy-done.10
  139.0 0.0 copy-done.11
  139.0 0.0 copy-done.4
  139.0 0.0 copy-start.13
  139.0 1.0 copy-done.13
  140.0 0.0 copy-start.23
  140.0 0.0 copy-done
  140.0 0.0 copy-done.3
  140.0 0.0 copy-done.22
  140.0 44.6 %hidden.1 = (f32[256,2048]{1,0:T(8,128)S(1)}, f32[256,1]{1,0:T(8,128)S(1)}, bf16[1024,2048]{1,0:T(8,128)(2,1)S(1)}) custom-call(bf16[512,1024]{1,0:T(8,128)(2,1)S(1)} %get-tuple-element.40.mixed_t.mixed_ref, bf16[2048,2048]{1,0:T(8,128)(2,1)} %get-tuple-element.41.proj_m, bf16[512,2048]{1,0:T(8,128)(2,1)S(1)} %copy-done, bf16[256,2048]{1,0:T(8,128)(2,1)S(1)} %copy-done.3, ...), custom_call_target="tpu_custom_call" | custom-call | tf_op jit(solution)/shard_map/hidden/pallas_call | solution.py:557
  184.6 0.0 copy-done.7
  184.6 0.0 copy-done.14
  184.6 0.0 copy-done.15
  184.6 0.0 copy-done.18
  184.6 0.0 copy-done.23
  184.6 0.0 copy-start.5
  184.6 2.0 copy-done.5
  186.6 1.3 copy-done.8
  188.0 0.7 copy-done.19
  188.6 450.3 %backward.1 = (bf16[2048,2048]{1,0:T(8,128)(2,1)}, bf16[512,8192]{1,0:T(8,128)(2,1)}, bf16[512,8192]{1,0:T(8,128)(2,1)}, bf16[512,2048]{1,0:T(8,128)(2,1)}, bf16...) custom-call(bf16[1024,2048]{1,0:T(8,128)(2,1)} %copy-done.5, ...), custom_call_target="tpu_custom_call" | custom-call | tf_op jit(solution)/shard_map/backward/pallas_call | solution.py:1606
  638.9 0.0 copy-start.26
  639.0 1.5 fusion.6
  640.4 1.4 fusion.5
  641.8 0.0 copy-start.25
  641.8 1.5 maximum_convert_fusion
  643.3 0.0 copy-done.26
  643.3 2.5 convert_element_type.29
  645.8 0.0 copy-done.25
  645.8 2.5 convert_element_type.32
  648.4 11.7 %convert_element_type.33 = f32[512,8192]{1,0:T(8,128)} convert(bf16[512,8192]{1,0:T(8,128)(2,1)} %get-tuple-element.60) | non-fusion elementwise | flops 4194304 | bytes 25165824 | tf_op jit(solution)/shard_map/convert_element_type | solution.py:1725
  660.1 11.7 %convert_element_type.34 = f32[512,8192]{1,0:T(8,128)} convert(bf16[512,8192]{1,0:T(8,128)(2,1)} %get-tuple-element.61) | non-fusion elementwise | flops 4194304 | bytes 25165824 | tf_op jit(solution)/shard_map/convert_element_type | solution.py:1725
  671.9 11.8 %convert_element_type.35 = f32[2048,2048]{1,0:T(8,128)} convert(bf16[2048,2048]{1,0:T(8,128)(2,1)} %get-tuple-element.62) | non-fusion elementwise | flops 4194304 | bytes 25165824 | tf_op jit(solution)/shard_map/convert_element_type | solution.py:1725
  683.7 0.0 copy-done.28
  683.7 1.3 copy.27
  685.0 1.0 copy-done.27
  686.0 1.3 copy.28
  (18 shorter events, 0.1 us)
Async XLA Ops:
  0.7 1.2 copy-start.2
  1.9 1.6 copy-start.9
  3.5 1.0 copy-start.16
  4.5 1.0 copy-start.17
  5.6 0.7 copy-start.24
  6.2 54.5 %copy-start.12 = (bf16[256,2048]{1,0:T(8,128)(2,1)S(1)}, bf16[256,2048]{1,0:T(8,128)(2,1)}, u32[]{:S(2)}) copy-start(bf16[256,2048]{1,0:T(8,128)(2,1)} %cot.1) | copy-start | bytes 3145732
  6.2 54.5 %copy-start.21 = (f32[2048]{0:T(1024)S(1)}, f32[2048]{0:T(1024)}, u32[]{:S(2)}) copy-start(f32[2048]{0:T(1024)} %param.18) | copy-start | bytes 24580
  54.4 1.7 copy-start.1
  56.1 2.0 copy-start.6
  58.1 80.9 %copy-start.20 = (s32[4,1,256]{2,1,0:T(1,128)}, s32[4,1,256]{2,1,0:T(1,128)S(1)}, u32[]{:S(2)}) copy-start(s32[4,1,256]{2,1,0:T(1,128)S(1)} %get-tuple-element.39) | copy-start | bytes 12292
  60.5 78.5 %copy-start.10 = (f32[32,1024]{1,0:T(8,128)}, f32[32,1024]{1,0:T(8,128)S(1)}, u32[]{:S(2)}) copy-start(f32[32,1024]{1,0:T(8,128)S(1)} %get-tuple-element.73.sin_ref) | copy-start | bytes 393220
  60.5 78.5 %copy-start.11 = (f32[32,1024]{1,0:T(8,128)}, f32[32,1024]{1,0:T(8,128)S(1)}, u32[]{:S(2)}) copy-start(f32[32,1024]{1,0:T(8,128)S(1)} %get-tuple-element.74.cos_ref) | copy-start | bytes 393220
  60.8 78.2 %copy-start.4 = (s32[1024,1]{1,0:T(8,128)}, s32[1024,1]{1,0:T(8,128)S(1)}, u32[]{:S(2)}) copy-start(s32[1024,1]{1,0:T(8,128)S(1)} %copy.23.seg_col) | copy-start | bytes 12292
  60.8 79.2 %copy-start = (bf16[512,2048]{1,0:T(8,128)(2,1)S(1)}, bf16[512,2048]{1,0:T(8,128)(2,1)}, u32[]{:S(2)}) copy-start(bf16[512,2048]{1,0:T(8,128)(2,1)} %proj_w.5) | copy-start | bytes 6291460
  60.8 79.2 %copy-start.3 = (bf16[256,2048]{1,0:T(8,128)(2,1)S(1)}, bf16[256,2048]{1,0:T(8,128)(2,1)}, u32[]{:S(2)}) copy-start(bf16[256,2048]{1,0:T(8,128)(2,1)} %tokens.5) | copy-start | bytes 3145732
  60.8 79.2 %copy-start.22 = (f32[2048]{0:T(1024)S(1)}, f32[2048]{0:T(1024)}, u32[]{:S(2)}) copy-start(f32[2048]{0:T(1024)} %param.22) | copy-start | bytes 24580
  139.0 1.0 copy-start.13
  140.0 44.6 %copy-start.7 = (bf16[512,1024]{1,0:T(8,128)(2,1)}, bf16[512,1024]{1,0:T(8,128)(2,1)S(1)}, u32[]{:S(2)}) copy-start(bf16[512,1024]{1,0:T(8,128)(2,1)S(1)} %get-tuple-element.40.mixed_t.mixed_ref) | copy-start | bytes 3145732
  140.0 44.6 %copy-start.14 = (bf16[2,1024,64]{2,1,0:T(8,128)(2,1)}, bf16[2,1024,64]{2,1,0:T(8,128)(2,1)S(1)}, u32[]{:S(2)}) copy-start(bf16[2,1024,64]{2,1,0:T(8,128)(2,1)S(1)} %get-tuple-element.51.k_ref) | copy-start | bytes 786436
  140.0 44.6 %copy-start.15 = (bf16[2,1024,64]{2,1,0:T(8,128)(2,1)}, bf16[2,1024,64]{2,1,0:T(8,128)(2,1)S(1)}, u32[]{:S(2)}) copy-start(bf16[2,1024,64]{2,1,0:T(8,128)(2,1)S(1)} %get-tuple-element.53.v_ref) | copy-start | bytes 786436
  140.0 44.6 %copy-start.18 = (bf16[128,1024]{1,0:T(8,128)(2,1)}, bf16[128,1024]{1,0:T(8,128)(2,1)S(1)}, u32[]{:S(2)}) copy-start(bf16[128,1024]{1,0:T(8,128)(2,1)S(1)} %get-tuple-element.52.kt_ref) | copy-start | bytes 786436
  140.0 44.6 %copy-start.23 = (f32[2,4,1024]{2,1,0:T(4,128)}, f32[2,4,1024]{2,1,0:T(4,128)S(1)}, u32[]{:S(2)}) copy-start(f32[2,4,1024]{2,1,0:T(4,128)S(1)} %get-tuple-element.49.lse_ref) | copy-start | bytes 98308
  184.6 2.0 copy-start.5
  186.6 1.3 copy-start.8
  188.0 0.7 copy-start.19
  638.9 4.3 copy-start.26
  641.8 4.0 copy-start.25
  671.9 11.8 %copy-start.28 = (f32[256,2048]{1,0:T(8,128)S(1)}, f32[256,2048]{1,0:T(8,128)}, u32[]{:S(2)}) copy-start(f32[256,2048]{1,0:T(8,128)} %get-tuple-element.88) | copy-start | bytes 6291460
  683.7 2.3 copy-start.27

commit v3 on v2

--- a/solution.py
+++ b/solution.py
@@ -16,6 +16,7 @@
 TILE = 256
 NEG = -1e30
 MIB = 1024 * 1024
+FULL = 63 * MIB + MIB // 2
 
 epsilon = 1e-05
 rope_base = 500000.0
@@ -266,7 +267,7 @@
         + Gather.semaphores(shards)
         + [pltpu.SemaphoreType.DMA((n,)), pltpu.SemaphoreType.DMA((n,)), pltpu.SemaphoreType.DMA],
         compiler_params=pltpu.CompilerParams(
-            collective_id=0, has_side_effects=True, vmem_limit_bytes=40 * MIB
+            collective_id=0, has_side_effects=True, vmem_limit_bytes=FULL
         ),
         name="first",
     )(tokens, seg, *weights)
@@ -490,7 +491,7 @@
         + 3 * Spread.semaphores(shards)
         + Gather.semaphores(shards),
         compiler_params=pltpu.CompilerParams(
-            collective_id=1, has_side_effects=True, vmem_limit_bytes=48 * MIB
+            collective_id=1, has_side_effects=True, vmem_limit_bytes=FULL
         ),
         name="attend",
     )(
@@ -500,8 +501,8 @@
 
 
 def hidden_kernel(
-    shards, mixed_t, proj_m, proj_w, tokens, gain, hidden_ref, rms_ref, normed_all,
-    proj_v, mixed_own, normed, proj_sem, mix_send, mix_recv, gather_send, gather_recv, local_sem,
+    shards, mixed_t, proj_m, proj_w, cot_all, down_w, tokens, gain, hidden_ref, rms_ref, normed_all,
+    grad_activ, proj_v, mixed_own, normed, cot_v, down_v, out_v, cot_sem, out_sem, proj_sem, mix_send, mix_recv, gather_send, gather_recv, local_sem,
 ):
     rep, me = place()
     part, _ = mixed_t.shape
@@ -516,6 +517,12 @@
     ]
     for copy in rows:
         copy.start()
+    early = [
+        pltpu.make_async_copy(cot_all, cot_v, cot_sem.at[0]),
+        pltpu.make_async_copy(down_w, down_v, cot_sem.at[1]),
+    ]
+    for copy in early:
+        copy.start()
     greet(plane_partners(rep, me, shards))
 
     def columns(shard):
@@ -546,37 +553,66 @@
     gather.start()
     for copy in copies:
         copy.wait_send()
+    for copy in early:
+        copy.wait()
+
+    steps = down_w.shape[0] // TILE
+
+    def store(i):
+        at = pl.ds(pl.multiple_of(i * TILE, TILE), TILE)
+        return pltpu.make_async_copy(out_v.at[i % 2], grad_activ.at[:, at], out_sem.at[i % 2])
+
+    def step(i, carry):
+        @pl.when(i >= 2)
+        def _():
+            store(i - 2).wait()
+
+        units = down_v[pl.ds(pl.multiple_of(i * TILE, TILE), TILE), :]
+        out_v[i % 2] = dot(cot_v[...], units, NT).astype(BF16)
+        store(i).start()
+        return carry
+
+    lax.fori_loop(0, steps // 2, step, 0)
     gather.hand_on()
+    lax.fori_loop(steps // 2, steps, step, 0)
+    for i in range(max(0, steps - 2), steps):
+        store(i).wait()
     gather.finish()
 
 
-def hidden_layer(mixed_t, proj_m, proj_w, tokens, gain, shards):
+def hidden_layer(mixed_t, proj_m, proj_w, cot_all, down_w, tokens, gain, shards):
     part, length = mixed_t.shape
     count, width = tokens.shape
     n = shards - 1
     return pl.pallas_call(
         functools.partial(hidden_kernel, shards),
-        in_specs=[IN_VMEM, ANY, ANY, IN_VMEM, IN_VMEM],
-        out_specs=[IN_VMEM, IN_VMEM, ANY],
+        in_specs=[IN_VMEM, ANY, ANY, ANY, ANY, IN_VMEM, IN_VMEM],
+        out_specs=[IN_VMEM, IN_VMEM, ANY, ANY],
         out_shape=[
             jax.ShapeDtypeStruct((count, width), F32),
             jax.ShapeDtypeStruct((count, 1), F32),
             jax.ShapeDtypeStruct((length, width), BF16),
+            jax.ShapeDtypeStruct((length, down_w.shape[0]), BF16),
         ],
         scratch_shapes=[
             pltpu.VMEM(proj_m.shape, BF16),
             pltpu.VMEM((n, part, count), BF16),
             pltpu.VMEM((count, width), BF16),
+            pltpu.VMEM(cot_all.shape, BF16),
+            pltpu.VMEM(down_w.shape, BF16),
+            pltpu.VMEM((2, length, TILE), BF16),
+            pltpu.SemaphoreType.DMA((2,)),
+            pltpu.SemaphoreType.DMA((2,)),
             pltpu.SemaphoreType.DMA((shards,)),
             pltpu.SemaphoreType.DMA((n,)),
             pltpu.SemaphoreType.DMA((n,)),
         ]
         + Gather.semaphores(shards),
         compiler_params=pltpu.CompilerParams(
-            collective_id=2, has_side_effects=True, vmem_limit_bytes=40 * MIB
+            collective_id=2, has_side_effects=True, vmem_limit_bytes=FULL
         ),
         name="hidden",
-    )(mixed_t, proj_m, proj_w, tokens, gain[None, :])
+    )(mixed_t, proj_m, proj_w, cot_all, down_w, tokens, gain[None, :])
 
 
 class Plan:
@@ -592,10 +628,10 @@
         self.proj_blocks = self.rows // self.proj_half
         self.tiles = ffn_part // TILE
         self.out_tiles = width // TILE
-        per_slot = 4
+        per_slot = 3
         self.back_slot = self.tiles
-        self.send_slot = self.back_slot + self.out_tiles // per_slot - 1
-        self.rows_slot = self.send_slot + 4
+        self.send_slot = self.back_slot + -(-self.out_tiles // per_slot) - 1
+        self.rows_slot = self.send_slot + 5
         self.pass_slot = self.rows_slot + 2
         self.mixed_slot = self.rows_slot + 4
         self.unit_slot = self.mixed_slot + 1
@@ -603,36 +639,49 @@
         self.units = (length // TILE) * (kv_part // HEAD)
         self.norm_slot = self.unit_slot + self.units // 2
         self.tokens_slot = self.norm_slot + 5
-        self.gain_slot = self.tokens_slot + 1
-        self.rep_slot = self.gain_slot + 1
-        proj = width // TILE // self.proj_blocks
         self.ffn_end = 3 * self.tiles
-        self.proj_at = max(self.ffn_end, self.norm_slot)
-        self.q_at = max(self.proj_at + proj, self.norm_slot + 1)
-        assert self.q_at == self.proj_at + proj
+        self.q_at = max(self.ffn_end, self.norm_slot)
         self.kv_at = self.q_at + q_part // TILE
-        self.chunks = self.kv_at + 1
+        self.proj_at = self.kv_at + 1
+        self.chunks = self.proj_at + width // TILE // self.proj_blocks
         self.res_slot = max(self.ffn_end + 1, self.norm_slot + 1)
-        self.result_slot = self.res_slot + self.out_tiles // 2 + 3
-        lag = 3 if self.layers <= 4 else 1
+        self.res_send_slot = max(self.res_slot + self.out_tiles // 2 - 1, self.tokens_slot + 1)
+        self.result_slot = self.res_send_slot + 8
+        lag = 2 if self.layers == 4 else 1
+        skips = [self.send_slot + 1] if self.layers == 4 else []
+        more = [self.send_slot + 3] if skips else []
+        self.skips = {hop: skips if hop == 1 else skips + more for hop in range(1, self.half + 1)}
         self.lag = lag
-        self.meet = 1 + lag * self.half
-        self.spread = 1 + lag * (self.layers - 1)
-        self.hand = self.spread + lag
-        self.slots = max(self.chunks + self.hand, self.rep_slot, self.result_slot) + 1
-        self.mine_ring = 2 + lag * (self.half - 1)
-        self.sum_ring = lag + 2
+        self.most = lag + len(skips)
+        self.arrive = 1 + self.most * (self.layers - 1)
+        self.spread_slot = self.pass_slot
+        self.hand = 6
+        self.gain_slot = self.tokens_slot + 2
+        self.rep_slot = max(self.chunks + self.arrive, self.gain_slot + 1)
+        self.slots = max(self.chunks + self.arrive + self.hand, self.rep_slot, self.result_slot) + 1
+        assert self.spread_slot + self.chunks // 2 < self.slots - self.hand
+        self.mine_ring = 2 + self.most * (self.half - 1)
+        self.sum_ring = self.most + 2
+
+    def hop_chunk(self, t, hop):
+        skips = self.skips.get(hop, [])
+        chunk = t - 1 - self.lag * hop
+        for skip in skips:
+            chunk = chunk - (t >= skip).astype(jnp.int32)
+        for skip in skips:
+            chunk = jnp.where(t == skip, -1, chunk)
+        return chunk
 
 
 def backward_kernel(
-    plan, early, x, cot_all, gate_w, up_w, gate_e, up_e, down_w, hidden, tokens, proj_w, qkv_m,
+    plan, early, x, cot_all, grad_activ, gate_w, up_w, gate_e, up_e, down_w, hidden, tokens, proj_w, qkv_m,
     normed,
     mlp_rms, mlp_gain, attn_gain, seg_col, seg_row, cos_ref, sin_ref, lse_ref, q_ref, mixed_ref,
     k_ref, kt_ref, v_ref,
     f_down, f_gate, f_up, f_proj, f_q, f_kv, result_ref, tokens_out, gains_out,
     swapped, from_outer, from_middle, totals, back_land, res_land, norm_land, norm_part,
     gate_m, up_m, activ, dgate, dup, back_part, res_part,
-    left_a, left_b, right, gate_v, up_v, down_v, back_v, tile_v, both, proj_v, qkv_v, hidden_v,
+    left_a, left_b, right, gate_v, up_v, grad_v, back_v, tile_v, both, proj_v, qkv_v, hidden_v,
     row_sum, land_v,
     mine, theirs, swap_v, outer_v, middle_v, sums, total_v,
     grad_hidden, gh_own, g_t, back_t, dk_acc, dv_acc,
@@ -671,6 +720,7 @@
     load_activ = load(activ, left_b.at[:, pl.ds(0, p.ffn_part)], 6)
     load_tokens = load(tokens, gh_own, 7)
     first_tile = early // TILE
+    assert first_tile >= 2 or p.tiles < 3
 
     def tile_bytes(tile, sem):
         piece = gate_m.at[pl.ds(0, 2 * n * p.block), pl.ds(0, TILE)]
@@ -702,8 +752,8 @@
                     device_id=(rep ^ 1, me), device_id_type=MESH,
                 ).start()
 
-    def load_down(tile):
-        return pltpu.make_async_copy(down_w.at[columns(tile), :], down_v, down_sem.at[0])
+    def load_grad(tile):
+        return pltpu.make_async_copy(grad_activ.at[:, columns(tile)], grad_v, down_sem.at[0])
 
     def load_tile(tile):
         @pl.when(tile >= first_tile)
@@ -729,7 +779,7 @@
                     src = full.at[rows, columns(tile)]
                     pltpu.make_async_copy(src, held.at[rows, :], sem).start()
 
-        load_down(tile).start()
+        load_grad(tile).start()
 
     def store_tile(tile):
         dup_columns = pl.ds(pl.multiple_of(p.ffn_part + tile * TILE, TILE), TILE)
@@ -751,7 +801,7 @@
     def ffn_tile(tile):
         for i, held in enumerate((gate_v, up_v)):
             pltpu.make_async_copy(held, held, down_sem.at[i + 1]).wait()
-        load_down(tile).wait()
+        load_grad(tile).wait()
         dup_columns = pl.ds(pl.multiple_of(p.ffn_part + tile * TILE, TILE), TILE)
 
         def go(i, carry):
@@ -759,14 +809,14 @@
             rows = left_b[here, :]
             gate = dot(rows, gate_v[...], NN)
             up = dot(rows, up_v[...], NN)
-            grad_activ = dot(left_a[here, :], down_v[...], NT)
+            grad = grad_v[here, :].astype(F32)
             sigm = jax.nn.sigmoid(gate)
             swish = gate * sigm
             tile_v[tile % 2, here, :] = (swish * up).astype(BF16)
             both[here, columns(tile)] = (
-                grad_activ * up * sigm * (1.0 + gate * (1.0 - sigm))
+                grad * up * sigm * (1.0 + gate * (1.0 - sigm))
             ).astype(BF16)
-            both[here, dup_columns] = (grad_activ * swish).astype(BF16)
+            both[here, dup_columns] = (grad * swish).astype(BF16)
             return carry
 
         lax.fori_loop(0, p.length // TILE, go, 0)
@@ -846,9 +896,10 @@
             store(tile).start()
             return carry
 
-        lax.fori_loop(0, p.per_slot, tile_go, 0)
-        for k in range(max(0, p.per_slot - 2), p.per_slot):
-            store(first + k).wait()
+        size = jnp.minimum(p.per_slot, p.out_tiles - first)
+        lax.fori_loop(0, size, tile_go, 0)
+        store(first + size - 2).wait()
+        store(first + size - 1).wait()
 
     def load_res(tile):
         def copies(action):
@@ -1178,7 +1229,7 @@
         def _():
             wide_chunk(left_b, right[t % 2].T, TILE)
 
-        @pl.when((t >= proj_at) & (t < q_at))
+        @pl.when((t >= proj_at) & (t < end_at))
         def _():
             def go(i, carry):
                 at = columns((t - proj_at) * p.proj_blocks + i)
@@ -1231,7 +1282,7 @@
                 ]
             )
 
-        @pl.when((j >= proj_at) & (j < q_at))
+        @pl.when((j >= proj_at) & (j < end_at))
         def _():
             action(
                 [
@@ -1355,13 +1406,13 @@
             inward_copies(j)[1].wait_recv()
             load_middle(j).start()
 
-        @pl.when(is_middle & valid(j - 1))
-        def _():
-            chunk_bytes(j - 1, total_store.at[0])
-
     def meet_in_middle(j):
         @pl.when(is_middle & valid(j))
         def _():
+            @pl.when(j >= 1)
+            def _():
+                chunk_bytes(j - 1, total_store.at[0])
+
             if p.half > 1:
 
                 @pl.when(j >= 2)
@@ -1386,6 +1437,11 @@
                     pltpu.make_async_copy(src, dst, total_store.at[0]).start()
 
             total_places(j, put)
+
+    def last_store(t):
+        @pl.when(is_middle & (t == p.chunks + p.arrive - 1))
+        def _():
+            chunk_bytes(p.chunks - 1, total_store.at[0])
 
     def send_outward(j):
         @pl.when(jnp.logical_not(is_middle) & valid(j))
@@ -1428,7 +1484,7 @@
         )
 
     def spread_total(j):
-        for kind, sem in ((is_chunk(j, 0), 0), ((j >= proj_at) & (j < q_at), 3)):
+        for kind, sem in ((is_chunk(j, 0), 0), ((j >= proj_at) & (j < end_at), 3)):
 
             @pl.when(kind)
             def _(sem=sem):
@@ -1476,15 +1532,38 @@
         copy.wait()
 
     def slot(t, carry):
-        take_inward(t - 1 - p.lag * depth)
-        take_middle(t - p.meet)
-        send_outward(t - p.spread + p.lag * depth)
-        spread_total(t - p.spread)
-        pass_on(t - p.hand)
+        inner = t - 1
+        for hop in range(1, p.half):
+            inner = jnp.where(depth == hop, p.hop_chunk(t, hop), inner)
+        met = p.hop_chunk(t, p.half)
+        take_inward(inner)
+        take_middle(met)
+        send_inward(inner)
+        meet_in_middle(met)
+        send_outward(t - p.arrive + p.most * depth)
+
+        def spread_until(u):
+            ready = jnp.minimum(u - p.arrive + 1, p.chunks)
+            return jnp.maximum(jnp.minimum(ready, 2 * (u - p.spread_slot + 1)), 0)
+
+        def over(action, u):
+            def go(j, c):
+                action(j)
+                return c
+
+            lax.fori_loop(spread_until(u - 1), spread_until(u), go, 0)
+
+        last_store(t)
+        over(spread_total, t)
+        over(pass_on, t - p.hand)
 
         @pl.when(t + first_tile + ahead < p.tiles)
         def _():
             send_tile(t + first_tile + ahead)
+
+        @pl.when((t > 0) & (t + 1 >= first_tile) & (t + 1 < p.tiles))
+        def _():
+            pass_tile(t + 1)
 
         @pl.when(t < p.tiles)
         def _():
@@ -1502,10 +1581,6 @@
         @pl.when(t == q_at)
         def _():
             load_normed.wait()
-
-        @pl.when(t < p.chunks)
-        def _():
-            make(t)
 
         def at(when, action):
             @pl.when(t == when)
@@ -1516,12 +1591,6 @@
             for copy in copies:
                 copy.start()
 
-        @pl.when((t + 2 >= first_tile) & (t + 2 < p.tiles))
-        def _():
-            pass_tile(t + 2)
-
-        send_inward(t - 1 - p.lag * depth)
-        meet_in_middle(t - p.meet)
         at(p.send_slot, lambda: start_rows(back_rows))
         at(p.rows_slot, hidden_back)
         at(p.pass_slot, gather.hand_on)
@@ -1536,6 +1605,11 @@
             lax.fori_loop(0, 2, go, 0)
 
         at(p.norm_slot, normed_back)
+
+        @pl.when(t < p.chunks)
+        def _():
+            make(t)
+
         at(p.tokens_slot, tokens_back)
         at(p.gain_slot, gains_plane)
         at(p.rep_slot, gains_reps)
@@ -1549,7 +1623,7 @@
 
             res_tiles((t - p.res_slot) * 2)
 
-        at(p.res_slot + p.out_tiles // 2 - 1, lambda: start_rows(res_rows))
+        at(p.res_send_slot, lambda: start_rows(res_rows))
         at(p.result_slot, finish_result)
         return carry
 
@@ -1590,7 +1664,7 @@
 
 
 def backward(
-    shards, reps, x, cot_all, gate_w, up_w, gate_e, up_e, down_w, hidden, tokens, proj_w,
+    shards, reps, x, cot_all, grad_activ, gate_w, up_w, gate_e, up_e, down_w, hidden, tokens, proj_w,
     qkv_m, normed, mlp_rms, mlp_gain, attn_gain, seg, cos_t, sin_t, lse, q_t, mixed_t, k, k_t, v,
 ):
     length, width = x.shape
@@ -1605,7 +1679,7 @@
     dma = pltpu.SemaphoreType.DMA
     return pl.pallas_call(
         functools.partial(backward_kernel, p, gate_e.shape[1]),
-        in_specs=[ANY] * 12 + [IN_VMEM] * 13,
+        in_specs=[ANY] * 13 + [IN_VMEM] * 13,
         out_specs=[ANY] * 8 + [IN_VMEM] + [ANY] * 15,
         out_shape=[
             shape((ffn_part, width), BF16),
@@ -1630,7 +1704,7 @@
             pltpu.VMEM((2, length, TILE), BF16),
             pltpu.VMEM((width, TILE), BF16),
             pltpu.VMEM((width, TILE), BF16),
-            pltpu.VMEM((TILE, width), BF16),
+            pltpu.VMEM((length, TILE), BF16),
             pltpu.VMEM((2, TILE, 2 * ffn_part), BF16),
             pltpu.VMEM((2, length, TILE), BF16),
             pltpu.VMEM((length, 2 * ffn_part), BF16),
@@ -1666,14 +1740,76 @@
         + [dma((p.tiles,))] * 4
         + [dma((3,)), dma((2, 2)), dma((3,))],
         compiler_params=pltpu.CompilerParams(
-            collective_id=3, has_side_effects=True, vmem_limit_bytes=63 * MIB + MIB // 2
+            collective_id=3, has_side_effects=True, vmem_limit_bytes=FULL
         ),
         name="backward",
     )(
-        x, cot_all, gate_w, up_w, gate_e, up_e, down_w, hidden, tokens, proj_w,
+        x, cot_all, grad_activ, gate_w, up_w, gate_e, up_e, down_w, hidden, tokens, proj_w,
         qkv_m, normed, mlp_rms, mlp_gain[None, :], attn_gain[None, :], seg[:, None], seg[None, :],
         cos_t, sin_t, lse, q_t, mixed_t, k, k_t, v,
     )[:9]
+
+
+def widen_kernel(count, rows, columns, *refs):
+    srcs, dsts = refs[:count], refs[count : 2 * count]
+    narrow, wide, in_sem, out_sem = refs[2 * count :]
+    depth = narrow.shape[0]
+    loads, stores = [], []
+    for src, dst in zip(srcs, dsts):
+        for r in range(src.shape[0] // rows):
+            for c in range(src.shape[1] // columns):
+                at = (pl.ds(r * rows, rows), pl.ds(c * columns, columns))
+                slot = len(loads) % depth
+                direct = src.dtype == dst.dtype
+                into = wide.at[slot] if direct else narrow.at[slot]
+                loads.append(pltpu.make_async_copy(src.at[at], into, in_sem.at[slot]))
+                stores.append(
+                    (pltpu.make_async_copy(wide.at[slot], dst.at[at], out_sem.at[slot]), direct)
+                )
+    total = len(loads)
+    ahead = depth - 1
+
+    def load(i):
+        if stores[i][1] and i >= depth:
+            stores[i - depth][0].wait()
+        loads[i].start()
+
+    for i in range(min(ahead, total)):
+        load(i)
+    for i in range(total):
+        slot = i % depth
+        store, direct = stores[i]
+        loads[i].wait()
+        if not direct:
+            if i >= depth:
+                stores[i - depth][0].wait()
+            for strip in range(0, rows, 64):
+                wide[slot, pl.ds(strip, 64), :] = narrow[slot, pl.ds(strip, 64), :].astype(F32)
+        store.start()
+        if i + ahead < total:
+            load(i + ahead)
+    for i in range(max(0, total - depth), total):
+        stores[i][0].wait()
+
+
+def widen(arrays):
+    rows, columns, depth = 256, 2048, 4
+    rows = min([rows] + [a.shape[0] for a in arrays])
+    shapes = [jax.ShapeDtypeStruct(a.shape, F32) for a in arrays]
+    return pl.pallas_call(
+        functools.partial(widen_kernel, len(arrays), rows, columns),
+        in_specs=[ANY] * len(arrays),
+        out_specs=[ANY] * len(arrays),
+        out_shape=shapes,
+        scratch_shapes=[
+            pltpu.VMEM((depth, rows, columns), BF16),
+            pltpu.VMEM((depth, rows, columns), F32),
+            pltpu.SemaphoreType.DMA((depth,)),
+            pltpu.SemaphoreType.DMA((depth,)),
+        ],
+        compiler_params=pltpu.CompilerParams(vmem_limit_bytes=FULL),
+        name="widen",
+    )(*arrays)
 
 
 def local(
@@ -1707,9 +1843,11 @@
         tokens_all, qkv_m, cotangent, proj_w, gate_w, up_w, attn_gain, seg, cos_t, sin_t,
         q_part, kv_part, early, shards,
     )
-    hidden, mlp_rms, normed_mlp = hidden_layer(mixed_t, proj_m, proj_w, tokens, mlp_gain, shards)
+    hidden, mlp_rms, normed_mlp, grad_activ = hidden_layer(
+        mixed_t, proj_m, proj_w, cot_all, down_w, tokens, mlp_gain, shards
+    )
     down, gate, up, proj, query, kv, result, grad_tokens, gains = backward(
-        shards, reps, normed_mlp, cot_all, gate_w, up_w, gate_e, up_e, down_w, hidden, tokens,
+        shards, reps, normed_mlp, cot_all, grad_activ, gate_w, up_w, gate_e, up_e, down_w, hidden, tokens,
         proj_w, qkv_m, normed, mlp_rms, mlp_gain, attn_gain, seg, cos_t, sin_t, lse, q_t,
         mixed_t, k, k_t, v,
     )
@@ -1720,9 +1858,12 @@
         ]
         return jnp.concatenate(parts, axis=1).astype(F32)
 
+    gate, up, down, query, proj, result, grad_tokens = widen(
+        [gate, up, down, query, proj, result, grad_tokens]
+    )
     return (
-        result, grad_tokens, query.astype(F32), every_other(0), every_other(1), proj.astype(F32),
-        gains[0], gate.astype(F32), up.astype(F32), down.astype(F32), gains[1],
+        result, grad_tokens, query, every_other(0), every_other(1), proj, gains[0], gate, up, down,
+        gains[1],
     )
 
 

time: 688 us -> 653 us (0.949)
  other arithmetic: 43.5 us -> 4.57 us
  Pallas kernels: 621 us -> 639 us
  local copies, waits for them, and re-layouts: 21.8 us -> 5.92 us
    convert_element_type x5 -> x0, other arithmetic: 40.4 us -> none  [the longest x1 11.8 us: local(): down.astype(F32)]
    pallas_call x0 -> x1, Pallas kernels: none -> 32.6 us  [widen(): pl.pallas_call(functools.partial(widen_kernel, len(arrays), rows, columns...]
    pallas_call x1, Pallas kernels: 450 us -> 431 us  [backward(): pl.pallas_call(functools.partial(backward_kernel, p, gate_e.shape[1]), in...]
    unnamed x60 -> x0, local copies, waits for them, and re-layouts: 17.9 us -> none
where the time goes in v3:
time: 653 us; the launch traced here: 650 us
  Pallas kernels  639 us (98%)
    pallas_call x1, Pallas kernels, backward(): pl.pallas_call(functools.partial(backward_kernel, p, gate_e.shape[1]), in...  431 us
    pallas_call x1, Pallas kernels, attend(): pl.pallas_call(functools.partial(attend_kernel, shards, part, early), in_...  79.9 us
    pallas_call x1, Pallas kernels, first(): pl.pallas_call(functools.partial(first_kernel, shards, parts), in_specs=[...  48.4 us
    pallas_call x1, Pallas kernels, hidden_layer(): pl.pallas_call(functools.partial(hidden_kernel, shards), in_specs=[IN_VME...  47.2 us
    pallas_call x1, Pallas kernels, widen(): pl.pallas_call(functools.partial(widen_kernel, len(arrays), rows, columns...  32.6 us

profile of v3, /device:TPU:0, one launch (start us, length us, event | category | flops | bytes accessed | tf_op | source)
XLA Modules:
  0.0 650.4 jit_solution(6902683241859290714)
XLA Ops:
  0.7 48.4 %first.1 = (bf16[1024,2048]{1,0:T(8,128)(2,1)}, s32[4,1,256]{2,1,0:T(1,128)}, bf16[2048,768]{1,0:T(8,128)(2,1)}) custom-call(bf16[256,2048]{1,0:T(8,128)(2,1)} %tokens.5, s32[1,256]{1,0:T(1,128)} %bitcast.32, bf16[512,2048]{1,0:T(8,128)(2,1)} %refs_0_.1, bf16[512,512]{1,0:T(8,128)(2,1)} %refs_1_.1, bf16[512,512]{1,0:T(8,128)(2,1)} %refs_2_.1), custom_call_target="tpu_custom_call" | custom-call | tf_op jit(solution)/shard_map/first/pallas_call | solution.py:254
  49.1 1.3 slice.45
  50.4 1.5 fusion.2
  51.8 0.3 reduce-window.9
  52.1 0.1 slice.47
  52.2 0.1 slice_reduce_fusion
  52.3 0.1 fusion.1
  52.4 1.2 multiply_sine_fusion
  53.7 1.7 copy.23.seg_col
  55.4 79.9 %attend.1 = (bf16[1024,2048]{1,0:T(8,128)(2,1)}, bf16[1024,2048]{1,0:T(8,128)(2,1)}, bf16[2048,2048]{1,0:T(8,128)(2,1)}, bf16[2048,512]{1,0:T(8,128)(2,1)}, bf16...) custom-call(bf16[1024,2048]{1,0:T(8,128)(2,1)} %get-tuple-element.45, ...), custom_call_target="tpu_custom_call" | custom-call | tf_op jit(solution)/shard_map/attend/pallas_call | solution.py:465
  135.2 47.2 %hidden.1 = (f32[256,2048]{1,0:T(8,128)}, f32[256,1]{1,0:T(8,128)}, bf16[1024,2048]{1,0:T(8,128)(2,1)}, bf16[1024,2048]{1,0:T(8,128)(2,1)}) custom-call(bf16[512,1024]{1,0:T(8,128)(2,1)} %get-tuple-element.48.mixed_t.mixed_ref, bf16[2048,2048]{1,0:T(8,128)(2,1)} %get-tuple-element.49.proj_m, bf16[512,2048]{1,0:T(8,128)(2,1)} %proj_w.5, ...), custom_call_target="tpu_custom_call" | custom-call | tf_op jit(solution)/shard_map/hidden/pallas_call | solution.py:587
  182.5 431.0 %backward.1 = (bf16[2048,2048]{1,0:T(8,128)(2,1)}, bf16[512,8192]{1,0:T(8,128)(2,1)}, bf16[512,8192]{1,0:T(8,128)(2,1)}, bf16[512,2048]{1,0:T(8,128)(2,1)}, bf16...) custom-call(bf16[1024,2048]{1,0:T(8,128)(2,1)} %get-tuple-element.51, ...), custom_call_target="tpu_custom_call" | custom-call | tf_op jit(solution)/shard_map/backward/pallas_call | solution.py:1680
  613.4 1.4 fusion.6
  614.8 1.4 fusion.5
  616.2 1.5 maximum_convert_fusion
  617.6 32.6 %widen.1 = (f32[512,8192]{1,0:T(8,128)}, f32[512,8192]{1,0:T(8,128)}, f32[2048,2048]{1,0:T(8,128)}, f32[512,2048]{1,0:T(8,128)}, f32[512,2048]{1,0:T(8,128)}, /*index=5*/f32[256,2048]{1,0:T(8,128)}, f32[256,2048]{1,0:T(8,128)}) custom-call(bf16[512,8192]{1,0:T(8,128)(2,1)} %get-tuple-element.63.refs_0_, bf16[512,8192]{1,0:T(8,128)(2,1)} %get-tuple-element.64.refs_1_, ...), custom_call_target="tpu_custom_call" | custom-call | tf_op jit(solution)/shard_map/widen/pallas_call | solution.py:1799
  (2 shorter events, 0.0 us)

commit v4 on v3

--- a/solution.py
+++ b/solution.py
@@ -14,6 +14,7 @@
 GROUP = HEADS // KV_HEADS
 SCALE = 1.0 / math.sqrt(HEAD)
 TILE = 256
+ROWS = 512
 NEG = -1e30
 MIB = 1024 * 1024
 FULL = 63 * MIB + MIB // 2
@@ -320,10 +321,14 @@
     def first_tiles(shard):
         return pl.ds(pl.multiple_of(shard * ffn_part, ffn_part), early)
 
-    proj = Spread(shards, proj_w, proj_m, None, *sems[:2])
-    gate = Spread(shards, gate_w, gate_m, first_tiles, *sems[2:4])
-    up = Spread(shards, up_w, up_m, first_tiles, *sems[4:6])
-    cots = Gather(shards, cot_v, cot_all, *sems[6:9])
+    halves = (pl.ds(0, width // 2), pl.ds(width // 2, width // 2))
+    projs = [
+        Spread(shards, proj_w.at[:, part], proj_m.at[:, part], None, *sems[2 * i : 2 * i + 2])
+        for i, part in enumerate(halves)
+    ]
+    gate = Spread(shards, gate_w, gate_m, first_tiles, *sems[4:6])
+    up = Spread(shards, up_w, up_m, first_tiles, *sems[6:8])
+    cots = Gather(shards, cot_v, cot_all, *sems[8:11])
 
     def block_rows(i):
         return pl.ds(pl.multiple_of(i * TILE, TILE), TILE)
@@ -342,7 +347,8 @@
     weights.start()
     load(0).start()
     greet(plane_partners(rep, me, shards) + pair_partners(rep, me))
-    proj.start()
+    for proj in projs:
+        proj.start()
     gate.start()
     up.start()
     take.wait()
@@ -403,8 +409,8 @@
     lax.fori_loop(0, blocks, project, 0)
     for i in range(max(0, blocks - 2), blocks):
         store(i).wait()
-    proj.hand_on()
-    gate.hand_on()
+    for proj in projs:
+        proj.hand_on()
     wide = GROUP * TILE
 
     def unit(at, carry_out):
@@ -443,13 +449,15 @@
 
     units = kv_heads * blocks
     lax.fori_loop(0, units // 2, unit, 0)
+    gate.hand_on()
     up.hand_on()
-    proj.hand_on_last()
+    lax.fori_loop(units // 2, units, unit, 0)
+    for proj in projs:
+        proj.hand_on_last()
+    cots.hand_on()
     gate.hand_on_last()
-    lax.fori_loop(units // 2, units, unit, 0)
     up.hand_on_last()
-    cots.hand_on()
-    for transfer in (proj, gate, up, cots):
+    for transfer in (*projs, gate, up, cots):
         transfer.finish()
 
 
@@ -488,7 +496,7 @@
             pltpu.VMEM(cot.shape, BF16),
             dma((2,)), dma((2,)), dma((2,)),
         ]
-        + 3 * Spread.semaphores(shards)
+        + 4 * Spread.semaphores(shards)
         + Gather.semaphores(shards),
         compiler_params=pltpu.CompilerParams(
             collective_id=1, has_side_effects=True, vmem_limit_bytes=FULL
@@ -628,49 +636,42 @@
         self.proj_blocks = self.rows // self.proj_half
         self.tiles = ffn_part // TILE
         self.out_tiles = width // TILE
-        per_slot = 3
+        per_slot = 2
         self.back_slot = self.tiles
         self.send_slot = self.back_slot + -(-self.out_tiles // per_slot) - 1
-        self.rows_slot = self.send_slot + 5
-        self.pass_slot = self.rows_slot + 2
-        self.mixed_slot = self.rows_slot + 4
+        self.rows_slot = self.send_slot + 4
+        self.pass_slot = self.rows_slot + 1
+        self.mixed_slot = self.rows_slot + 3
         self.unit_slot = self.mixed_slot + 1
         self.per_slot = per_slot
         self.units = (length // TILE) * (kv_part // HEAD)
         self.norm_slot = self.unit_slot + self.units // 2
-        self.tokens_slot = self.norm_slot + 5
         self.ffn_end = 3 * self.tiles
         self.q_at = max(self.ffn_end, self.norm_slot)
         self.kv_at = self.q_at + q_part // TILE
         self.proj_at = self.kv_at + 1
         self.chunks = self.proj_at + width // TILE // self.proj_blocks
-        self.res_slot = max(self.ffn_end + 1, self.norm_slot + 1)
-        self.res_send_slot = max(self.res_slot + self.out_tiles // 2 - 1, self.tokens_slot + 1)
-        self.result_slot = self.res_send_slot + 8
-        lag = 2 if self.layers == 4 else 1
-        skips = [self.send_slot + 1] if self.layers == 4 else []
-        more = [self.send_slot + 3] if skips else []
-        self.skips = {hop: skips if hop == 1 else skips + more for hop in range(1, self.half + 1)}
-        self.lag = lag
-        self.most = lag + len(skips)
-        self.arrive = 1 + self.most * (self.layers - 1)
-        self.spread_slot = self.pass_slot
+        self.tokens_slot = max(self.norm_slot + 7, self.chunks + self.half + 1)
+        self.early_res = length <= 1024
+        if self.early_res:
+            self.res_slot = self.send_slot + 1
+            self.res_send_slot = max(self.mixed_slot + 1, self.res_slot + self.out_tiles // 2)
+            self.result_slot = self.res_send_slot + 5
+            assert self.result_slot < self.norm_slot + 4
+        else:
+            self.res_slot = max(self.ffn_end + 1, self.norm_slot + 1)
+            self.res_send_slot = max(self.res_slot + self.out_tiles // 2 - 1, self.tokens_slot + 1)
+            self.result_slot = self.res_send_slot + 6
+        self.arrive = self.layers + 2
+        self.spread_slot = self.mixed_slot + 1
+        self.spread_first = max(0, self.send_slot - self.arrive)
         self.hand = 6
         self.gain_slot = self.tokens_slot + 2
         self.rep_slot = max(self.chunks + self.arrive, self.gain_slot + 1)
         self.slots = max(self.chunks + self.arrive + self.hand, self.rep_slot, self.result_slot) + 1
         assert self.spread_slot + self.chunks // 2 < self.slots - self.hand
-        self.mine_ring = 2 + self.most * (self.half - 1)
-        self.sum_ring = self.most + 2
-
-    def hop_chunk(self, t, hop):
-        skips = self.skips.get(hop, [])
-        chunk = t - 1 - self.lag * hop
-        for skip in skips:
-            chunk = chunk - (t >= skip).astype(jnp.int32)
-        for skip in skips:
-            chunk = jnp.where(t == skip, -1, chunk)
-        return chunk
+        self.mine_ring = self.half + 1
+        self.sum_ring = 3
 
 
 def backward_kernel(
@@ -684,7 +685,7 @@
     left_a, left_b, right, gate_v, up_v, grad_v, back_v, tile_v, both, proj_v, qkv_v, hidden_v,
     row_sum, land_v,
     mine, theirs, swap_v, outer_v, middle_v, sums, total_v,
-    grad_hidden, gh_own, g_t, back_t, dk_acc, dv_acc,
+    grad_hidden, gh_own, g_t, back_t, dk_acc, dv_acc, activ_v,
     gain_part, gain_land, gain_sum, gain_reps,
     load_sem, right_sem, small_sem, swap_send, swap_recv, in_send, outer_recv, middle_recv,
     out_send, total_recv, total_store, cross_recv, cross_send, pass_send, pass_recv,
@@ -781,13 +782,16 @@
 
         load_grad(tile).start()
 
+    def units_of(tile):
+        return activ_v.at[:, columns(tile)] if p.early_res else tile_v.at[tile % 2]
+
     def store_tile(tile):
         dup_columns = pl.ds(pl.multiple_of(p.ffn_part + tile * TILE, TILE), TILE)
         return [
             pltpu.make_async_copy(src, dst.at[:, columns(tile)], tile_sem.at[i])
             for i, (src, dst) in enumerate(
                 (
-                    (tile_v.at[tile % 2], activ),
+                    (units_of(tile), activ),
                     (both.at[:, columns(tile)], dgate),
                     (both.at[:, dup_columns], dup),
                 )
@@ -805,21 +809,21 @@
         dup_columns = pl.ds(pl.multiple_of(p.ffn_part + tile * TILE, TILE), TILE)
 
         def go(i, carry):
-            here = columns(i)
+            here = columns(i, ROWS)
             rows = left_b[here, :]
             gate = dot(rows, gate_v[...], NN)
             up = dot(rows, up_v[...], NN)
             grad = grad_v[here, :].astype(F32)
             sigm = jax.nn.sigmoid(gate)
             swish = gate * sigm
-            tile_v[tile % 2, here, :] = (swish * up).astype(BF16)
+            units_of(tile)[here, :] = (swish * up).astype(BF16)
             both[here, columns(tile)] = (
                 grad * up * sigm * (1.0 + gate * (1.0 - sigm))
             ).astype(BF16)
             both[here, dup_columns] = (grad * swish).astype(BF16)
             return carry
 
-        lax.fori_loop(0, p.length // TILE, go, 0)
+        lax.fori_loop(0, p.length // ROWS, go, 0)
 
         @pl.when(tile >= 2)
         def _():
@@ -835,6 +839,10 @@
         @pl.when(tile + 1 < p.tiles)
         def _():
             load_tile(tile + 1)
+
+        @pl.when(tile + 1 == p.tiles)
+        def _():
+            load_back(0)
 
     def load_back(tile):
         slot = tile % 2
@@ -873,7 +881,6 @@
         @pl.when(first == 0)
         def _():
             stored(p.tiles - 1)
-            load_back(0)
 
         def tile_go(k, carry):
             tile = first + k
@@ -888,11 +895,11 @@
                 store(tile - 2).wait()
 
             def go(i, c):
-                here = columns(i)
+                here = columns(i, ROWS)
                 tile_v[tile % 2, here, :] = dot(both[here, :], back_v[tile % 2], NT).astype(BF16)
                 return c
 
-            lax.fori_loop(0, p.length // TILE, go, 0)
+            lax.fori_loop(0, p.length // ROWS, go, 0)
             store(tile).start()
             return carry
 
@@ -916,6 +923,8 @@
         return copies
 
     def res_tiles(first):
+        hidden_units = activ_v if p.early_res else left_b
+
         def store(tile):
             return pltpu.make_async_copy(
                 tile_v.at[tile % 2], res_part.at[:, columns(tile)], tile_sem.at[tile % 2]
@@ -930,13 +939,13 @@
                 load_res(tile + 1)(lambda copy: copy.start())
 
             def go(i, c, k=k, held=held):
-                here = columns(i)
+                here = columns(i, ROWS)
                 tile_v[k, here, :] = dot(
-                    left_b[here, : p.ffn_part], held[: p.ffn_part, :], NN
+                    hidden_units[here, : p.ffn_part], held[: p.ffn_part, :], NN
                 ).astype(BF16)
                 return c
 
-            lax.fori_loop(0, p.length // TILE, go, 0)
+            lax.fori_loop(0, p.length // ROWS, go, 0)
             store(tile).start()
         store(first).wait()
         store(first + 1).wait()
@@ -958,35 +967,112 @@
 
         return copies
 
-    def scatter(part, land, sends, recvs):
-        return [
-            remote(split_rows(part, me ^ (i + 1), count), land.at[i], sends, recvs, i, rep, me ^ (i + 1))
-            for i in range(n)
-        ]
-
-    back_rows = scatter(back_part, back_land, back_send, back_recv)
-    res_rows = scatter(res_part, res_land, res_send, res_recv)
-    norm_rows = scatter(norm_part, norm_land, norm_send, norm_recv)
-
-    def fetch_rows(copies, part, land):
-        for copy in copies:
-            copy.wait_recv()
-        pieces = [split_rows(part, me, count)] + [land.at[i] for i in range(n)]
-        loads = [
-            pltpu.make_async_copy(piece, land_v.at[i % 2], small_sem.at[i % 2])
-            for i, piece in enumerate(pieces)
-        ]
-        loads[0].start()
-        for i, piece in enumerate(loads):
-            if i + 1 < len(loads):
-                loads[i + 1].start()
-            piece.wait()
-
-            def strip(here, i=i):
-                value = land_v[i % 2, here, :].astype(F32)
-                row_sum[here, :] = value if i == 0 else row_sum[here, :] + value
+    side = p.width // 2
+    left_half, right_half = pl.ds(0, side), pl.ds(side, side)
+
+    def rows_of(shard):
+        return pl.ds(pl.multiple_of(shard * count, count), count)
+
+    class Scatter:
+        def __init__(self, part, land, sends, recvs):
+            self.part, self.land = part, land
+            self.second = []
+            if shards != 4:
+                self.first = [
+                    remote(split_rows(part, me ^ (i + 1), count), land.at[i], sends, recvs, i, rep, me ^ (i + 1))
+                    for i in range(n)
+                ]
+                return
+            order = (
+                (3, left_half, 0, right_half, 1),
+                (3, right_half, 1, right_half, 2),
+                (1, left_half, 0, left_half, 1),
+                (2, right_half, 1, left_half, 2),
+            )
+            self.first = [
+                remote(
+                    part.at[rows_of(me ^ block), cols], land.at[into, :, into_cols],
+                    sends, recvs, i, rep, me ^ to,
+                )
+                for i, (block, cols, into, into_cols, to) in enumerate(order)
+            ]
+            self.second = [
+                remote(gh_own.at[:, cols], land.at[2, :, cols], sends, recvs, 4 + i, rep, me ^ to)
+                for i, (cols, to) in enumerate(((left_half, 2), (right_half, 1)))
+            ]
+
+        def start(self):
+            for copy in self.first:
+                copy.start()
+
+        def hand_on(self):
+            if not self.second:
+                return
+            for copy in self.first[:2]:
+                copy.wait_recv()
+            loads = [
+                (self.part.at[rows_of(me ^ 2), left_half], 0, left_half),
+                (self.part.at[rows_of(me ^ 1), right_half], 0, right_half),
+                (self.land.at[0, :, right_half], 1, left_half),
+                (self.land.at[1, :, right_half], 1, right_half),
+            ]
+            for src, slot, cols in loads:
+                pltpu.make_async_copy(src, land_v.at[slot, :, cols], small_sem.at[slot]).start()
+            for slot in range(2):
+                pltpu.make_async_copy(land_v.at[slot], land_v.at[slot], small_sem.at[slot]).wait()
+
+            def strip(here):
+                gh_own[here, :] = (
+                    land_v[0, here, :].astype(F32) + land_v[1, here, :].astype(F32)
+                ).astype(BF16)
 
             strips(strip)
+            for copy in self.second:
+                copy.start()
+
+        def fetch(self):
+            for copy in self.first[2 if self.second else 0 :] + self.second:
+                copy.wait_recv()
+            for copy in self.second:
+                copy.wait_send()
+            pieces = [[(split_rows(self.part, me, count), pl.ds(0, p.width))]]
+            if self.second:
+                pieces.append(
+                    [
+                        (self.land.at[0, :, left_half], left_half),
+                        (self.land.at[1, :, left_half], right_half),
+                    ]
+                )
+                pieces.append([(self.land.at[2], pl.ds(0, p.width))])
+            else:
+                pieces += [[(self.land.at[i], pl.ds(0, p.width))] for i in range(n)]
+
+            def load(i):
+                for src, cols in pieces[i]:
+                    pltpu.make_async_copy(
+                        src, land_v.at[i % 2, :, cols], small_sem.at[i % 2]
+                    ).start()
+
+            load(0)
+            for i in range(len(pieces)):
+                if i + 1 < len(pieces):
+                    load(i + 1)
+                held = land_v.at[i % 2]
+                pltpu.make_async_copy(held, held, small_sem.at[i % 2]).wait()
+
+                def strip(here, i=i):
+                    value = land_v[i % 2, here, :].astype(F32)
+                    row_sum[here, :] = value if i == 0 else row_sum[here, :] + value
+
+                strips(strip)
+
+        def settle(self):
+            for copy in self.first:
+                copy.wait_send()
+
+    back_rows = Scatter(back_part, back_land, back_send, back_recv)
+    res_rows = Scatter(res_part, res_land, res_send, res_recv)
+    norm_rows = Scatter(norm_part, norm_land, norm_send, norm_recv)
 
     STRIP = 32
 
@@ -1008,7 +1094,7 @@
 
     def hidden_back():
         load_hidden.wait()
-        fetch_rows(back_rows, back_part, back_land)
+        back_rows.fetch()
         gain_part[...] = jnp.zeros_like(gain_part)
 
         def strip(here):
@@ -1023,7 +1109,7 @@
         gather.start()
 
     def finish_result():
-        fetch_rows(res_rows, res_part, res_land)
+        res_rows.fetch()
 
         def strip(here):
             row_sum[here, :] = hidden_v[here, :] + row_sum[here, :]
@@ -1114,8 +1200,7 @@
             store.start()
         for store in stores[-2:]:
             store.wait()
-        for copy in norm_rows:
-            copy.start()
+        norm_rows.start()
 
     gain_cols = p.width // shards
 
@@ -1135,9 +1220,9 @@
     ]
 
     def tokens_back():
+        norm_rows.fetch()
         load_tokens.start()
         load_tokens.wait()
-        fetch_rows(norm_rows, norm_part, norm_land)
 
         def strip(here):
             values = gh_own[here, :].astype(F32)
@@ -1204,15 +1289,13 @@
         def _():
             left = right[t % 2].T
 
-            def go(i, carry):
-                def product(which):
-                    at = pl.multiple_of(which * p.rows + i * TILE, TILE)
-                    return dot(left, left_a[:, pl.ds(at, TILE)], NN)
-
-                store_chunk(slot, other, i * TILE, TILE, product)
-                return carry
-
-            lax.fori_loop(0, p.rows // TILE, go, 0)
+            def product(which):
+                return dot(left, left_a[:, columns(which, p.rows)], NN).astype(BF16)
+
+            ours, others = product(core), product(1 - core)
+            for at in range(0, p.rows, TILE):
+                mine[slot, at : at + TILE, :] = ours[:, at : at + TILE]
+                theirs[other, at : at + TILE, :] = others[:, at : at + TILE]
 
         def wide_chunk(left, factor, columns):
             def go(s, carry):
@@ -1532,19 +1615,17 @@
         copy.wait()
 
     def slot(t, carry):
-        inner = t - 1
-        for hop in range(1, p.half):
-            inner = jnp.where(depth == hop, p.hop_chunk(t, hop), inner)
-        met = p.hop_chunk(t, p.half)
+        inner = t - 1 - depth
+        met = t - 1 - p.half
         take_inward(inner)
-        take_middle(met)
         send_inward(inner)
-        meet_in_middle(met)
-        send_outward(t - p.arrive + p.most * depth)
+        send_outward(t - p.arrive + depth)
 
         def spread_until(u):
             ready = jnp.minimum(u - p.arrive + 1, p.chunks)
-            return jnp.maximum(jnp.minimum(ready, 2 * (u - p.spread_slot + 1)), 0)
+            later = p.spread_first + 2 * jnp.maximum(u - p.spread_slot + 1, 0)
+            most = jnp.where(u < p.send_slot, p.chunks, later)
+            return jnp.maximum(jnp.minimum(ready, most), 0)
 
         def over(action, u):
             def go(j, c):
@@ -1576,7 +1657,8 @@
         @pl.when(t == ffn_end)
         def _():
             load_normed.start()
-            load_activ.start()
+            if not p.early_res:
+                load_activ.start()
 
         @pl.when(t == q_at)
         def _():
@@ -1587,11 +1669,10 @@
             def _():
                 action()
 
-        def start_rows(copies):
-            for copy in copies:
-                copy.start()
-
-        at(p.send_slot, lambda: start_rows(back_rows))
+        take_middle(met)
+        meet_in_middle(met)
+        at(p.send_slot, back_rows.start)
+        at(p.send_slot + 2, back_rows.hand_on)
         at(p.rows_slot, hidden_back)
         at(p.pass_slot, gather.hand_on)
         at(p.mixed_slot, mixed_back)
@@ -1605,6 +1686,7 @@
             lax.fori_loop(0, 2, go, 0)
 
         at(p.norm_slot, normed_back)
+        at(p.norm_slot + 4, norm_rows.hand_on)
 
         @pl.when(t < p.chunks)
         def _():
@@ -1618,12 +1700,14 @@
         def _():
             @pl.when(t == p.res_slot)
             def _():
-                load_activ.wait()
+                if not p.early_res:
+                    load_activ.wait()
                 load_res(0)(lambda copy: copy.start())
 
             res_tiles((t - p.res_slot) * 2)
 
-        at(p.res_send_slot, lambda: start_rows(res_rows))
+        at(p.res_send_slot, res_rows.start)
+        at(p.res_send_slot + 3, res_rows.hand_on)
         at(p.result_slot, finish_result)
         return carry
 
@@ -1640,7 +1724,9 @@
             for j in range(max(0, p.chunks - 2), p.chunks):
                 chunk_bytes(j, out_send.at[j % 2])
 
-    for copies in (back_rows, res_rows, norm_rows, gain_plane, gain_all):
+    for rows in (back_rows, res_rows, norm_rows):
+        rows.settle()
+    for copies in (gain_plane, gain_all):
         for copy in copies:
             copy.wait_send()
 
@@ -1726,6 +1812,7 @@
             pltpu.VMEM((q_part + 2 * kv_part, length), BF16),
             pltpu.VMEM((HEAD, length), F32),
             pltpu.VMEM((HEAD, length), F32),
+            pltpu.VMEM((length, ffn_part) if p.early_res else (16, 128), BF16),
             pltpu.VMEM((8, width), F32),
             pltpu.VMEM((shards, 8, own), F32),
             pltpu.VMEM((8, own), F32),
@@ -1733,8 +1820,8 @@
             dma((12,)), dma((2,)), dma((5,)), dma((2,)), dma((p.chunks,)), dma((p.sum_ring,)),
             dma((p.chunks,)), dma((p.chunks,)), dma((2,)), dma((p.chunks,)), dma((2,)),
             dma((p.chunks,)), dma((6,)), dma((6,)), dma((6,)),
-            dma((n,)), dma((n,)), dma((n,)), dma((n,)), dma((n,)), dma((n,)),
         ]
+        + [dma((max(6, n),))] * 6
         + Gather.semaphores(shards)
         + [dma((n,)), dma((n,)), dma((reps - 1,)), dma((reps - 1,))]
         + [dma((p.tiles,))] * 4

time: 653 us -> 620 us (0.949)
  Pallas kernels: 639 us -> 606 us
    pallas_call x1, Pallas kernels: 431 us -> 400 us  [backward(): pl.pallas_call(functools.partial(backward_kernel, p, gate_e.shape[1]), in...]
where the time goes in v4:
time: 620 us; the launch traced here: 617 us
  Pallas kernels  606 us (98%)
    pallas_call x1, Pallas kernels, backward(): pl.pallas_call(functools.partial(backward_kernel, p, gate_e.shape[1]), in...  400 us
    pallas_call x1, Pallas kernels, attend(): pl.pallas_call(functools.partial(attend_kernel, shards, part, early), in_...  74.6 us
    pallas_call x1, Pallas kernels, hidden_layer(): pl.pallas_call(functools.partial(hidden_kernel, shards), in_specs=[IN_VME...  50.1 us
    pallas_call x1, Pallas kernels, first(): pl.pallas_call(functools.partial(first_kernel, shards, parts), in_specs=[...  48.4 us
    pallas_call x1, Pallas kernels, widen(): pl.pallas_call(functools.partial(widen_kernel, len(arrays), rows, columns...  32.6 us

profile of v4, /device:TPU:0, one launch (start us, length us, event | category | flops | bytes accessed | tf_op | source)
XLA Modules:
  0.0 617.3 jit_solution(11890482619751677985)
XLA Ops:
  0.7 48.4 %first.1 = (bf16[1024,2048]{1,0:T(8,128)(2,1)}, s32[4,1,256]{2,1,0:T(1,128)}, bf16[2048,768]{1,0:T(8,128)(2,1)}) custom-call(bf16[256,2048]{1,0:T(8,128)(2,1)} %tokens.5, s32[1,256]{1,0:T(1,128)} %bitcast.32, bf16[512,2048]{1,0:T(8,128)(2,1)} %refs_0_.1, bf16[512,512]{1,0:T(8,128)(2,1)} %refs_1_.1, bf16[512,512]{1,0:T(8,128)(2,1)} %refs_2_.1), custom_call_target="tpu_custom_call" | custom-call | tf_op jit(solution)/shard_map/first/pallas_call | solution.py:255
  49.1 1.3 slice.45
  50.4 1.5 fusion.2
  51.8 0.3 reduce-window.9
  52.1 0.1 slice.47
  52.2 0.1 slice_reduce_fusion
  52.3 0.1 fusion.1
  52.4 1.2 multiply_sine_fusion
  53.7 1.7 copy.23.seg_col
  55.4 74.6 %attend.1 = (bf16[1024,2048]{1,0:T(8,128)(2,1)}, bf16[1024,2048]{1,0:T(8,128)(2,1)}, bf16[2048,2048]{1,0:T(8,128)(2,1)}, bf16[2048,512]{1,0:T(8,128)(2,1)}, bf16...) custom-call(bf16[1024,2048]{1,0:T(8,128)(2,1)} %get-tuple-element.45, ...), custom_call_target="tpu_custom_call" | custom-call | tf_op jit(solution)/shard_map/attend/pallas_call | solution.py:473
  129.9 50.1 %hidden.1 = (f32[256,2048]{1,0:T(8,128)}, f32[256,1]{1,0:T(8,128)}, bf16[1024,2048]{1,0:T(8,128)(2,1)}, bf16[1024,2048]{1,0:T(8,128)(2,1)}) custom-call(bf16[512,1024]{1,0:T(8,128)(2,1)} %get-tuple-element.48.mixed_t.mixed_ref, bf16[2048,2048]{1,0:T(8,128)(2,1)} %get-tuple-element.49.proj_m, bf16[512,2048]{1,0:T(8,128)(2,1)} %proj_w.5, ...), custom_call_target="tpu_custom_call" | custom-call | tf_op jit(solution)/shard_map/hidden/pallas_call | solution.py:595
  180.0 400.2 %backward.1 = (bf16[2048,2048]{1,0:T(8,128)(2,1)}, bf16[512,8192]{1,0:T(8,128)(2,1)}, bf16[512,8192]{1,0:T(8,128)(2,1)}, bf16[512,2048]{1,0:T(8,128)(2,1)}, bf16...) custom-call(bf16[1024,2048]{1,0:T(8,128)(2,1)} %get-tuple-element.51, ...), custom_call_target="tpu_custom_call" | custom-call | tf_op jit(solution)/shard_map/backward/pallas_call | solution.py:1766
  580.3 1.4 fusion.6
  581.7 1.4 fusion.5
  583.1 1.5 maximum_convert_fusion
  584.5 32.6 %widen.1 = (f32[512,8192]{1,0:T(8,128)}, f32[512,8192]{1,0:T(8,128)}, f32[2048,2048]{1,0:T(8,128)}, f32[512,2048]{1,0:T(8,128)}, f32[512,2048]{1,0:T(8,128)}, /*index=5*/f32[256,2048]{1,0:T(8,128)}, f32[256,2048]{1,0:T(8,128)}) custom-call(bf16[512,8192]{1,0:T(8,128)(2,1)} %get-tuple-element.63.refs_0_, bf16[512,8192]{1,0:T(8,128)(2,1)} %get-tuple-element.64.refs_1_, ...), custom_call_target="tpu_custom_call" | custom-call | tf_op jit(solution)/shard_map/widen/pallas_call | solution.py:1886
  (2 shorter events, 0.0 us)

commit v5 on v4

--- a/solution.py
+++ b/solution.py
@@ -202,88 +202,11 @@
 IN_VMEM = pl.BlockSpec(memory_space=pltpu.VMEM)
 
 
-def first_kernel(shards, parts, tokens, seg, *refs):
-    rep, me = place()
-    count = len(parts)
-    weights, (tokens_all, seg_all, qkv_m, tokens_v) = refs[:count], refs[count : count + 4]
-    held, held_sem, sems = refs[count + 4 : 2 * count + 4], refs[2 * count + 4], refs[2 * count + 5 :]
-    take = pltpu.make_async_copy(tokens, tokens_v, held_sem.at[count, 0])
-    take.start()
-    greet(plane_partners(rep, me, shards) + pair_partners(rep, me))
-    at, spreads = 0, []
-    for weight, part, i in zip(weights, parts, range(count)):
-        full = qkv_m.at[:, pl.ds(at, part)]
-        spreads.append(
-            Spread(
-                shards, weight, full, column_block(part), *sems[2 * i : 2 * i + 2],
-                held[i], held_sem.at[i],
-            )
-        )
-        at += part
-    sems = sems[2 * count :]
-    rows = Gather(shards, tokens_v, tokens_all, *sems[:3])
-    seg_send, seg_recv, seg_local = sems[3:]
-    segs = [
-        remote(seg, seg_all.at[me], seg_send, seg_recv, i, rep, me ^ (i + 1))
-        for i in range(shards - 1)
-    ]
-    for spread in spreads:
-        spread.start()
-    for copy in segs:
-        copy.start()
-    take.wait()
-    rows.start()
-    own_seg = pltpu.make_async_copy(seg, seg_all.at[me], seg_local)
-    own_seg.start()
-    for spread in spreads:
-        spread.hand_on()
-    rows.hand_on()
-    for spread in spreads:
-        spread.hand_on_last()
-    for spread in spreads:
-        spread.finish()
-    rows.finish()
-    for copy in segs:
-        copy.wait()
-    own_seg.wait()
-
-
-def first(tokens, seg, weights, shards):
-    rows, width = tokens.shape
-    parts = [w.shape[1] // shards for w in weights]
-    n = shards - 1
-    return pl.pallas_call(
-        functools.partial(first_kernel, shards, parts),
-        in_specs=[ANY] * (2 + len(weights)),
-        out_specs=[ANY] * 3,
-        out_shape=[
-            jax.ShapeDtypeStruct((shards * rows, width), tokens.dtype),
-            jax.ShapeDtypeStruct((shards,) + seg.shape, seg.dtype),
-            jax.ShapeDtypeStruct((width, sum(parts)), BF16),
-        ],
-        scratch_shapes=[pltpu.VMEM(tokens.shape, BF16)]
-        + [pltpu.VMEM((w.shape[0], part), BF16) for w, part in zip(weights, parts)]
-        + [pltpu.SemaphoreType.DMA((len(weights) + 1, 2))]
-        + len(weights) * Spread.semaphores(shards)
-        + Gather.semaphores(shards)
-        + [pltpu.SemaphoreType.DMA((n,)), pltpu.SemaphoreType.DMA((n,)), pltpu.SemaphoreType.DMA],
-        compiler_params=pltpu.CompilerParams(
-            collective_id=0, has_side_effects=True, vmem_limit_bytes=FULL
-        ),
-        name="first",
-    )(tokens, seg, *weights)
-
-
-def doc_positions(seg_ids):
-    index = jnp.arange(seg_ids.shape[0], dtype=jnp.int32)
-    fresh = (index == 0) | (seg_ids != jnp.roll(seg_ids, 1))
-    begins = lax.cummax(jnp.where(fresh, index, jnp.zeros_like(index)), axis=0)
-    return index - begins
-
-
-def rope_tables(positions):
-    freqs = rope_base ** (-(jnp.arange(HEAD // 2, dtype=F32) * (2.0 / HEAD)))
-    angles = freqs[:, None] * positions.astype(F32)[None, :]
+def rope_tables(seg_col, seg_row, freqs):
+    length = seg_row.shape[1]
+    begins = jnp.sum((seg_col < seg_row).astype(jnp.int32), axis=0, keepdims=True)
+    positions = lax.broadcasted_iota(jnp.int32, (1, length), 1) - begins
+    angles = freqs * positions.astype(F32)
     return (jnp.cos(angles), jnp.sin(angles))
 
 
@@ -307,16 +230,43 @@
 
 
 def attend_kernel(
-    shards, ffn_part, early, tokens, qkv_m, cot, proj_w, gate_w, up_w, gain, seg_col, seg_row,
-    cos_ref, sin_ref,
-    normed_out, cot_all, proj_m, gate_m, up_m, q_ref, k_ref, kt_ref, v_ref, out_ref, lse_ref,
-    tokens_v, normed_v, qkv_v, turned_v, vt_ref, cot_v, load_sem, store_sem, qkv_sem, *sems,
+    shards, ffn_part, early, parts, tokens, seg, cot, proj_w, gate_w, up_w, *refs,
 ):
+    count = len(parts)
+    weights, refs = refs[:count], refs[count:]
+    (
+        gain, freqs, normed_out, cot_all, proj_m, gate_m, up_m, qkv_m,
+        q_ref, k_ref, kt_ref, v_ref, out_ref, lse_ref, cos_ref, sin_ref, seg_col, seg_row,
+        tokens_v, normed_v, qkv_v, turned_v, vt_ref, cot_v, seg_v, store_sem, qkv_sem, own_sem,
+        seg_send, seg_recv, *sems,
+    ) = refs
     rep, me = place()
-    length, width = tokens.shape
+    length, width = tokens_v.shape
     kv_heads = k_ref.shape[0]
     q_part, kv_part = q_ref.shape[0], kt_ref.shape[0]
     blocks = length // TILE
+
+    at, spreads, own = 0, [], []
+    for i, (weight, part) in enumerate(zip(weights, parts)):
+        full, rows = qkv_v.at[:, pl.ds(at, part)], weight.shape[0]
+        spreads.append(
+            Spread(shards, weight, full, column_block(part), *sems[2 * i : 2 * i + 2])
+        )
+        own.append(
+            pltpu.make_async_copy(
+                weight.at[:, column_block(part)(me)], split_rows(full, me, rows), own_sem.at[i]
+            )
+        )
+        at += part
+    sems = sems[2 * count :]
+    rows = Gather(shards, tokens, tokens_v, *sems[:3])
+    segs = [
+        remote(seg, seg_v.at[me], seg_send, seg_recv, i, rep, me ^ (i + 1))
+        for i in range(shards - 1)
+    ]
+    own.append(pltpu.make_async_copy(seg, seg_v.at[me], own_sem.at[count]))
+    take = pltpu.make_async_copy(cot, cot_v, own_sem.at[count + 1])
+    sems = sems[3:]
 
     def first_tiles(shard):
         return pl.ds(pl.multiple_of(shard * ffn_part, ffn_part), early)
@@ -330,53 +280,61 @@
     up = Spread(shards, up_w, up_m, first_tiles, *sems[6:8])
     cots = Gather(shards, cot_v, cot_all, *sems[8:11])
 
+    for copy in (*own, take):
+        copy.start()
+    greet(plane_partners(rep, me, shards) + pair_partners(rep, me))
+    for spread in spreads:
+        spread.start()
+    for copy in segs:
+        copy.start()
+    rows.start()
+    for spread in spreads:
+        spread.hand_on()
+    rows.hand_on()
+    for transfer in (*projs, gate, up):
+        transfer.start()
+    take.wait()
+    cots.start()
+    for spread in spreads:
+        spread.hand_on_last()
+
+    for copy in segs:
+        copy.wait()
+    for copy in own:
+        copy.wait()
+    seg_row[...] = jnp.concatenate([seg_v[i] for i in range(shards)], axis=1)
+    tall = jnp.broadcast_to(seg_row[...], (8, length)).astype(F32).T[:, :1]
+    seg_col[...] = tall.astype(jnp.int32)
+    cos_ref[...], sin_ref[...] = rope_tables(seg_col[...], seg_row[...], freqs[...])
+    for spread in spreads:
+        spread.finish()
+    keep_qkv = pltpu.make_async_copy(qkv_v, qkv_m, qkv_sem)
+    keep_qkv.start()
+
     def block_rows(i):
         return pl.ds(pl.multiple_of(i * TILE, TILE), TILE)
-
-    def load(i):
-        return pltpu.make_async_copy(tokens.at[block_rows(i), :], tokens_v.at[i % 2], load_sem.at[i % 2])
 
     def store(i):
         return pltpu.make_async_copy(
             normed_v.at[i % 2], normed_out.at[block_rows(i), :], store_sem.at[i % 2]
         )
 
-    weights = pltpu.make_async_copy(qkv_m, qkv_v, qkv_sem.at[0])
-    take = pltpu.make_async_copy(cot, cot_v, qkv_sem.at[1])
-    take.start()
-    weights.start()
-    load(0).start()
-    greet(plane_partners(rep, me, shards) + pair_partners(rep, me))
-    for proj in projs:
-        proj.start()
-    gate.start()
-    up.start()
-    take.wait()
-    cots.start()
-    weights.wait()
-
     def turn_weights(i, carry):
         turned_v[:, block_rows(i)] = qkv_v[block_rows(i), :].T
         return carry
 
     lax.fori_loop(0, width // TILE, turn_weights, 0)
-
+    rows.finish()
     half = HEAD // 2
 
     def project(i, carry):
         here = block_rows(i)
 
-        @pl.when(i + 1 < blocks)
-        def _():
-            load(i + 1).start()
-
-        load(i).wait()
-
         @pl.when(i >= 2)
         def _():
             store(i - 2).wait()
 
-        values = tokens_v[i % 2].astype(F32)
+        values = tokens_v[here, :].astype(F32)
         rms = lax.rsqrt(jnp.mean(values * values, axis=-1, keepdims=True) + epsilon)
         normed_v[i % 2] = (values * rms * gain[...]).astype(BF16)
         store(i).start()
@@ -409,8 +367,6 @@
     lax.fori_loop(0, blocks, project, 0)
     for i in range(max(0, blocks - 2), blocks):
         store(i).wait()
-    for proj in projs:
-        proj.hand_on()
     wide = GROUP * TILE
 
     def unit(at, carry_out):
@@ -449,9 +405,11 @@
 
     units = kv_heads * blocks
     lax.fori_loop(0, units // 2, unit, 0)
+    for proj in projs:
+        proj.hand_on()
+    lax.fori_loop(units // 2, units, unit, 0)
     gate.hand_on()
     up.hand_on()
-    lax.fori_loop(units // 2, units, unit, 0)
     for proj in projs:
         proj.hand_on_last()
     cots.hand_on()
@@ -459,53 +417,62 @@
     up.hand_on_last()
     for transfer in (*projs, gate, up, cots):
         transfer.finish()
+    keep_qkv.wait()
 
 
 def attend(
-    tokens_all, qkv_m, cot, proj_w, gate_w, up_w, gain, seg, cos_t, sin_t, q_part, kv_part,
-    early, shards,
+    tokens, seg, weights, cot, proj_w, gate_w, up_w, gain, q_part, kv_part, early, shards
 ):
-    length, width = tokens_all.shape
+    count, width = tokens.shape
+    length = shards * count
     kv_heads = kv_part // HEAD
-    part = gate_w.shape[1] // shards
+    ffn_part = gate_w.shape[1] // shards
+    parts = [w.shape[1] // shards for w in weights]
+    freqs = rope_base ** (-(jnp.arange(HEAD // 2, dtype=F32) * (2.0 / HEAD)))
     shape = jax.ShapeDtypeStruct
     dma = pltpu.SemaphoreType.DMA
+    n = shards - 1
     return pl.pallas_call(
-        functools.partial(attend_kernel, shards, part, early),
-        in_specs=[ANY] * 6 + [IN_VMEM] * 5,
-        out_specs=[ANY] * 5 + [IN_VMEM] * 6,
+        functools.partial(attend_kernel, shards, ffn_part, early, parts),
+        in_specs=[ANY] * (6 + len(weights)) + [IN_VMEM] * 2,
+        out_specs=[ANY] * 6 + [IN_VMEM] * 10,
         out_shape=[
             shape((length, width), BF16),
             shape((length, width), BF16),
             shape((shards * proj_w.shape[0], width), BF16),
             shape((width, early), BF16),
             shape((width, early), BF16),
+            shape((width, sum(parts)), BF16),
             shape((q_part, length), BF16),
             shape((kv_heads, length, HEAD), BF16),
             shape((kv_part, length), BF16),
             shape((kv_heads, length, HEAD), BF16),
             shape((q_part, length), BF16),
             shape((kv_heads, GROUP, length), F32),
+            shape((HEAD // 2, length), F32),
+            shape((HEAD // 2, length), F32),
+            shape((length, 1), jnp.int32),
+            shape((1, length), jnp.int32),
         ],
         scratch_shapes=[
+            pltpu.VMEM((length, width), BF16),
             pltpu.VMEM((2, TILE, width), BF16),
-            pltpu.VMEM((2, TILE, width), BF16),
-            pltpu.VMEM(qkv_m.shape, BF16),
-            pltpu.VMEM(qkv_m.shape[::-1], BF16),
+            pltpu.VMEM((width, sum(parts)), BF16),
+            pltpu.VMEM((sum(parts), width), BF16),
             pltpu.VMEM((kv_part, length), BF16),
             pltpu.VMEM(cot.shape, BF16),
-            dma((2,)), dma((2,)), dma((2,)),
+            pltpu.VMEM((shards, 1, count), jnp.int32),
+            dma((2,)), dma, dma((len(weights) + 2,)), dma((n,)), dma((n,)),
         ]
+        + len(weights) * Spread.semaphores(shards)
+        + Gather.semaphores(shards)
         + 4 * Spread.semaphores(shards)
         + Gather.semaphores(shards),
         compiler_params=pltpu.CompilerParams(
             collective_id=1, has_side_effects=True, vmem_limit_bytes=FULL
         ),
         name="attend",
-    )(
-        tokens_all, qkv_m, cot, proj_w, gate_w, up_w, gain[None, :], seg[:, None], seg[None, :],
-        cos_t, sin_t,
-    )
+    )(tokens, seg, cot, proj_w, gate_w, up_w, *weights, gain[None, :], freqs[:, None])
 
 
 def hidden_kernel(
@@ -646,28 +613,30 @@
         self.per_slot = per_slot
         self.units = (length // TILE) * (kv_part // HEAD)
         self.norm_slot = self.unit_slot + self.units // 2
+        self.down_at = 2 * self.tiles
         self.ffn_end = 3 * self.tiles
         self.q_at = max(self.ffn_end, self.norm_slot)
         self.kv_at = self.q_at + q_part // TILE
         self.proj_at = self.kv_at + 1
         self.chunks = self.proj_at + width // TILE // self.proj_blocks
-        self.tokens_slot = max(self.norm_slot + 7, self.chunks + self.half + 1)
+        self.tokens_slot = max(self.norm_slot + 7, self.chunks + 1)
         self.early_res = length <= 1024
         if self.early_res:
             self.res_slot = self.send_slot + 1
             self.res_send_slot = max(self.mixed_slot + 1, self.res_slot + self.out_tiles // 2)
-            self.result_slot = self.res_send_slot + 5
-            assert self.result_slot < self.norm_slot + 4
+            self.result_slot = max(self.res_send_slot + 5, self.norm_slot + 4)
+            assert self.result_slot < self.norm_slot + 5
         else:
             self.res_slot = max(self.ffn_end + 1, self.norm_slot + 1)
             self.res_send_slot = max(self.res_slot + self.out_tiles // 2 - 1, self.tokens_slot + 1)
             self.result_slot = self.res_send_slot + 6
         self.arrive = self.layers + 2
         self.spread_slot = self.mixed_slot + 1
-        self.spread_first = max(0, self.send_slot - self.arrive)
-        self.hand = 6
+        self.spread_first = max(0, self.send_slot + 1 - self.arrive)
+        assert self.tiles >= 3
+        self.hand = 4
         self.gain_slot = self.tokens_slot + 2
-        self.rep_slot = max(self.chunks + self.arrive, self.gain_slot + 1)
+        self.rep_slot = max(self.chunks + self.arrive - 1, self.gain_slot + 1)
         self.slots = max(self.chunks + self.arrive + self.hand, self.rep_slot, self.result_slot) + 1
         assert self.spread_slot + self.chunks // 2 < self.slots - self.hand
         self.mine_ring = self.half + 1
@@ -825,16 +794,16 @@
 
         lax.fori_loop(0, p.length // ROWS, go, 0)
 
-        @pl.when(tile >= 2)
+        @pl.when(tile >= 3)
         def _():
             stored(tile - 1)
 
         for copy in store_tile(tile):
             copy.start()
 
-        @pl.when(tile == 0)
-        def _():
-            stored(0)
+        @pl.when(tile <= 1)
+        def _():
+            stored(tile)
 
         @pl.when(tile + 1 < p.tiles)
         def _():
@@ -950,18 +919,25 @@
         store(first).wait()
         store(first + 1).wait()
 
+    def is_chunk(j, kind):
+        if kind == 0:
+            return (j >= p.down_at) & (j < ffn_end)
+        return (j >= 0) & (j < p.down_at) & (j % 2 == kind - 1)
+
+    def tile_of(j):
+        return jnp.where(j < p.down_at, j // 2, j - p.down_at)
+
     def load_right(t):
         slot = right.at[t % 2]
-        tile, kind = t // 3, t % 3
 
         def copies(action):
             for i, ref in enumerate((activ, dgate, dup)):
 
-                @pl.when((t < ffn_end) & (kind == i))
+                @pl.when(is_chunk(t, i))
                 def _(ref=ref):
                     action(
                         pltpu.make_async_copy(
-                            ref.at[:, columns(tile)], slot, right_sem.at[t % 2]
+                            ref.at[:, columns(tile_of(t))], slot, right_sem.at[t % 2]
                         )
                     )
 
@@ -1136,7 +1112,8 @@
     mid = HEAD // 2
 
     def attention_unit(unit):
-        g, block = unit // blocks, unit % blocks
+        g, turn = unit // blocks, unit % blocks
+        block = jnp.where(turn % 2 == 0, turn // 2, blocks - 1 - turn // 2)
         query_at = pl.multiple_of(block * TILE, TILE)
         here_q = pl.ds(query_at, TILE)
 
@@ -1146,7 +1123,7 @@
         lse = jnp.concatenate([lse_ref[g, h : h + 1, here_q] for h in range(GROUP)], axis=1)
         inner = jnp.sum(grads.astype(F32) * mixed.astype(F32), axis=0, keepdims=True)
 
-        @pl.when(block == 0)
+        @pl.when(turn == 0)
         def _():
             dk_acc[...] = jnp.zeros_like(dk_acc)
             dv_acc[...] = jnp.zeros_like(dv_acc)
@@ -1173,7 +1150,7 @@
             back_t[pl.ds(at, mid), here_q] = (first * cos + second * sin).astype(BF16)
             back_t[pl.ds(at + mid, mid), here_q] = (second * cos - first * sin).astype(BF16)
 
-        @pl.when(block == blocks - 1)
+        @pl.when(turn == blocks - 1)
         def _():
             cos, sin = cos_ref[...], sin_ref[...]
             first, second = dk_acc[:mid, :], dk_acc[mid:, :]
@@ -1285,7 +1262,7 @@
         def _():
             load_right(t + 1)(lambda copy: copy.start())
 
-        @pl.when((t < ffn_end) & (t % 3 == 0))
+        @pl.when(is_chunk(t, 0))
         def _():
             left = right[t % 2].T
 
@@ -1308,7 +1285,7 @@
 
             lax.fori_loop(0, shards, go, 0)
 
-        @pl.when((t < ffn_end) & (t % 3 > 0))
+        @pl.when(t < p.down_at)
         def _():
             wide_chunk(left_b, right[t % 2].T, TILE)
 
@@ -1357,7 +1334,7 @@
                     (
                         i * TILE, TILE, TILE,
                         f_down.at[
-                            columns(j // 3),
+                            columns(tile_of(j)),
                             pl.ds(pl.multiple_of(core * p.rows + i * TILE, TILE), TILE),
                         ],
                     )
@@ -1555,13 +1532,10 @@
         at = pl.multiple_of(shard * part + tile * columns, columns)
         return full.at[pl.ds(pl.multiple_of(core * p.block, p.block), p.block), pl.ds(at, columns)]
 
-    def is_chunk(j, kind):
-        return (j >= 0) & (j < ffn_end) & (j % 3 == kind)
-
     def wide_kinds(j):
         return (
-            (is_chunk(j, 1), f_gate, p.ffn_part, j // 3, 1, TILE),
-            (is_chunk(j, 2), f_up, p.ffn_part, j // 3, 2, TILE),
+            (is_chunk(j, 1), f_gate, p.ffn_part, tile_of(j), 1, TILE),
+            (is_chunk(j, 2), f_up, p.ffn_part, tile_of(j), 2, TILE),
             ((j >= q_at) & (j < kv_at), f_q, p.q_part, j - q_at, 4, TILE),
             (j == kv_at, f_kv, 2 * p.kv_part, 0, 5, 2 * p.kv_part),
         )
@@ -1624,7 +1598,7 @@
         def spread_until(u):
             ready = jnp.minimum(u - p.arrive + 1, p.chunks)
             later = p.spread_first + 2 * jnp.maximum(u - p.spread_slot + 1, 0)
-            most = jnp.where(u < p.send_slot, p.chunks, later)
+            most = jnp.where(u <= p.send_slot, p.chunks, later)
             return jnp.maximum(jnp.minimum(ready, most), 0)
 
         def over(action, u):
@@ -1669,6 +1643,7 @@
             def _():
                 action()
 
+        at(p.tokens_slot, tokens_back)
         take_middle(met)
         meet_in_middle(met)
         at(p.send_slot, back_rows.start)
@@ -1686,13 +1661,12 @@
             lax.fori_loop(0, 2, go, 0)
 
         at(p.norm_slot, normed_back)
-        at(p.norm_slot + 4, norm_rows.hand_on)
+        at(p.norm_slot + 5, norm_rows.hand_on)
 
         @pl.when(t < p.chunks)
         def _():
             make(t)
 
-        at(p.tokens_slot, tokens_back)
         at(p.gain_slot, gains_plane)
         at(p.rep_slot, gains_reps)
 
@@ -1751,7 +1725,8 @@
 
 def backward(
     shards, reps, x, cot_all, grad_activ, gate_w, up_w, gate_e, up_e, down_w, hidden, tokens, proj_w,
-    qkv_m, normed, mlp_rms, mlp_gain, attn_gain, seg, cos_t, sin_t, lse, q_t, mixed_t, k, k_t, v,
+    qkv_m, normed, mlp_rms, mlp_gain, attn_gain, seg_col, seg_row, cos_t, sin_t, lse, q_t, mixed_t,
+    k, k_t, v,
 ):
     length, width = x.shape
     count = tokens.shape[0]
@@ -1832,61 +1807,91 @@
         name="backward",
     )(
         x, cot_all, grad_activ, gate_w, up_w, gate_e, up_e, down_w, hidden, tokens, proj_w,
-        qkv_m, normed, mlp_rms, mlp_gain[None, :], attn_gain[None, :], seg[:, None], seg[None, :],
+        qkv_m, normed, mlp_rms, mlp_gain[None, :], attn_gain[None, :], seg_col, seg_row,
         cos_t, sin_t, lse, q_t, mixed_t, k, k_t, v,
     )[:9]
 
 
-def widen_kernel(count, rows, columns, *refs):
-    srcs, dsts = refs[:count], refs[count : 2 * count]
-    narrow, wide, in_sem, out_sem = refs[2 * count :]
+def widen_kernel(count, rows, columns, group, *refs):
+    paired = 1 if group else 0
+    srcs, dsts = refs[:count], refs[count : 2 * count + paired]
+    narrow, wide, in_sem, out_sem = refs[2 * count + paired :]
     depth = narrow.shape[0]
-    loads, stores = [], []
-    for src, dst in zip(srcs, dsts):
+    jobs = []
+    for i, src in enumerate(srcs):
+        width = min(columns, src.shape[1])
         for r in range(src.shape[0] // rows):
-            for c in range(src.shape[1] // columns):
-                at = (pl.ds(r * rows, rows), pl.ds(c * columns, columns))
-                slot = len(loads) % depth
-                direct = src.dtype == dst.dtype
-                into = wide.at[slot] if direct else narrow.at[slot]
-                loads.append(pltpu.make_async_copy(src.at[at], into, in_sem.at[slot]))
-                stores.append(
-                    (pltpu.make_async_copy(wide.at[slot], dst.at[at], out_sem.at[slot]), direct)
-                )
-    total = len(loads)
+            for c in range(src.shape[1] // width):
+                slot = len(jobs) % depth
+                at = (pl.ds(r * rows, rows), pl.ds(c * width, width))
+                own = (slice(None), pl.ds(0, width))
+                pair = paired and i == 0
+                direct = src.dtype == F32
+                into = (wide if direct else narrow).at[slot].at[own]
+                load = pltpu.make_async_copy(src.at[at], into, in_sem.at[slot])
+                held = wide.at[slot].at[own]
+                if pair:
+                    side = width // 2
+                    puts = [
+                        pltpu.make_async_copy(
+                            wide.at[slot, :, pl.ds(k * side, side)],
+                            dsts[k].at[pl.ds(r * rows, rows), :],
+                            out_sem.at[slot],
+                        )
+                        for k in range(2)
+                    ]
+                else:
+                    puts = [pltpu.make_async_copy(held, dsts[i + paired].at[at], out_sem.at[slot])]
+                done = pltpu.make_async_copy(held, held, out_sem.at[slot])
+                jobs.append((load, puts, done, direct, pair, width))
+    total = len(jobs)
     ahead = depth - 1
 
     def load(i):
-        if stores[i][1] and i >= depth:
-            stores[i - depth][0].wait()
-        loads[i].start()
+        if jobs[i][3] and i >= depth:
+            jobs[i - depth][2].wait()
+        jobs[i][0].start()
 
     for i in range(min(ahead, total)):
         load(i)
     for i in range(total):
         slot = i % depth
-        store, direct = stores[i]
-        loads[i].wait()
+        fetch, puts, _, direct, pair, width = jobs[i]
+        fetch.wait()
         if not direct:
             if i >= depth:
-                stores[i - depth][0].wait()
+                jobs[i - depth][2].wait()
             for strip in range(0, rows, 64):
-                wide[slot, pl.ds(strip, 64), :] = narrow[slot, pl.ds(strip, 64), :].astype(F32)
-        store.start()
+                here = pl.ds(strip, 64)
+                if pair:
+                    for k in range(width // group):
+                        to = (k % 2) * (width // 2) + (k // 2) * group
+                        wide[slot, here, pl.ds(to, group)] = narrow[
+                            slot, here, pl.ds(k * group, group)
+                        ].astype(F32)
+                else:
+                    wide[slot, here, pl.ds(0, width)] = narrow[
+                        slot, here, pl.ds(0, width)
+                    ].astype(F32)
+        for put in puts:
+            put.start()
         if i + ahead < total:
             load(i + ahead)
     for i in range(max(0, total - depth), total):
-        stores[i][0].wait()
-
-
-def widen(arrays):
+        jobs[i][2].wait()
+
+
+def widen(arrays, group):
     rows, columns, depth = 256, 2048, 4
     rows = min([rows] + [a.shape[0] for a in arrays])
     shapes = [jax.ShapeDtypeStruct(a.shape, F32) for a in arrays]
+    if group:
+        tall, width = arrays[0].shape
+        shapes[:1] = [jax.ShapeDtypeStruct((tall, width // 2), F32)] * 2
     return pl.pallas_call(
-        functools.partial(widen_kernel, len(arrays), rows, columns),
+        functools.partial(widen_kernel, len(arrays), rows, columns, group),
         in_specs=[ANY] * len(arrays),
-        out_specs=[ANY] * len(arrays),
+        out_specs=[ANY] * len(shapes),
         out_shape=shapes,
         scratch_shapes=[
             pltpu.VMEM((depth, rows, columns), BF16),
@@ -1922,12 +1927,12 @@
         weights = (query_w, kv_w)
     else:
         weights = (query_w, key_w, value_w)
-    tokens_all, seg, qkv_m = first(tokens, segments[None, :], weights, shards)
-    seg = seg.reshape(length)
-    cos_t, sin_t = rope_tables(doc_positions(seg))
     early = min(2 * TILE, down_w.shape[0] // 2)
-    normed, cot_all, proj_m, gate_e, up_e, q_t, k, k_t, v, mixed_t, lse = attend(
-        tokens_all, qkv_m, cotangent, proj_w, gate_w, up_w, attn_gain, seg, cos_t, sin_t,
+    (
+        normed, cot_all, proj_m, gate_e, up_e, qkv_m,
+        q_t, k, k_t, v, mixed_t, lse, cos_t, sin_t, seg_col, seg_row,
+    ) = attend(
+        tokens, segments[None, :], weights, cotangent, proj_w, gate_w, up_w, attn_gain,
         q_part, kv_part, early, shards,
     )
     hidden, mlp_rms, normed_mlp, grad_activ = hidden_layer(
@@ -1935,8 +1940,8 @@
     )
     down, gate, up, proj, query, kv, result, grad_tokens, gains = backward(
         shards, reps, normed_mlp, cot_all, grad_activ, gate_w, up_w, gate_e, up_e, down_w, hidden, tokens,
-        proj_w, qkv_m, normed, mlp_rms, mlp_gain, attn_gain, seg, cos_t, sin_t, lse, q_t,
-        mixed_t, k, k_t, v,
+        proj_w, qkv_m, normed, mlp_rms, mlp_gain, attn_gain, seg_col, seg_row, cos_t, sin_t, lse,
+        q_t, mixed_t, k, k_t, v,
     )
 
     def every_other(first):
@@ -1945,12 +1950,14 @@
         ]
         return jnp.concatenate(parts, axis=1).astype(F32)
 
-    gate, up, down, query, proj, result, grad_tokens = widen(
-        [gate, up, down, query, proj, result, grad_tokens]
-    )
+    others = [gate, up, down, query, proj, result, grad_tokens]
+    if kv_part % 128:
+        key, value = every_other(0), every_other(1)
+        gate, up, down, query, proj, result, grad_tokens = widen(others, 0)
+    else:
+        key, value, gate, up, down, query, proj, result, grad_tokens = widen([kv] + others, kv_part)
     return (
-        result, grad_tokens, query, every_other(0), every_other(1), proj, gains[0], gate, up, down,
-        gains[1],
+        result, grad_tokens, query, key, value, proj, gains[0], gate, up, down, gains[1],
     )
 
 

time: 620 us -> 606 us (0.977)
    pallas_call x2 -> x1, Pallas kernels: 123 us -> 120 us  [attend(): pl.pallas_call(functools.partial(attend_kernel, shards, ffn_part, early,...]
where the time goes in v5:
time: 606 us; the launch traced here: 603 us
  Pallas kernels  600 us (99%)
    pallas_call x1, Pallas kernels, backward(): pl.pallas_call(functools.partial(backward_kernel, p, gate_e.shape[1]), in...  395 us
    pallas_call x1, Pallas kernels, attend(): pl.pallas_call(functools.partial(attend_kernel, shards, ffn_part, early,...  120 us
    pallas_call x1, Pallas kernels, hidden_layer(): pl.pallas_call(functools.partial(hidden_kernel, shards), in_specs=[IN_VME...  52 us
    pallas_call x1, Pallas kernels, widen(): pl.pallas_call(functools.partial(widen_kernel, len(arrays), rows, columns...  33.7 us

profile of v5, /device:TPU:0, one launch (start us, length us, event | category | flops | bytes accessed | tf_op | source)
XLA Modules:
  0.0 603.0 jit_solution(3789312959058956262)
XLA Ops:
  0.6 0.6 negate_power_fusion.refs_4_
  1.3 119.5 %attend.1 = (bf16[1024,2048]{1,0:T(8,128)(2,1)}, bf16[1024,2048]{1,0:T(8,128)(2,1)}, bf16[2048,2048]{1,0:T(8,128)(2,1)}, bf16[2048,512]{1,0:T(8,128)(2,1)}, bf16...) custom-call(bf16[256,2048]{1,0:T(8,128)(2,1)} %tokens.5, ...), custom_call_target="tpu_custom_call" | custom-call | tf_op jit(solution)/shard_map/attend/pallas_call | solution.py:435
  120.8 52.0 %hidden.1 = (f32[256,2048]{1,0:T(8,128)}, f32[256,1]{1,0:T(8,128)}, bf16[1024,2048]{1,0:T(8,128)(2,1)}, bf16[1024,2048]{1,0:T(8,128)(2,1)}) custom-call(bf16[512,1024]{1,0:T(8,128)(2,1)} %get-tuple-element.49.mixed_t.mixed_ref, bf16[2048,2048]{1,0:T(8,128)(2,1)} %get-tuple-element.50.proj_m, bf16[512,2048]{1,0:T(8,128)(2,1)} %proj_w.5, ...), custom_call_target="tpu_custom_call" | custom-call | tf_op jit(solution)/shard_map/hidden/pallas_call | solution.py:562
  172.9 394.9 %backward.1 = (bf16[2048,2048]{1,0:T(8,128)(2,1)}, bf16[512,8192]{1,0:T(8,128)(2,1)}, bf16[512,8192]{1,0:T(8,128)(2,1)}, bf16[512,2048]{1,0:T(8,128)(2,1)}, bf16...) custom-call(bf16[1024,2048]{1,0:T(8,128)(2,1)} %get-tuple-element.52, ...), custom_call_target="tpu_custom_call" | custom-call | tf_op jit(solution)/shard_map/backward/pallas_call | solution.py:1741
  567.7 1.4 fusion
  569.1 33.7 %widen.1 = (f32[512,512]{1,0:T(8,128)}, f32[512,512]{1,0:T(8,128)}, f32[512,8192]{1,0:T(8,128)}, f32[512,8192]{1,0:T(8,128)}, f32[2048,2048]{1,0:T(8,128)}, /*in...) custom-call(bf16[512,1024]{1,0:T(8,128)(2,1)} %get-tuple-element.69.refs_0_, ...), custom_call_target="tpu_custom_call" | custom-call | tf_op jit(solution)/shard_map/widen/pallas_call | solution.py:1891

commit v6 on v5

--- a/solution.py
+++ b/solution.py
@@ -125,6 +125,76 @@
     @staticmethod
     def semaphores(shards):
         n = 4 * (shards - 1)
+        return [pltpu.SemaphoreType.DMA((n,)), pltpu.SemaphoreType.DMA((n,))]
+
+
+class WideSpread:
+    def __init__(self, shards, own, full, sends, recvs):
+        rep, me = place()
+        eighth = rep % 8
+        count = own.shape[0]
+        part = count // 8
+        own_rows = pl.ds(pl.multiple_of(eighth * part, part), part)
+
+        def at(shard, which):
+            return full.at[pl.ds(pl.multiple_of(shard * count + which * part, part), part), :]
+
+        self.first, self.near, self.layer, self.far, self.passed = [], [], [], [], []
+        n = shards - 1
+        for i in range(n):
+            peer = me ^ (i + 1)
+
+            def hand(which, kind, to, i=i, peer=peer):
+                piece = at(peer, which)
+                return remote(piece, piece, sends, recvs, kind * n + i, to, me)
+
+            self.first.append(
+                remote(own.at[own_rows, :], at(me, eighth), sends, recvs, i, rep, peer)
+            )
+            self.layer.append(hand(eighth, 1, rep ^ 2))
+            self.far.append((hand(eighth, 2, rep ^ 4), hand(eighth ^ 2, 3, rep ^ 4)))
+            self.passed.append(
+                tuple(
+                    hand(which, 4 + k, rep ^ 1)
+                    for k, which in enumerate((eighth, eighth ^ 2, eighth ^ 4, eighth ^ 6))
+                )
+            )
+
+    def start(self):
+        for copy in self.first:
+            copy.start()
+
+    def hand_on(self):
+        for i, copy in enumerate(self.first):
+            copy.wait_recv()
+            self.layer[i].start()
+            self.passed[i][0].start()
+        for far in self.far:
+            far[0].start()
+
+    def hand_on_next(self):
+        for i, copy in enumerate(self.layer):
+            copy.wait_recv()
+            self.far[i][1].start()
+            self.passed[i][1].start()
+
+    def hand_on_last(self):
+        for k in range(2):
+            for i, far in enumerate(self.far):
+                far[k].wait_recv()
+                self.passed[i][2 + k].start()
+
+    def finish(self):
+        for passed in self.passed:
+            for copy in passed:
+                copy.wait_recv()
+        for i in range(len(self.first)):
+            for copy in (self.first[i], self.layer[i], *self.far[i], *self.passed[i]):
+                copy.wait_send()
+
+    @staticmethod
+    def semaphores(shards):
+        n = 8 * (shards - 1)
         return [pltpu.SemaphoreType.DMA((n,)), pltpu.SemaphoreType.DMA((n,))]
 
 
@@ -271,30 +341,29 @@
     def first_tiles(shard):
         return pl.ds(pl.multiple_of(shard * ffn_part, ffn_part), early)
 
-    halves = (pl.ds(0, width // 2), pl.ds(width // 2, width // 2))
-    projs = [
-        Spread(shards, proj_w.at[:, part], proj_m.at[:, part], None, *sems[2 * i : 2 * i + 2])
-        for i, part in enumerate(halves)
-    ]
-    gate = Spread(shards, gate_w, gate_m, first_tiles, *sems[4:6])
-    up = Spread(shards, up_w, up_m, first_tiles, *sems[6:8])
-    cots = Gather(shards, cot_v, cot_all, *sems[8:11])
+    proj = WideSpread(shards, proj_w, proj_m, *sems[:2])
+    gate = Spread(shards, gate_w, gate_m, first_tiles, *sems[2:4])
+    up = Spread(shards, up_w, up_m, first_tiles, *sems[4:6])
+    cots = Gather(shards, cot_v, cot_all, *sems[6:9])
 
     for copy in (*own, take):
         copy.start()
-    greet(plane_partners(rep, me, shards) + pair_partners(rep, me))
+    greet(plane_partners(rep, me, shards) + pair_partners(rep, me) + [(rep ^ 4, me)])
+    proj.start()
     for spread in spreads:
         spread.start()
     for copy in segs:
         copy.start()
     rows.start()
+    proj.hand_on()
     for spread in spreads:
         spread.hand_on()
     rows.hand_on()
-    for transfer in (*projs, gate, up):
-        transfer.start()
+    gate.start()
+    up.start()
     take.wait()
     cots.start()
+    proj.hand_on_next()
     for spread in spreads:
         spread.hand_on_last()
 
@@ -405,17 +474,14 @@
 
     units = kv_heads * blocks
     lax.fori_loop(0, units // 2, unit, 0)
-    for proj in projs:
-        proj.hand_on()
     lax.fori_loop(units // 2, units, unit, 0)
     gate.hand_on()
     up.hand_on()
-    for proj in projs:
-        proj.hand_on_last()
     cots.hand_on()
+    proj.hand_on_last()
     gate.hand_on_last()
     up.hand_on_last()
-    for transfer in (*projs, gate, up, cots):
+    for transfer in (proj, gate, up, cots):
         transfer.finish()
     keep_qkv.wait()
 
@@ -466,7 +532,8 @@
         ]
         + len(weights) * Spread.semaphores(shards)
         + Gather.semaphores(shards)
-        + 4 * Spread.semaphores(shards)
+        + WideSpread.semaphores(shards)
+        + 2 * Spread.semaphores(shards)
         + Gather.semaphores(shards),
         compiler_params=pltpu.CompilerParams(
             collective_id=1, has_side_effects=True, vmem_limit_bytes=FULL
@@ -1585,8 +1652,7 @@
         send_tile(tile)
     for copy in (load_hidden, load_proj, load_qkv):
         copy.start()
-    for copy in (load_x, load_cot):
-        copy.wait()
+    load_x.wait()
 
     def slot(t, carry):
         inner = t - 1 - depth
@@ -1648,6 +1714,7 @@
         meet_in_middle(met)
         at(p.send_slot, back_rows.start)
         at(p.send_slot + 2, back_rows.hand_on)
+        at(p.send_slot, load_cot.wait)
         at(p.rows_slot, hidden_back)
         at(p.pass_slot, gather.hand_on)
         at(p.mixed_slot, mixed_back)

time: 606 us -> 600 us (0.990)
    pallas_call x1, Pallas kernels: 120 us -> 111 us  [attend(): pl.pallas_call(functools.partial(attend_kernel, shards, ffn_part, early,...]
where the time goes in v6:
time: 600 us; the launch traced here: 597 us
  Pallas kernels  594 us (99%)
    pallas_call x1, Pallas kernels, backward(): pl.pallas_call(functools.partial(backward_kernel, p, gate_e.shape[1]), in...  396 us
    pallas_call x1, Pallas kernels, attend(): pl.pallas_call(functools.partial(attend_kernel, shards, ffn_part, early,...  111 us
    pallas_call x1, Pallas kernels, hidden_layer(): pl.pallas_call(functools.partial(hidden_kernel, shards), in_specs=[IN_VME...  53.6 us
    pallas_call x1, Pallas kernels, widen(): pl.pallas_call(functools.partial(widen_kernel, len(arrays), rows, columns...  33.7 us

profile of v6, /device:TPU:0, one launch (start us, length us, event | category | flops | bytes accessed | tf_op | source)
XLA Modules:
  0.0 596.9 jit_solution(450610227598339699)
XLA Ops:
  0.6 0.6 negate_power_fusion.refs_4_
  1.3 110.5 %attend.1 = (bf16[1024,2048]{1,0:T(8,128)(2,1)}, bf16[1024,2048]{1,0:T(8,128)(2,1)}, bf16[2048,2048]{1,0:T(8,128)(2,1)}, bf16[2048,512]{1,0:T(8,128)(2,1)}, bf16...) custom-call(bf16[256,2048]{1,0:T(8,128)(2,1)} %tokens.5, ...), custom_call_target="tpu_custom_call" | custom-call | tf_op jit(solution)/shard_map/attend/pallas_call | solution.py:501
  111.8 53.6 %hidden.1 = (f32[256,2048]{1,0:T(8,128)}, f32[256,1]{1,0:T(8,128)}, bf16[1024,2048]{1,0:T(8,128)(2,1)}, bf16[1024,2048]{1,0:T(8,128)(2,1)}) custom-call(bf16[512,1024]{1,0:T(8,128)(2,1)} %get-tuple-element.49.mixed_t.mixed_ref, bf16[2048,2048]{1,0:T(8,128)(2,1)} %get-tuple-element.50.proj_m, bf16[512,2048]{1,0:T(8,128)(2,1)} %proj_w.5, ...), custom_call_target="tpu_custom_call" | custom-call | tf_op jit(solution)/shard_map/hidden/pallas_call | solution.py:629
  165.4 396.2 %backward.1 = (bf16[2048,2048]{1,0:T(8,128)(2,1)}, bf16[512,8192]{1,0:T(8,128)(2,1)}, bf16[512,8192]{1,0:T(8,128)(2,1)}, bf16[512,2048]{1,0:T(8,128)(2,1)}, bf16...) custom-call(bf16[1024,2048]{1,0:T(8,128)(2,1)} %get-tuple-element.52, ...), custom_call_target="tpu_custom_call" | custom-call | tf_op jit(solution)/shard_map/backward/pallas_call | solution.py:1808
  561.7 1.4 fusion
  563.1 33.7 %widen.1 = (f32[512,512]{1,0:T(8,128)}, f32[512,512]{1,0:T(8,128)}, f32[512,8192]{1,0:T(8,128)}, f32[512,8192]{1,0:T(8,128)}, f32[2048,2048]{1,0:T(8,128)}, /*in...) custom-call(bf16[512,1024]{1,0:T(8,128)(2,1)} %get-tuple-element.69.refs_0_, ...), custom_call_target="tpu_custom_call" | custom-call | tf_op jit(solution)/shard_map/widen/pallas_call | solution.py:1958

commit v7 on v6

--- a/solution.py
+++ b/solution.py
@@ -3,6 +3,7 @@
 
 import jax
 import jax.numpy as jnp
+import numpy as np
 from jax import lax
 from jax.experimental import pallas as pl
 from jax.experimental.pallas import tpu as pltpu
@@ -494,7 +495,7 @@
     kv_heads = kv_part // HEAD
     ffn_part = gate_w.shape[1] // shards
     parts = [w.shape[1] // shards for w in weights]
-    freqs = rope_base ** (-(jnp.arange(HEAD // 2, dtype=F32) * (2.0 / HEAD)))
+    freqs = np.asarray(rope_base ** (-(np.arange(HEAD // 2) * (2.0 / HEAD))), np.float32)
     shape = jax.ShapeDtypeStruct
     dma = pltpu.SemaphoreType.DMA
     n = shards - 1
@@ -539,7 +540,7 @@
             collective_id=1, has_side_effects=True, vmem_limit_bytes=FULL
         ),
         name="attend",
-    )(tokens, seg, cot, proj_w, gate_w, up_w, *weights, gain[None, :], freqs[:, None])
+    )(tokens, seg, cot, proj_w, gate_w, up_w, *weights, gain[None, :], jnp.asarray(freqs[:, None]))
 
 
 def hidden_kernel(
@@ -701,7 +702,7 @@
         self.spread_slot = self.mixed_slot + 1
         self.spread_first = max(0, self.send_slot + 1 - self.arrive)
         assert self.tiles >= 3
-        self.hand = 4
+        self.hand = 3
         self.gain_slot = self.tokens_slot + 2
         self.rep_slot = max(self.chunks + self.arrive - 1, self.gain_slot + 1)
         self.slots = max(self.chunks + self.arrive + self.hand, self.rep_slot, self.result_slot) + 1
@@ -1949,7 +1950,7 @@
 
 
 def widen(arrays, group):
-    rows, columns, depth = 256, 2048, 4
+    rows, columns, depth = 64, 2048, 12
     rows = min([rows] + [a.shape[0] for a in arrays])
     shapes = [jax.ShapeDtypeStruct(a.shape, F32) for a in arrays]
     if group:

time: 600 us -> 603 us (level)
  no operation moved by 1% of the time
where the time goes in v7:
time: 603 us; the launch traced here: 599 us
  Pallas kernels  596 us (99%)
    pallas_call x1, Pallas kernels, backward(): pl.pallas_call(functools.partial(backward_kernel, p, gate_e.shape[1]), in...  399 us
    pallas_call x1, Pallas kernels, attend(): pl.pallas_call(functools.partial(attend_kernel, shards, ffn_part, early,...  111 us
    pallas_call x1, Pallas kernels, hidden_layer(): pl.pallas_call(functools.partial(hidden_kernel, shards), in_specs=[IN_VME...  53.6 us
    pallas_call x1, Pallas kernels, widen(): pl.pallas_call(functools.partial(widen_kernel, len(arrays), rows, columns...  33.3 us

profile of v7, /device:TPU:0, one launch (start us, length us, event | category | flops | bytes accessed | tf_op | source)
XLA Modules:
  0.0 598.6 jit_solution(9466858617713717369)
XLA Ops:
  0.6 110.6 %attend.1 = (bf16[1024,2048]{1,0:T(8,128)(2,1)}, bf16[1024,2048]{1,0:T(8,128)(2,1)}, bf16[2048,2048]{1,0:T(8,128)(2,1)}, bf16[2048,512]{1,0:T(8,128)(2,1)}, bf16...) custom-call(bf16[256,2048]{1,0:T(8,128)(2,1)} %tokens.5, ...), custom_call_target="tpu_custom_call" | custom-call | tf_op jit(solution)/shard_map/attend/pallas_call | solution.py:502
  111.2 53.6 %hidden.1 = (f32[256,2048]{1,0:T(8,128)}, f32[256,1]{1,0:T(8,128)}, bf16[1024,2048]{1,0:T(8,128)(2,1)}, bf16[1024,2048]{1,0:T(8,128)(2,1)}) custom-call(bf16[512,1024]{1,0:T(8,128)(2,1)} %get-tuple-element.49.mixed_t.mixed_ref, bf16[2048,2048]{1,0:T(8,128)(2,1)} %get-tuple-element.50.proj_m, bf16[512,2048]{1,0:T(8,128)(2,1)} %proj_w.5, ...), custom_call_target="tpu_custom_call" | custom-call | tf_op jit(solution)/shard_map/hidden/pallas_call | solution.py:630
  164.8 398.9 %backward.1 = (bf16[2048,2048]{1,0:T(8,128)(2,1)}, bf16[512,8192]{1,0:T(8,128)(2,1)}, bf16[512,8192]{1,0:T(8,128)(2,1)}, bf16[512,2048]{1,0:T(8,128)(2,1)}, bf16...) custom-call(bf16[1024,2048]{1,0:T(8,128)(2,1)} %get-tuple-element.52, ...), custom_call_target="tpu_custom_call" | custom-call | tf_op jit(solution)/shard_map/backward/pallas_call | solution.py:1809
  563.8 1.4 fusion
  565.1 33.3 %widen.1 = (f32[512,512]{1,0:T(8,128)}, f32[512,512]{1,0:T(8,128)}, f32[512,8192]{1,0:T(8,128)}, f32[512,8192]{1,0:T(8,128)}, f32[2048,2048]{1,0:T(8,128)}, /*in...) custom-call(bf16[512,1024]{1,0:T(8,128)(2,1)} %get-tuple-element.69.refs_0_, ...), custom_call_target="tpu_custom_call" | custom-call | tf_op jit(solution)/shard_map/widen/pallas_call | solution.py:1959
